TPU v7x, 32 devices: a whole 2x2x4 slice. The times are simulated.
32 devices in a mesh: tgt: 8 (over y, x, core), src: 4 (over z).
Axes of the slice: x: 2, y: 2, z: 4, core: 2. Of those that a mesh axis runs over, the one named last changes fastest.
Arguments:
- sources: bfloat16 [4, 1024, 32, 128], P('src', 'tgt'), may hold values from -6 to 6
- first_factors: bfloat16 [4, 1024, 2, 64, 128], P('src', 'tgt'), may hold values from -0.375 to 0.375
- second_factors: bfloat16 [1024, 2, 64, 128], P('tgt'), may hold values from -0.375 to 0.375
- pattern: int32 [1024], P('tgt'), may hold values from 0 to 127, as said below
Outputs:
- targets: float32 [1024, 32, 128], P(('tgt', 'src'))
Inputs may be any that keep to these rules, and one draw needn't show every extreme that they name: Within each aligned group of 128 blocks, pattern is a permutation of 0 to 127.
All inputs are finite; a program needn't handle non-finite values.
Results may differ from a plain program's by a relative error of at most 0.0003.
Values may be sent and summed in bfloat16 or wider, within the bound.
No kernel may reach another device: no remote copies, remote signals or barrier semaphores. Data moves between devices by JAX's collectives and lax.ppermute only.
A program may use at most 64 MiB of HBM per device.

v0:
```python
import jax
import jax.numpy as jnp
from jax import lax
from jax.sharding import PartitionSpec as P


def swapped(block, axis, stride):
    count = lax.axis_size(axis)
    route = []
    for low in range(count):
        high = low | 1 << stride
        if high != low and high < count:
            route += [(low, high), (high, low)]
    return lax.ppermute(block, axis, route)


def apply_factor(values, factor, precise):
    blocks, rows, width = values.shape
    rank = width // 2
    split_values = values.reshape(blocks, rows, 2, rank)
    if precise:
        product = jnp.einsum(
            "brck,bkj->brcj",
            split_values,
            factor.astype(jnp.float32),
            precision=lax.Precision.HIGHEST,
        )
    else:
        product = jnp.einsum(
            "brck,bkj->brcj", split_values, factor, preferred_element_type=jnp.float32
        )
    real_part = product[:, :, 0, :rank] - product[:, :, 1, rank:]
    imag_part = product[:, :, 0, rank:] + product[:, :, 1, :rank]
    return jnp.concatenate([real_part, imag_part], axis=-1)


def on_device(sources, first_factors, second_factors, pattern):
    top_bit = lax.axis_size("tgt").bit_length() - 2
    src_count = lax.axis_size("src")
    local_values = sources[0]
    local_factors = first_factors[0]
    block_count = local_values.shape[0]
    shares = block_count // src_count
    remote_values = swapped(local_values, "tgt", top_bit)
    partner_values = jnp.take(remote_values, pattern, axis=0)
    summed = lax.psum_scatter(
        apply_factor(local_values, local_factors[:, 0], False)
        + apply_factor(partner_values, local_factors[:, 1], False),
        "src",
        scatter_dimension=0,
        tiled=True,
    )
    remote_summed = swapped(summed, "tgt", top_bit - 1)
    mine = lax.dynamic_slice_in_dim(second_factors, lax.axis_index("src") * shares, shares, 0)
    return apply_factor(summed, mine[:, 0], True) + apply_factor(remote_summed, mine[:, 1], True)


def solution(mesh):
    return jax.shard_map(
        on_device,
        mesh=mesh,
        in_specs=(
            P("src", "tgt", None, None),
            P("src", "tgt", None, None, None),
            P("tgt", None, None, None),
            P("tgt"),
        ),
        out_specs=P(("tgt", "src"), None, None),
        check_vma=False,
    )
```

profile of v0, /device:TPU:0, one launch (start us, length us, event | category | flops | bytes accessed | tf_op | source)
XLA Modules:
  0.0 119.2 jit_solution(15109440569830007469)
XLA Ops:
  6.5 3.0 %collective-permute-start = (bf16[128,32,128]{2,1,0:T(8,128)(2,1)}, bf16[128,32,128]{2,1,0:T(8,128)(2,1)}, u32[]{:S(2)}, u32[]{:S(2)}) collective-permute-start(bf16[128,32,128]{2,1,0:T(8,128)(2,1)} %bitcast.72), channel_id=1, source_target_pairs={{0,16},{16,0},{4,20},{20,4},{8,24},{24,8},{12,28},{28,12},{1,17},{... | collective-permute-start | bytes 3145736 | tf_op jit(solution)/shard_map/ppermute | solution.py:14
  9.5 2.0 %copy.42 = bf16[1,128,32,128]{1,3,2,0:T(8,128)(2,1)S(1)} copy(bf16[1,128,32,128]{3,2,1,0:T(8,128)(2,1)} %param.4) | data formatting | bytes 2097152 | tf_op args[0]
  11.5 5.4 %copy.82 = bf16[1,128,2,64,128]{4,3,1,2,0:T(8,128)(2,1)} copy(bf16[1,128,2,64,128]{4,3,2,1,0:T(8,128)(2,1)} %param.5) | data formatting | bytes 8388608 | tf_op args[1]
  16.8 3.0 %copy.44 = bf16[128,32,2,64]{3,1,2,0:T(8,128)(2,1)S(1)} copy(bf16[128,32,2,64]{0,3,2,1:T(8,128)(2,1)S(1)} %bitcast.70) | data formatting | bytes 2097152 | tf_op jit(solution)/shard_map/reshape;squeeze | solution.py:20
  19.9 2.3 %fusion.6 = f32[128,32,2,128]{3,1,2,0:T(8,128)S(1)} fusion(bf16[128,32,2,64]{3,1,2,0:T(8,128)(2,1)S(1)} %copy.44, bf16[128,2,64,128]{3,2,0,1:T(8,128)(2,1)} %bitcast.68), kind=kOutput, calls=%fused_computation.15 | convolution fusion | flops 134217728 | bytes 7340032 | tf_op jit(solution)/shard_map/brck,bkj->brcj/dot_general | solution.py:29
  22.2 0.6 fusion.3
  22.8 1.3 %copy-done = f32[128,32,2,128]{3,1,2,0:T(8,128)} copy-done((f32[128,32,2,128]{3,1,2,0:T(8,128)}, f32[128,32,2,128]{3,1,2,0:T(8,128)S(1)}, u32[]{:S(2)}) %copy-start) | copy-done | bytes 4194328
  24.1 8.9 %collective-permute-done = bf16[128,32,128]{2,1,0:T(8,128)(2,1)} collective-permute-done((bf16[128,32,128]{2,1,0:T(8,128)(2,1)}, bf16[128,32,128]{2,1,0:T(8,128)(2,1)}, u32[]{:S(2)}, u32[]{:S(2)}) %collective-permute-start) | collective-permute-done | bytes 1048608 | tf_op jit(solution)/shard_map/ppermute | solution.py:14
  33.0 2.0 %gather_fusion = bf16[128,32,128]{2,1,0:T(8,128)(2,1)S(1)} fusion(bf16[128,32,128]{2,1,0:T(8,128)(2,1)} %collective-permute-done, s32[1024]{0:T(1024)S(1)} %pad_clamp_fusion), kind=kCustom, calls=%fused_computation | custom fusion | bytes 2097664 | tf_op jit(solution)/shard_map/jit(_take)/gather | solution.py:45
  35.0 1.7 %copy.47 = bf16[128,32,128]{0,2,1:T(8,128)(2,1)} copy(bf16[128,32,128]{2,1,0:T(8,128)(2,1)S(1)} %gather_fusion) | data formatting | bytes 2097152 | tf_op jit(solution)/shard_map/jit(_take)/gather | solution.py:45
  36.7 1.3 %broadcast_select_fusion = bf16[128,32,2,64]{0,3,2,1:T(8,128)(2,1)S(1)} fusion(bf16[128,32,2,64]{0,3,2,1:T(8,128)(2,1)} %bitcast.71, pred[128]{0:T(512)(128)(4,1)S(1)} %compare_and_fusion), kind=kLoop, calls=%fused_computation.21 | loop fusion | flops 524288 | bytes 2097280 | tf_op jit(solution)/shard_map/jit(_take)/select_n | solution.py:45
  38.0 3.7 %copy.63 = bf16[128,32,2,64]{3,1,0,2:T(8,128)(2,1)} copy(bf16[128,32,2,64]{0,3,2,1:T(8,128)(2,1)S(1)} %broadcast_select_fusion) | data formatting | bytes 2097152 | tf_op jit(solution)/shard_map/jit(_take)/select_n | solution.py:45
  41.7 3.1 %fusion.2 = f32[128,32,2,128]{3,1,0,2:T(8,128)S(1)} fusion(bf16[128,32,2,64]{3,1,0,2:T(8,128)(2,1)} %copy.63, bf16[128,2,64,128]{3,2,0,1:T(8,128)(2,1)} %bitcast.69), kind=kOutput, calls=%fused_computation.7 | convolution fusion | flops 134217728 | bytes 8388608 | tf_op jit(solution)/shard_map/brck,bkj->brcj/dot_general | solution.py:29
  44.8 0.4 copy-done.1
  45.2 1.7 %fusion.1 = (f32[128,32,64]{2,1,0:T(8,128)S(1)}, f32[128,32,64]{2,1,0:T(8,128)S(1)}, f32[128,32,64]{2,1,0:T(8,128)S(1)}) fusion(f32[128,32,2,128]{3,1,0,2:T(8,128)S(1)} %fusion.2, f32[128,32,2,128]{3,1,2,0:T(8,128)S(1)} %copy-done.1), kind=kLoop, calls=%fused_computation.5 | loop fusion | flops 786432 | bytes 9437184 | tf_op jit(solution)/shard_map/sub | solution.py:32
  46.8 2.5 %maximum_add_fusion = f32[128,32,128]{2,1,0:T(8,128)} fusion(f32[128,32,64]{2,1,0:T(8,128)S(1)} %fusion.3, f32[128,32,64]{2,1,0:T(8,128)S(1)} %get-tuple-element.9, f32[128,32,64]{2,1,0:T(8,128)S(1)} %get-tuple-element.6, f32[128,32,64]{2,1,0:T(8,128)S(1)} %get-tuple-element.5), kind=kLoop, calls=%fused_computation.16 | loop fusion | flops 1572864 | bytes 6291456 | tf_op jit(solution)/shard_map/add | solution.py:47
  49.4 45.5 %reduce-scatter.2.cloned.1.call-done = f32[32,32,128]{2,1,0:T(8,128)} async-done(((f32[128,32,128]{2,1,0:T(8,128)}), f32[32,32,128]{2,1,0:T(8,128)}) %reduce-scatter.2.cloned.1.call-update) | async-done | bytes 524304 | tf_op jit(solution)/shard_map/reduce_scatter | solution.py:46
  94.9 1.5 %collective-permute-start.1 = (f32[32,32,128]{2,1,0:T(8,128)}, f32[32,32,128]{2,1,0:T(8,128)S(1)}, u32[]{:S(2)}, u32[]{:S(2)}) collective-permute-start(f32[32,32,128]{2,1,0:T(8,128)} %reduce-scatter.2.cloned.1.call-done), channel_id=1, source_target_pairs={{0,8},{8,0},{4,12},{12,4},{16,24},{24,16},{20,28},{28,20},{1,9},{9... | collective-permute-start | bytes 1572872 | tf_op jit(solution)/shard_map/ppermute | solution.py:14
  96.3 1.7 %reshape.21 = f32[32,32,2,64]{3,2,1,0:T(2,128)S(1)} reshape(f32[32,32,128]{2,1,0:T(8,128)} %reduce-scatter.2.cloned.1.call-done) | data formatting | bytes 1048576 | tf_op jit(solution)/shard_map/reshape | solution.py:20
  98.0 1.7 %fusion.9 = f32[32,32,2,128]{3,1,2,0:T(8,128)S(1)} fusion(f32[32,32,2,64]{3,2,1,0:T(2,128)S(1)} %reshape.21, bf16[128,2,64,128]{3,2,1,0:T(8,128)(2,1)} %param.6, s32[]{:T(128)S(6)} %select_n.15), kind=kOutput, calls=%fused_computation.19 | convolution fusion | flops 201326592 | bytes 2097156 | tf_op jit(solution)/shard_map/brck,bkj->brcj/dot_general | solution.py:22
  100.1 8.5 %collective-permute-done.1 = f32[32,32,128]{2,1,0:T(8,128)S(1)} collective-permute-done((f32[32,32,128]{2,1,0:T(8,128)}, f32[32,32,128]{2,1,0:T(8,128)S(1)}, u32[]{:S(2)}, u32[]{:S(2)}) %collective-permute-start.1) | collective-permute-done | bytes 524320 | tf_op jit(solution)/shard_map/ppermute | solution.py:14
  108.6 0.6 reshape.22
  109.2 1.7 %fusion.7 = f32[32,32,2,128]{3,1,0,2:T(8,128)S(1)} fusion(f32[32,32,2,64]{3,2,1,0:T(2,128)S(1)} %reshape.22, bf16[128,2,64,128]{3,2,1,0:T(8,128)(2,1)} %param.6, s32[]{:T(128)S(6)} %select_n.15, s32[]{:T(128)S(6)} %add.56), kind=kOutput, calls=%fused_computation.17 | convolution fusion | flops 201326592 | bytes 2097160 | tf_op jit(solution)/shard_map/brck,bkj->brcj/dot_general | solution.py:22
  111.2 1.1 maximum_add_fusion.1
  (12 shorter events, 0.8 us)
Async XLA Ops:
  6.5 88.3 %reduce-scatter.2.cloned.1.call-start = ((), (), s32[]{:S(2)}) async-start(), calls=%async_computation.1 | async-start | bytes 2621440 | tf_op jit(solution)/shard_map/reduce_scatter | solution.py:46
  6.5 26.4 %collective-permute-start = (bf16[128,32,128]{2,1,0:T(8,128)(2,1)}, bf16[128,32,128]{2,1,0:T(8,128)(2,1)}, u32[]{:S(2)}, u32[]{:S(2)}) collective-permute-start(bf16[128,32,128]{2,1,0:T(8,128)(2,1)} %bitcast.72), channel_id=1, source_target_pairs={{0,16},{16,0},{4,20},{20,4},{8,24},{24,8},{12,28},{28,12},{1,17},{... | collective-permute-start | bytes 3145736 | tf_op jit(solution)/shard_map/ppermute | solution.py:14
  16.8 3.0 %copy-start.2 = (s32[128]{0:T(128)S(1)}, s32[128]{0:T(128)}, u32[]{:S(2)}) copy-start(s32[128]{0:T(128)} %param.7) | copy-start | bytes 1540
  22.2 1.9 %copy-start = (f32[128,32,2,128]{3,1,2,0:T(8,128)}, f32[128,32,2,128]{3,1,2,0:T(8,128)S(1)}, u32[]{:S(2)}) copy-start(f32[128,32,2,128]{3,1,2,0:T(8,128)S(1)} %fusion.6) | copy-start | bytes 12582916
  41.7 3.4 %copy-start.1 = (f32[128,32,2,128]{3,1,2,0:T(8,128)S(1)}, f32[128,32,2,128]{3,1,2,0:T(8,128)}, u32[]{:S(2)}) copy-start(f32[128,32,2,128]{3,1,2,0:T(8,128)} %copy-done) | copy-start | bytes 12582916
  94.9 13.7 %collective-permute-start.1 = (f32[32,32,128]{2,1,0:T(8,128)}, f32[32,32,128]{2,1,0:T(8,128)S(1)}, u32[]{:S(2)}, u32[]{:S(2)}) collective-permute-start(f32[32,32,128]{2,1,0:T(8,128)} %reduce-scatter.2.cloned.1.call-done), channel_id=1, source_target_pairs={{0,8},{8,0},{4,12},{12,4},{16,24},{24,16},{20,28},{28,20},{1,9},{9... | collective-permute-start | bytes 1572872 | tf_op jit(solution)/shard_map/ppermute | solution.py:14
Sparse Core Ops, SparseCore 0:
  49.5 45.3 reduce-scatter.1
where the time goes:
time: 120 us; the launch traced here: 119 us
  waiting for transfers between devices  62.8 us (52%)
  local copies, waits for them, and re-layouts  21.7 us (18%)
  between operations  13.5 us (11%)
  matrix products  8.71 us (7%)
  other arithmetic  8.01 us (7%)
  starting transfers between devices  4.43 us (4%)
    reduce_scatter x1, waiting for transfers between devices, on_device(): lax.psum_scatter(apply_factor(local_values, local_factors[:, 0], False) +...  45.5 us
    ppermute x2, waiting for transfers between devices, swapped(): return lax.ppermute(block, axis, route)  17.3 us
    unnamed x8, local copies, waits for them, and re-layouts  9.03 us
    dot_general x2, matrix products, apply_factor(): jnp.einsum('brck,bkj->brcj', split_values, factor, preferred_element_type...  5.34 us
    ppermute x2, starting transfers between devices, swapped(): return lax.ppermute(block, axis, route)  4.43 us
    gather x2, local copies, waits for them, and re-layouts, on_device(): partner_values = jnp.take(remote_values, pattern, axis=0)  3.72 us
    select_n x1, local copies, waits for them, and re-layouts, on_device(): partner_values = jnp.take(remote_values, pattern, axis=0)  3.69 us
    dot_general x2, matrix products, apply_factor(): jnp.einsum('brck,bkj->brcj', split_values, factor.astype(jnp.float32), pr...  3.37 us
  transfers between devices with their start and end apart: 3, of which 3 were waited for; matrix products, arithmetic and copies ran while one was open for 14% of the time, Pallas kernels for 0%

commit v1 on v0

v1 whole, which is shorter than its diff:
```python
import functools

import jax
import jax.numpy as jnp
from jax import lax
from jax.experimental import pallas as pl
from jax.experimental.pallas import tpu as pltpu
from jax.sharding import PartitionSpec as P

CHUNKS = (8, 8, 8, 8)
VMEM = pl.BlockSpec(memory_space=pltpu.VMEM)
SMEM = pl.BlockSpec(memory_space=pltpu.SMEM)
PARAMS = pltpu.CompilerParams(vmem_limit_bytes=16 << 20)


def swapped(block, axis, mask):
    return lax.ppermute(block, axis, [(i, i ^ mask) for i in range(lax.axis_size(axis))])


def left_half(shape):
    return lax.broadcasted_iota(jnp.int32, shape, len(shape) - 1) < shape[-1] // 2


def stacked(own, partner):
    half = own.shape[-1] // 2
    left = left_half(own.shape)
    top = jnp.where(left, own, pltpu.roll(partner, half, 1))
    bottom = jnp.where(left, pltpu.roll(own, half, 1), partner)
    return jnp.concatenate([top, bottom], axis=0)


def folded(product):
    rows = product.shape[0] // 2
    turned = pltpu.roll(product[rows:], product.shape[1] // 2, 1)
    return product[:rows] + jnp.where(left_half(turned.shape), -turned, turned)


def encode(read, peak, out):
    count = out.shape[0] - 1
    exponent = jnp.floor(jnp.log2(jnp.maximum(peak, 1e-30))) + 1.0
    scale = jnp.exp2(15.0 - exponent)
    for i in range(count):
        code = jnp.clip(jnp.round(read(i) * scale), -32767.0, 32767.0)
        out[i] = code.astype(jnp.int32).astype(jnp.int16)
    out[count] = exponent.astype(jnp.int32).astype(jnp.int16)


def unit(coded):
    return jnp.exp2(coded[coded.shape[0] - 1].astype(jnp.float32) - 15.0)


def first_kernel(me_ref, pattern_ref, own_ref, partner_ref, factor_ref, *rest):
    *outs, total = rest
    me = me_ref[0]
    rows, width = own_ref.shape[1:]
    share = outs[0].shape[0]
    for turn in (*range(1, len(outs)), 0):
        base = (me ^ turn) * share
        out = outs[turn]
        peak = jnp.zeros((rows, width), jnp.float32)
        for i in range(share):
            own = own_ref[base + i].astype(jnp.float32)
            partner = partner_ref[pattern_ref[base + i]].astype(jnp.float32)
            values = stacked(own, partner).astype(jnp.bfloat16)
            factor = factor_ref[base + i].reshape(width, width)
            result = folded(jnp.dot(values, factor, preferred_element_type=jnp.float32))
            if turn == 0:
                out[i] = result
            else:
                total[turn - 1, i] = result
                peak = jnp.maximum(peak, jnp.abs(result))
        if turn:
            encode(lambda i: total[turn - 1, i], peak, out)


def first_level(me, pattern, own, partner, factors, parts):
    blocks, rows, width = own.shape
    share = blocks // parts
    coded = jax.ShapeDtypeStruct((share + 1, rows, width), jnp.int16)
    return pl.pallas_call(
        first_kernel,
        in_specs=[SMEM, SMEM, VMEM, VMEM, VMEM],
        out_specs=[VMEM] * parts,
        out_shape=[jax.ShapeDtypeStruct((share, rows, width), jnp.float32)] + [coded] * (parts - 1),
        scratch_shapes=[pltpu.VMEM((parts - 1, share, rows, width), jnp.float32)],
        compiler_params=PARAMS,
        name="first_level",
    )(me, pattern, own, partner, factors)


def sum_kernel(own_ref, *rest):
    *coded, total, out = rest
    units = [unit(c) for c in coded]
    peak = jnp.zeros(own_ref.shape[1:], jnp.float32)
    for i in range(own_ref.shape[0]):
        result = own_ref[i]
        for c, u in zip(coded, units):
            result = result + c[i].astype(jnp.float32) * u
        total[i] = result
        peak = jnp.maximum(peak, jnp.abs(result))
    encode(lambda i: total[i], peak, out)


def quarter_sum(own, coded):
    share, rows, width = own.shape
    return pl.pallas_call(
        sum_kernel,
        in_specs=[VMEM] * (1 + len(coded)),
        out_specs=[VMEM, VMEM],
        out_shape=[
            jax.ShapeDtypeStruct((share, rows, width), jnp.float32),
            jax.ShapeDtypeStruct((share + 1, rows, width), jnp.int16),
        ],
        compiler_params=PARAMS,
        name="quarter_sum",
    )(own, *coded)


def second_kernel(chunks, *refs):
    owns, partners, factor_ref, out = refs[:chunks], refs[chunks : 2 * chunks], refs[-2], refs[-1]
    width = out.shape[2]
    units = [unit(c) for c in partners]
    for i in range(out.shape[0]):
        own = jnp.concatenate([o[i] for o in owns], axis=0)
        partner = jnp.concatenate([c[i].astype(jnp.float32) * u for c, u in zip(partners, units)], axis=0)
        values = stacked(own, partner)
        high = values.astype(jnp.bfloat16)
        low = (values - high.astype(jnp.float32)).astype(jnp.bfloat16)
        factor = factor_ref[i].reshape(width, width)
        product = jnp.dot(jnp.concatenate([high, low], axis=0), factor, preferred_element_type=jnp.float32)
        out[i] = folded(product[: 2 * own.shape[0]] + product[2 * own.shape[0] :])


def second_level(owns, partners, factors):
    share, _, width = owns[0].shape
    rows = sum(o.shape[1] for o in owns)
    return pl.pallas_call(
        functools.partial(second_kernel, len(owns)),
        in_specs=[VMEM] * (2 * len(owns) + 1),
        out_specs=VMEM,
        out_shape=jax.ShapeDtypeStruct((share, rows, width), jnp.float32),
        compiler_params=PARAMS,
        name="second_level",
    )(*owns, *partners, factors)


def on_device(sources, first_factors, second_factors, pattern):
    half = lax.axis_size("tgt") // 2
    parts = lax.axis_size("src")
    sources, first_factors = sources[0], first_factors[0]
    share = sources.shape[0] // parts
    me = lax.axis_index("src").astype(jnp.int32)
    starts = [sum(CHUNKS[:c]) for c in range(len(CHUNKS))]
    values = [sources[:, start : start + rows] for start, rows in zip(starts, CHUNKS)]
    partners = [swapped(v, "tgt", half) for v in values]
    mine = lax.dynamic_slice_in_dim(second_factors, me * share, share, 0)
    owns, others = [], []
    for own, partner in zip(values, partners):
        kept, *sent = first_level(me.reshape(1), pattern, own, partner, first_factors, parts)
        arrived = [swapped(s, "src", turn + 1) for turn, s in enumerate(sent)]
        total, coded = quarter_sum(kept, arrived)
        owns.append(total)
        others.append(swapped(coded, "tgt", half // 2))
    return second_level(owns, others, mine)


def solution(mesh):
    return jax.shard_map(
        on_device,
        mesh=mesh,
        in_specs=(
            P("src", "tgt", None, None),
            P("src", "tgt", None, None, None),
            P("tgt", None, None, None),
            P("tgt"),
        ),
        out_specs=P(("tgt", "src"), None, None),
        check_vma=False,
    )
```

time: 120 us -> 54.4 us (0.45)
  waiting for transfers between devices: 62.8 us -> 9.51 us
  starting transfers between devices: 4.43 us -> 29.8 us
  local copies, waits for them, and re-layouts: 21.7 us -> 5.42 us
  between operations: 13.5 us -> 0.12 us
  Pallas kernels: 0 us -> 9.31 us
  matrix products: 8.71 us -> 0 us
  other arithmetic: 8.01 us -> 0 us
    reduce_scatter x1 -> x0, waiting for transfers between devices: 45.5 us -> none  [on_device(): lax.psum_scatter(apply_factor(local_values, local_factors[:, 0], False) +...]
    ppermute x2 -> x20, starting transfers between devices: 4.43 us -> 29.8 us  [swapped(): lax.ppermute(block, axis, [(i, i ^ mask) for i in range(lax.axis_size(axi...]
    pallas_call x0 -> x9, Pallas kernels: none -> 9.31 us  [the longest x4 7.52 us: first_level(): pl.pallas_call(first_kernel, in_specs=[SMEM, SMEM, VMEM, VMEM, VMEM], out...]
    dot_general x4 -> x0, matrix products: 8.71 us -> none  [the longest x2 5.34 us: apply_factor(): jnp.einsum('brck,bkj->brcj', split_values, factor, preferred_element_type...]
    ppermute x2 -> x20, waiting for transfers between devices: 17.3 us -> 9.51 us  [swapped(): lax.ppermute(block, axis, [(i, i ^ mask) for i in range(lax.axis_size(axi...]
    unnamed x8 -> x6, local copies, waits for them, and re-layouts: 9.03 us -> 2.85 us
    add x4 -> x0, other arithmetic: 4.45 us -> none  [the longest x1 2.5 us: on_device(): apply_factor(local_values, local_factors[:, 0], False)]
    gather x2 -> x0, local copies, waits for them, and re-layouts: 3.72 us -> none  [on_device(): partner_values = jnp.take(remote_values, pattern, axis=0)]
  transfers between devices with their start and end apart: 3 -> 20, of which waited for: 3 -> 4; matrix products, arithmetic and copies ran while one was open for 14% -> 2% of each run, Pallas kernels for 0% -> 15%
where the time goes in v1:
time: 54.4 us; the launch traced here: 54.1 us
  starting transfers between devices  29.8 us (55%)
  waiting for transfers between devices  9.51 us (17%)
  Pallas kernels  9.31 us (17%)
  local copies, waits for them, and re-layouts  5.42 us (10%)
    ppermute x20, starting transfers between devices, swapped(): lax.ppermute(block, axis, [(i, i ^ mask) for i in range(lax.axis_size(axi...  29.8 us
    ppermute x20, waiting for transfers between devices, swapped(): lax.ppermute(block, axis, [(i, i ^ mask) for i in range(lax.axis_size(axi...  9.51 us
    pallas_call x4, Pallas kernels, first_level(): pl.pallas_call(first_kernel, in_specs=[SMEM, SMEM, VMEM, VMEM, VMEM], out...  7.52 us
    unnamed x6, local copies, waits for them, and re-layouts  2.85 us
    pallas_call x1, Pallas kernels, second_level(): pl.pallas_call(functools.partial(second_kernel, len(owns)), in_specs=[VME...  1.39 us
    dynamic_slice x1, local copies, waits for them, and re-layouts, on_device(): mine = lax.dynamic_slice_in_dim(second_factors, me * share, share, 0)  1.29 us
    slice x1, local copies, waits for them, and re-layouts, on_device(): sources[:, start:start + rows]  1.28 us
  transfers between devices with their start and end apart: 20, of which 4 were waited for; matrix products, arithmetic and copies ran while one was open for 2% of the time, Pallas kernels for 15%

profile of v1, /device:TPU:0, one launch (start us, length us, event | category | flops | bytes accessed | tf_op | source)
XLA Modules:
  0.0 54.1 jit_solution(11044185104130871170)
XLA Ops:
  0.0 1.3 %fusion = (bf16[128,8,128]{2,1,0:T(8,128)(2,1)S(1)}, bf16[128,8,128]{2,1,0:T(8,128)(2,1)S(1)}, bf16[128,8,128]{2,1,0:T(8,128)(2,1)S(1)}, bf16[128,8,128]{2,1,0:T(8,128)(2,1)S(1)}) fusion(bf16[128,32,128]{2,1,0:T(8,128)(2,1)} %bitcast.7), kind=kLoop, calls=%fused_computation.1 | loop fusion | bytes 2097152 | tf_op jit(solution)/shard_map/slice | solution.py:154
  1.3 3.0 %collective-permute-start.12 = (bf16[128,8,128]{2,1,0:T(8,128)(2,1)S(1)}, bf16[128,8,128]{2,1,0:T(8,128)(2,1)S(1)}, u32[]{:S(2)}, u32[]{:S(2)}) collective-permute-start(bf16[128,8,128]{2,1,0:T(8,128)(2,1)S(1)} %get-tuple-element.53.own_ref), channel_id=1, source_target_pairs={{0,16},{4,20},{8,24},{12,28},{16,0},{20,4},{24,8},{28,12},{1,17},{... | collective-permute-start | bytes 786440 | tf_op jit(solution)/shard_map/ppermute | solution.py:17
  4.4 1.9 %collective-permute-start.4 = (bf16[128,8,128]{2,1,0:T(8,128)(2,1)S(1)}, bf16[128,8,128]{2,1,0:T(8,128)(2,1)S(1)}, u32[]{:S(2)}, u32[]{:S(2)}) collective-permute-start(bf16[128,8,128]{2,1,0:T(8,128)(2,1)S(1)} %get-tuple-element.55.own_ref), channel_id=1, source_target_pairs={{0,16},{4,20},{8,24},{12,28},{16,0},{20,4},{24,8},{28,12},{1,17},{... | collective-permute-start | bytes 786440 | tf_op jit(solution)/shard_map/ppermute | solution.py:17
  6.4 5.0 %collective-permute-done.12.partner_ref = bf16[128,8,128]{2,1,0:T(8,128)(2,1)S(1)} collective-permute-done((bf16[128,8,128]{2,1,0:T(8,128)(2,1)S(1)}, bf16[128,8,128]{2,1,0:T(8,128)(2,1)S(1)}, u32[]{:S(2)}, u32[]{:S(2)}) %collective-permute-start.12) | collective-permute-done | bytes 262176 | tf_op jit(solution)/shard_map/ppermute | solution.py:17
  11.5 2.2 %copy-done = bf16[1,128,2,64,128]{4,3,2,1,0:T(8,128)(2,1)S(1)} copy-done((bf16[1,128,2,64,128]{4,3,2,1,0:T(8,128)(2,1)S(1)}, bf16[1,128,2,64,128]{4,3,2,1,0:T(8,128)(2,1)}, u32[]{:S(2)}) %copy-start) | copy-done | bytes 4194328
  14.3 1.9 %first_level.7 = (f32[32,8,128]{2,1,0:T(8,128)S(1)}, s16[33,8,128]{2,1,0:T(8,128)(2,1)S(1)}, s16[33,8,128]{2,1,0:T(8,128)(2,1)S(1)}, s16[33,8,128]{2,1,0:T(8,128)(2,1)S(1)}) custom-call(s32[1]{0:T(128)} %bitcast.me_ref, s32[128]{0:T(128)S(1)} %copy-done.2, bf16[128,8,128]{2,1,0:T(8,128)(2,1)S(1)} %get-tuple-element.53.own_ref, ...), custom_call_target="tpu_custom_call" | custom-call | tf_op jit(solution)/shard_map/first_level/pallas_call | solution.py:80
  16.2 2.2 %collective-permute-start.13 = (s16[33,8,128]{2,1,0:T(8,128)(2,1)S(1)}, s16[33,8,128]{2,1,0:T(8,128)(2,1)S(1)}, u32[]{:S(2)}, u32[]{:S(2)}) collective-permute-start(s16[33,8,128]{2,1,0:T(8,128)(2,1)S(1)} %get-tuple-element.45), channel_id=1, source_target_pairs={{0,1},{1,0},{2,3},{3,2},{4,5},{5,4},{6,7},{7,6},{8,9},{9,8},{10,11... | collective-permute-start | bytes 202760 | tf_op jit(solution)/shard_map/ppermute | solution.py:17
  18.4 2.6 %collective-permute-start.14 = (s16[33,8,128]{2,1,0:T(8,128)(2,1)S(1)}, s16[33,8,128]{2,1,0:T(8,128)(2,1)S(1)}, u32[]{:S(2)}, u32[]{:S(2)}) collective-permute-start(s16[33,8,128]{2,1,0:T(8,128)(2,1)S(1)} %get-tuple-element.46), channel_id=1, source_target_pairs={{0,2},{1,3},{2,0},{3,1},{4,6},{5,7},{6,4},{7,5},{8,10},{9,11},{10,... | collective-permute-start | bytes 202760 | tf_op jit(solution)/shard_map/ppermute | solution.py:17
  21.2 1.9 %first_level.6 = (f32[32,8,128]{2,1,0:T(8,128)S(1)}, s16[33,8,128]{2,1,0:T(8,128)(2,1)S(1)}, s16[33,8,128]{2,1,0:T(8,128)(2,1)S(1)}, s16[33,8,128]{2,1,0:T(8,128)(2,1)S(1)}) custom-call(s32[1]{0:T(128)} %bitcast.me_ref, s32[128]{0:T(128)S(1)} %copy-done.2, bf16[128,8,128]{2,1,0:T(8,128)(2,1)S(1)} %get-tuple-element.54.own_ref, ...), custom_call_target="tpu_custom_call" | custom-call | tf_op jit(solution)/shard_map/first_level/pallas_call | solution.py:80
  23.1 2.7 %collective-permute-start.10 = (s16[33,8,128]{2,1,0:T(8,128)(2,1)S(1)}, s16[33,8,128]{2,1,0:T(8,128)(2,1)S(1)}, u32[]{:S(2)}, u32[]{:S(2)}) collective-permute-start(s16[33,8,128]{2,1,0:T(8,128)(2,1)S(1)} %get-tuple-element.41), channel_id=1, source_target_pairs={{0,2},{1,3},{2,0},{3,1},{4,6},{5,7},{6,4},{7,5},{8,10},{9,11},{10,... | collective-permute-start | bytes 202760 | tf_op jit(solution)/shard_map/ppermute | solution.py:17
  25.8 1.9 %first_level.5 = (f32[32,8,128]{2,1,0:T(8,128)S(1)}, s16[33,8,128]{2,1,0:T(8,128)(2,1)S(1)}, s16[33,8,128]{2,1,0:T(8,128)(2,1)S(1)}, s16[33,8,128]{2,1,0:T(8,128)(2,1)S(1)}) custom-call(s32[1]{0:T(128)} %bitcast.me_ref, s32[128]{0:T(128)S(1)} %copy-done.2, bf16[128,8,128]{2,1,0:T(8,128)(2,1)S(1)} %get-tuple-element.55.own_ref, ...), custom_call_target="tpu_custom_call" | custom-call | tf_op jit(solution)/shard_map/first_level/pallas_call | solution.py:80
  27.7 3.6 %collective-permute-start.11 = (s16[33,8,128]{2,1,0:T(8,128)(2,1)S(1)}, s16[33,8,128]{2,1,0:T(8,128)(2,1)S(1)}, u32[]{:S(2)}, u32[]{:S(2)}) collective-permute-start(s16[33,8,128]{2,1,0:T(8,128)(2,1)S(1)} %get-tuple-element.42), channel_id=1, source_target_pairs={{0,3},{1,2},{2,1},{3,0},{4,7},{5,6},{6,5},{7,4},{8,11},{9,10},{10,... | collective-permute-start | bytes 202760 | tf_op jit(solution)/shard_map/ppermute | solution.py:17
  31.3 2.0 %collective-permute-start.5 = (s16[33,8,128]{2,1,0:T(8,128)(2,1)S(1)}, s16[33,8,128]{2,1,0:T(8,128)(2,1)S(1)}, u32[]{:S(2)}, u32[]{:S(2)}) collective-permute-start(s16[33,8,128]{2,1,0:T(8,128)(2,1)S(1)} %get-tuple-element.35), channel_id=1, source_target_pairs={{0,1},{1,0},{2,3},{3,2},{4,5},{5,4},{6,7},{7,6},{8,9},{9,8},{10,11... | collective-permute-start | bytes 202760 | tf_op jit(solution)/shard_map/ppermute | solution.py:17
  33.3 1.9 %first_level.4 = (f32[32,8,128]{2,1,0:T(8,128)S(1)}, s16[33,8,128]{2,1,0:T(8,128)(2,1)S(1)}, s16[33,8,128]{2,1,0:T(8,128)(2,1)S(1)}, s16[33,8,128]{2,1,0:T(8,128)(2,1)S(1)}) custom-call(s32[1]{0:T(128)} %bitcast.me_ref, s32[128]{0:T(128)S(1)} %copy-done.2, bf16[128,8,128]{2,1,0:T(8,128)(2,1)S(1)} %get-tuple-element.56.own_ref, ...), custom_call_target="tpu_custom_call" | custom-call | tf_op jit(solution)/shard_map/first_level/pallas_call | solution.py:80
  35.3 2.4 %collective-permute-start.7 = (s16[33,8,128]{2,1,0:T(8,128)(2,1)S(1)}, s16[33,8,128]{2,1,0:T(8,128)(2,1)S(1)}, u32[]{:S(2)}, u32[]{:S(2)}) collective-permute-start(s16[33,8,128]{2,1,0:T(8,128)(2,1)S(1)} %get-tuple-element.37), channel_id=1, source_target_pairs={{0,3},{1,2},{2,1},{3,0},{4,7},{5,6},{6,5},{7,4},{8,11},{9,10},{10,... | collective-permute-start | bytes 202760 | tf_op jit(solution)/shard_map/ppermute | solution.py:17
  37.7 1.1 %collective-permute-start.1 = (s16[33,8,128]{2,1,0:T(8,128)(2,1)S(1)}, s16[33,8,128]{2,1,0:T(8,128)(2,1)S(1)}, u32[]{:S(2)}, u32[]{:S(2)}) collective-permute-start(s16[33,8,128]{2,1,0:T(8,128)(2,1)S(1)} %get-tuple-element.30), channel_id=1, source_target_pairs={{0,1},{1,0},{2,3},{3,2},{4,5},{5,4},{6,7},{7,6},{8,9},{9,8},{10,11... | collective-permute-start | bytes 202760 | tf_op jit(solution)/shard_map/ppermute | solution.py:17
  38.8 1.0 %collective-permute-start.2 = (s16[33,8,128]{2,1,0:T(8,128)(2,1)S(1)}, s16[33,8,128]{2,1,0:T(8,128)(2,1)S(1)}, u32[]{:S(2)}, u32[]{:S(2)}) collective-permute-start(s16[33,8,128]{2,1,0:T(8,128)(2,1)S(1)} %get-tuple-element.31), channel_id=1, source_target_pairs={{0,2},{1,3},{2,0},{3,1},{4,6},{5,7},{6,4},{7,5},{8,10},{9,11},{10,... | collective-permute-start | bytes 202760 | tf_op jit(solution)/shard_map/ppermute | solution.py:17
  39.8 2.3 %collective-permute-start.3 = (s16[33,8,128]{2,1,0:T(8,128)(2,1)S(1)}, s16[33,8,128]{2,1,0:T(8,128)(2,1)S(1)}, u32[]{:S(2)}, u32[]{:S(2)}) collective-permute-start(s16[33,8,128]{2,1,0:T(8,128)(2,1)S(1)} %get-tuple-element.32), channel_id=1, source_target_pairs={{0,3},{1,2},{2,1},{3,0},{4,7},{5,6},{6,5},{7,4},{8,11},{9,10},{10,... | collective-permute-start | bytes 202760 | tf_op jit(solution)/shard_map/ppermute | solution.py:17
  42.3 2.2 %collective-permute-done.6.rest_1_ = s16[33,8,128]{2,1,0:T(8,128)(2,1)S(1)} collective-permute-done((s16[33,8,128]{2,1,0:T(8,128)(2,1)S(1)}, s16[33,8,128]{2,1,0:T(8,128)(2,1)S(1)}, u32[]{:S(2)}, u32[]{:S(2)}) %collective-permute-start.6) | collective-permute-done | bytes 67616 | tf_op jit(solution)/shard_map/ppermute | solution.py:17
  44.6 1.5 %collective-permute-start.19 = (s16[33,8,128]{2,1,0:T(8,128)(2,1)S(1)}, s16[33,8,128]{2,1,0:T(8,128)(2,1)S(1)}, u32[]{:S(2)}, u32[]{:S(2)}) collective-permute-start(s16[33,8,128]{2,1,0:T(8,128)(2,1)S(1)} %get-tuple-element.52), channel_id=1, source_target_pairs={{0,8},{4,12},{8,0},{12,4},{16,24},{20,28},{24,16},{28,20},{1,9},{5... | collective-permute-start | bytes 202760 | tf_op jit(solution)/shard_map/ppermute | solution.py:17
  46.7 1.6 %collective-permute-start.17 = (s16[33,8,128]{2,1,0:T(8,128)(2,1)S(1)}, s16[33,8,128]{2,1,0:T(8,128)(2,1)S(1)}, u32[]{:S(2)}, u32[]{:S(2)}) collective-permute-start(s16[33,8,128]{2,1,0:T(8,128)(2,1)S(1)} %get-tuple-element.50), channel_id=1, source_target_pairs={{0,8},{4,12},{8,0},{12,4},{16,24},{20,28},{24,16},{28,20},{1,9},{5... | collective-permute-start | bytes 202760 | tf_op jit(solution)/shard_map/ppermute | solution.py:17
  49.2 1.3 %constant_dynamic-slice_fusion.refs_8_ = bf16[32,2,64,128]{3,2,1,0:T(8,128)(2,1)S(1)} fusion(bf16[128,2,64,128]{3,2,1,0:T(8,128)(2,1)} %param.6, s32[]{:T(128)S(6)} %select_n.3), kind=kLoop, calls=%fused_computation | loop fusion | bytes 2097156 | tf_op jit(solution)/shard_map/dynamic_slice | solution.py:156
  51.1 1.7 %collective-permute-done.16.refs_4_ = s16[33,8,128]{2,1,0:T(8,128)(2,1)S(1)} collective-permute-done((s16[33,8,128]{2,1,0:T(8,128)(2,1)S(1)}, s16[33,8,128]{2,1,0:T(8,128)(2,1)S(1)}, u32[]{:S(2)}, u32[]{:S(2)}) %collective-permute-start.16) | collective-permute-done | bytes 67616 | tf_op jit(solution)/shard_map/ppermute | solution.py:17
  52.7 1.4 %second_level.1 = f32[32,32,128]{2,1,0:T(8,128)} custom-call(f32[32,8,128]{2,1,0:T(8,128)S(1)} %get-tuple-element.33.refs_0_, f32[32,8,128]{2,1,0:T(8,128)S(1)} %get-tuple-element.38.refs_1_, f32[32,8,128]{2,1,0:T(8,128)S(1)} %get-tuple-element.43.refs_2_, f32[32,8,128]{2,1,0:T(8,128)S(1)} %get-tuple-element.48.refs_3_, ...), custom_call_target="tpu_custom_call" | custom-call | tf_op jit(solution)/shard_map/second_level/pallas_call | solution.py:137
  (33 shorter events, 3.5 us)
Async XLA Ops:
  1.3 10.2 %collective-permute-start.12 = (bf16[128,8,128]{2,1,0:T(8,128)(2,1)S(1)}, bf16[128,8,128]{2,1,0:T(8,128)(2,1)S(1)}, u32[]{:S(2)}, u32[]{:S(2)}) collective-permute-start(bf16[128,8,128]{2,1,0:T(8,128)(2,1)S(1)} %get-tuple-element.53.own_ref), channel_id=1, source_target_pairs={{0,16},{4,20},{8,24},{12,28},{16,0},{20,4},{24,8},{28,12},{1,17},{... | collective-permute-start | bytes 786440 | tf_op jit(solution)/shard_map/ppermute | solution.py:17
  4.3 16.6 %collective-permute-start.8 = (bf16[128,8,128]{2,1,0:T(8,128)(2,1)S(1)}, bf16[128,8,128]{2,1,0:T(8,128)(2,1)S(1)}, u32[]{:S(2)}, u32[]{:S(2)}) collective-permute-start(bf16[128,8,128]{2,1,0:T(8,128)(2,1)S(1)} %get-tuple-element.54.own_ref), channel_id=1, source_target_pairs={{0,16},{4,20},{8,24},{12,28},{16,0},{20,4},{24,8},{28,12},{1,17},{... | collective-permute-start | bytes 786440 | tf_op jit(solution)/shard_map/ppermute | solution.py:17
  4.4 18.7 %collective-permute-start.4 = (bf16[128,8,128]{2,1,0:T(8,128)(2,1)S(1)}, bf16[128,8,128]{2,1,0:T(8,128)(2,1)S(1)}, u32[]{:S(2)}, u32[]{:S(2)}) collective-permute-start(bf16[128,8,128]{2,1,0:T(8,128)(2,1)S(1)} %get-tuple-element.55.own_ref), channel_id=1, source_target_pairs={{0,16},{4,20},{8,24},{12,28},{16,0},{20,4},{24,8},{28,12},{1,17},{... | collective-permute-start | bytes 786440 | tf_op jit(solution)/shard_map/ppermute | solution.py:17
  6.3 21.4 %collective-permute-start = (bf16[128,8,128]{2,1,0:T(8,128)(2,1)S(1)}, bf16[128,8,128]{2,1,0:T(8,128)(2,1)S(1)}, u32[]{:S(2)}, u32[]{:S(2)}) collective-permute-start(bf16[128,8,128]{2,1,0:T(8,128)(2,1)S(1)} %get-tuple-element.56.own_ref), channel_id=1, source_target_pairs={{0,16},{4,20},{8,24},{12,28},{16,0},{20,4},{24,8},{28,12},{1,17},{... | collective-permute-start | bytes 786440 | tf_op jit(solution)/shard_map/ppermute | solution.py:17
  11.5 2.2 %copy-start = (bf16[1,128,2,64,128]{4,3,2,1,0:T(8,128)(2,1)S(1)}, bf16[1,128,2,64,128]{4,3,2,1,0:T(8,128)(2,1)}, u32[]{:S(2)}) copy-start(bf16[1,128,2,64,128]{4,3,2,1,0:T(8,128)(2,1)} %param.5) | copy-start | bytes 12582916
  13.6 0.7 %copy-start.2 = (s32[128]{0:T(128)S(1)}, s32[128]{0:T(128)}, u32[]{:S(2)}) copy-start(s32[128]{0:T(128)} %pattern_ref.7) | copy-start | bytes 1540
  16.2 15.1 %collective-permute-start.13 = (s16[33,8,128]{2,1,0:T(8,128)(2,1)S(1)}, s16[33,8,128]{2,1,0:T(8,128)(2,1)S(1)}, u32[]{:S(2)}, u32[]{:S(2)}) collective-permute-start(s16[33,8,128]{2,1,0:T(8,128)(2,1)S(1)} %get-tuple-element.45), channel_id=1, source_target_pairs={{0,1},{1,0},{2,3},{3,2},{4,5},{5,4},{6,7},{7,6},{8,9},{9,8},{10,11... | collective-permute-start | bytes 202760 | tf_op jit(solution)/shard_map/ppermute | solution.py:17
  18.4 13.0 %collective-permute-start.14 = (s16[33,8,128]{2,1,0:T(8,128)(2,1)S(1)}, s16[33,8,128]{2,1,0:T(8,128)(2,1)S(1)}, u32[]{:S(2)}, u32[]{:S(2)}) collective-permute-start(s16[33,8,128]{2,1,0:T(8,128)(2,1)S(1)} %get-tuple-element.46), channel_id=1, source_target_pairs={{0,2},{1,3},{2,0},{3,1},{4,6},{5,7},{6,4},{7,5},{8,10},{9,11},{10,... | collective-permute-start | bytes 202760 | tf_op jit(solution)/shard_map/ppermute | solution.py:17
  20.9 12.4 %copy-start.1 = (bf16[1,128,2,64,128]{4,3,2,1,0:T(8,128)(2,1)S(1)}, bf16[1,128,2,64,128]{4,3,2,1,0:T(8,128)(2,1)}, u32[]{:S(2)}) copy-start(bf16[1,128,2,64,128]{4,3,2,1,0:T(8,128)(2,1)} %param.5) | copy-start | bytes 12582916
  20.9 14.3 %collective-permute-start.15 = (s16[33,8,128]{2,1,0:T(8,128)(2,1)S(1)}, s16[33,8,128]{2,1,0:T(8,128)(2,1)S(1)}, u32[]{:S(2)}, u32[]{:S(2)}) collective-permute-start(s16[33,8,128]{2,1,0:T(8,128)(2,1)S(1)} %get-tuple-element.47), channel_id=1, source_target_pairs={{0,3},{1,2},{2,1},{3,0},{4,7},{5,6},{6,5},{7,4},{8,11},{9,10},{10,... | collective-permute-start | bytes 202760 | tf_op jit(solution)/shard_map/ppermute | solution.py:17
  23.1 12.2 %collective-permute-start.10 = (s16[33,8,128]{2,1,0:T(8,128)(2,1)S(1)}, s16[33,8,128]{2,1,0:T(8,128)(2,1)S(1)}, u32[]{:S(2)}, u32[]{:S(2)}) collective-permute-start(s16[33,8,128]{2,1,0:T(8,128)(2,1)S(1)} %get-tuple-element.41), channel_id=1, source_target_pairs={{0,2},{1,3},{2,0},{3,1},{4,6},{5,7},{6,4},{7,5},{8,10},{9,11},{10,... | collective-permute-start | bytes 202760 | tf_op jit(solution)/shard_map/ppermute | solution.py:17
  27.7 10.0 %collective-permute-start.11 = (s16[33,8,128]{2,1,0:T(8,128)(2,1)S(1)}, s16[33,8,128]{2,1,0:T(8,128)(2,1)S(1)}, u32[]{:S(2)}, u32[]{:S(2)}) collective-permute-start(s16[33,8,128]{2,1,0:T(8,128)(2,1)S(1)} %get-tuple-element.42), channel_id=1, source_target_pairs={{0,3},{1,2},{2,1},{3,0},{4,7},{5,6},{6,5},{7,4},{8,11},{9,10},{10,... | collective-permute-start | bytes 202760 | tf_op jit(solution)/shard_map/ppermute | solution.py:17
  31.3 7.5 %collective-permute-start.9 = (s16[33,8,128]{2,1,0:T(8,128)(2,1)S(1)}, s16[33,8,128]{2,1,0:T(8,128)(2,1)S(1)}, u32[]{:S(2)}, u32[]{:S(2)}) collective-permute-start(s16[33,8,128]{2,1,0:T(8,128)(2,1)S(1)} %get-tuple-element.40), channel_id=1, source_target_pairs={{0,1},{1,0},{2,3},{3,2},{4,5},{5,4},{6,7},{7,6},{8,9},{9,8},{10,11... | collective-permute-start | bytes 202760 | tf_op jit(solution)/shard_map/ppermute | solution.py:17
  31.3 8.5 %collective-permute-start.5 = (s16[33,8,128]{2,1,0:T(8,128)(2,1)S(1)}, s16[33,8,128]{2,1,0:T(8,128)(2,1)S(1)}, u32[]{:S(2)}, u32[]{:S(2)}) collective-permute-start(s16[33,8,128]{2,1,0:T(8,128)(2,1)S(1)} %get-tuple-element.35), channel_id=1, source_target_pairs={{0,1},{1,0},{2,3},{3,2},{4,5},{5,4},{6,7},{7,6},{8,9},{9,8},{10,11... | collective-permute-start | bytes 202760 | tf_op jit(solution)/shard_map/ppermute | solution.py:17
  35.2 9.3 %collective-permute-start.6 = (s16[33,8,128]{2,1,0:T(8,128)(2,1)S(1)}, s16[33,8,128]{2,1,0:T(8,128)(2,1)S(1)}, u32[]{:S(2)}, u32[]{:S(2)}) collective-permute-start(s16[33,8,128]{2,1,0:T(8,128)(2,1)S(1)} %get-tuple-element.36), channel_id=1, source_target_pairs={{0,2},{1,3},{2,0},{3,1},{4,6},{5,7},{6,4},{7,5},{8,10},{9,11},{10,... | collective-permute-start | bytes 202760 | tf_op jit(solution)/shard_map/ppermute | solution.py:17
  35.3 10.8 %collective-permute-start.7 = (s16[33,8,128]{2,1,0:T(8,128)(2,1)S(1)}, s16[33,8,128]{2,1,0:T(8,128)(2,1)S(1)}, u32[]{:S(2)}, u32[]{:S(2)}) collective-permute-start(s16[33,8,128]{2,1,0:T(8,128)(2,1)S(1)} %get-tuple-element.37), channel_id=1, source_target_pairs={{0,3},{1,2},{2,1},{3,0},{4,7},{5,6},{6,5},{7,4},{8,11},{9,10},{10,... | collective-permute-start | bytes 202760 | tf_op jit(solution)/shard_map/ppermute | solution.py:17
  37.7 9.0 %collective-permute-start.1 = (s16[33,8,128]{2,1,0:T(8,128)(2,1)S(1)}, s16[33,8,128]{2,1,0:T(8,128)(2,1)S(1)}, u32[]{:S(2)}, u32[]{:S(2)}) collective-permute-start(s16[33,8,128]{2,1,0:T(8,128)(2,1)S(1)} %get-tuple-element.30), channel_id=1, source_target_pairs={{0,1},{1,0},{2,3},{3,2},{4,5},{5,4},{6,7},{7,6},{8,9},{9,8},{10,11... | collective-permute-start | bytes 202760 | tf_op jit(solution)/shard_map/ppermute | solution.py:17
  38.8 9.5 %collective-permute-start.2 = (s16[33,8,128]{2,1,0:T(8,128)(2,1)S(1)}, s16[33,8,128]{2,1,0:T(8,128)(2,1)S(1)}, u32[]{:S(2)}, u32[]{:S(2)}) collective-permute-start(s16[33,8,128]{2,1,0:T(8,128)(2,1)S(1)} %get-tuple-element.31), channel_id=1, source_target_pairs={{0,2},{1,3},{2,0},{3,1},{4,6},{5,7},{6,4},{7,5},{8,10},{9,11},{10,... | collective-permute-start | bytes 202760 | tf_op jit(solution)/shard_map/ppermute | solution.py:17
  39.8 8.5 %collective-permute-start.3 = (s16[33,8,128]{2,1,0:T(8,128)(2,1)S(1)}, s16[33,8,128]{2,1,0:T(8,128)(2,1)S(1)}, u32[]{:S(2)}, u32[]{:S(2)}) collective-permute-start(s16[33,8,128]{2,1,0:T(8,128)(2,1)S(1)} %get-tuple-element.32), channel_id=1, source_target_pairs={{0,3},{1,2},{2,1},{3,0},{4,7},{5,6},{6,5},{7,4},{8,11},{9,10},{10,... | collective-permute-start | bytes 202760 | tf_op jit(solution)/shard_map/ppermute | solution.py:17
  44.6 5.9 %collective-permute-start.19 = (s16[33,8,128]{2,1,0:T(8,128)(2,1)S(1)}, s16[33,8,128]{2,1,0:T(8,128)(2,1)S(1)}, u32[]{:S(2)}, u32[]{:S(2)}) collective-permute-start(s16[33,8,128]{2,1,0:T(8,128)(2,1)S(1)} %get-tuple-element.52), channel_id=1, source_target_pairs={{0,8},{4,12},{8,0},{12,4},{16,24},{20,28},{24,16},{28,20},{1,9},{5... | collective-permute-start | bytes 202760 | tf_op jit(solution)/shard_map/ppermute | solution.py:17
  46.1 4.5 %collective-permute-start.18 = (s16[33,8,128]{2,1,0:T(8,128)(2,1)S(1)}, s16[33,8,128]{2,1,0:T(8,128)(2,1)S(1)}, u32[]{:S(2)}, u32[]{:S(2)}) collective-permute-start(s16[33,8,128]{2,1,0:T(8,128)(2,1)S(1)} %get-tuple-element.51), channel_id=1, source_target_pairs={{0,8},{4,12},{8,0},{12,4},{16,24},{20,28},{24,16},{28,20},{1,9},{5... | collective-permute-start | bytes 202760 | tf_op jit(solution)/shard_map/ppermute | solution.py:17
  46.7 4.4 %collective-permute-start.17 = (s16[33,8,128]{2,1,0:T(8,128)(2,1)S(1)}, s16[33,8,128]{2,1,0:T(8,128)(2,1)S(1)}, u32[]{:S(2)}, u32[]{:S(2)}) collective-permute-start(s16[33,8,128]{2,1,0:T(8,128)(2,1)S(1)} %get-tuple-element.50), channel_id=1, source_target_pairs={{0,8},{4,12},{8,0},{12,4},{16,24},{20,28},{24,16},{28,20},{1,9},{5... | collective-permute-start | bytes 202760 | tf_op jit(solution)/shard_map/ppermute | solution.py:17
  48.4 4.4 %collective-permute-start.16 = (s16[33,8,128]{2,1,0:T(8,128)(2,1)S(1)}, s16[33,8,128]{2,1,0:T(8,128)(2,1)S(1)}, u32[]{:S(2)}, u32[]{:S(2)}) collective-permute-start(s16[33,8,128]{2,1,0:T(8,128)(2,1)S(1)} %get-tuple-element.49), channel_id=1, source_target_pairs={{0,8},{4,12},{8,0},{12,4},{16,24},{20,28},{24,16},{28,20},{1,9},{5... | collective-permute-start | bytes 202760 | tf_op jit(solution)/shard_map/ppermute | solution.py:17

commit v2 on v0

v2 whole, which is shorter than its diff:
```python
import functools

import jax
import jax.numpy as jnp
from jax import lax
from jax.experimental import pallas as pl
from jax.experimental.pallas import tpu as pltpu
from jax.sharding import PartitionSpec as P

CHUNKS = (8, 8, 8, 8)
DIRECT = (0, 0, 0, 1)
VMEM = pl.BlockSpec(memory_space=pltpu.VMEM)
SMEM = pl.BlockSpec(memory_space=pltpu.SMEM)
ANY = pl.BlockSpec(memory_space=pl.ANY)
PARAMS = pltpu.CompilerParams(vmem_limit_bytes=16 << 20)


def swapped(block, axis, mask):
    return lax.ppermute(block, axis, [(i, i ^ mask) for i in range(lax.axis_size(axis))])


def left_half(shape):
    return lax.broadcasted_iota(jnp.int32, shape, len(shape) - 1) < shape[-1] // 2


def turned(values):
    return pltpu.roll(values, values.shape[-1] // 2, 1)


def halves(values):
    values = values.astype(jnp.float32)
    return jnp.concatenate([values, turned(values)], axis=0)[:, : values.shape[-1] // 2].astype(jnp.bfloat16)


def stacked(own, partner):
    left = left_half(own.shape)
    top = jnp.where(left, own, turned(partner))
    bottom = jnp.where(left, turned(own), partner)
    return jnp.concatenate([top, bottom], axis=0)


def folded(product):
    rows = product.shape[0] // 2
    other = turned(product[rows:])
    return product[:rows] + jnp.where(left_half(other.shape), -other, other)


def dot(a, b):
    return jnp.dot(a, b, preferred_element_type=jnp.float32)


def encode(read, peak, out, first, count, where=slice(None)):
    exponent = jnp.floor(jnp.log2(jnp.maximum(peak, 1e-30))) + 1.0
    scale = jnp.exp2(15.0 - exponent)
    for i in range(count):
        code = jnp.clip(jnp.round(read(i) * scale), -32767.0, 32767.0)
        out[first + i, where] = code.astype(jnp.int32).astype(jnp.int16)
    out[first + count, where] = exponent.astype(jnp.int32).astype(jnp.int16)


def decoder(coded, first, count):
    unit = jnp.exp2(coded[first + count].astype(jnp.float32) - 15.0)
    return lambda i: coded[first + i].astype(jnp.float32) * unit


def call(kernel, name, in_specs, outs, *args, after=(), **more):
    count = len(args)

    def body(*refs):
        kernel(*refs[:count], *refs[count + len(after) :])

    return pl.pallas_call(
        body,
        in_specs=in_specs + [ANY] * len(after),
        out_specs=[VMEM] * len(outs),
        out_shape=[jax.ShapeDtypeStruct(shape, kind) for shape, kind in outs],
        compiler_params=PARAMS,
        name=name,
        **more,
    )(*args, *after)


def rows_kernel(start, values_ref, *outs):
    for out in outs:
        rows = out.shape[1]
        out[...] = values_ref[:, pl.ds(start, rows)]
        start += rows


def rows_of(values, start, counts, after=()):
    blocks, _, width = values.shape
    outs = [((blocks, rows, width), values.dtype) for rows in counts]
    return call(functools.partial(rows_kernel, start), "rows_of", [VMEM], outs, values, after=after)


def own_kernel(chunks, *refs):
    values, factor_ref, outs, partner_factors = refs[:chunks], refs[chunks], refs[chunks + 1 : -1], refs[-1]
    for i in range(factor_ref.shape[0]):
        value = jnp.concatenate([v[i].astype(jnp.float32) for v in values], axis=0)
        result = folded(dot(halves(value), factor_ref[i, 0]))
        start = 0
        for out in outs:
            out[i] = result[start : start + out.shape[1]]
            start += out.shape[1]
        partner_factors[i] = factor_ref[i, 1]


def own_part(values, factors):
    blocks, _, rank, width = factors.shape
    outs = [(v.shape, jnp.float32) for v in values] + [((blocks, rank, width), factors.dtype)]
    *owns, partner_factors = call(
        functools.partial(own_kernel, len(values)), "own_part", [VMEM] * (len(values) + 1), outs, *values, factors
    )
    return owns, partner_factors


def partner_kernel(split, me_ref, pattern_ref, own_ref, partner_ref, factor_ref, kept, *rest):
    *outs, total = rest
    me = me_ref[0]
    share = kept.shape[1]
    rows, width = own_ref.shape[1:]

    def block(b):
        return own_ref[b] + folded(dot(halves(partner_ref[pattern_ref[b]]), factor_ref[b]))

    sent = [turn for turns in split for turn in turns]
    for out, turns in zip(outs, split):
        for place, turn in enumerate(turns):
            peak = jnp.zeros((rows, width), jnp.float32)
            held = total.at[sent.index(turn)]
            for i in range(share):
                result = block((me ^ turn) * share + i)
                held[i] = result
                peak = jnp.maximum(peak, jnp.abs(result))
            encode(lambda i: held[i], peak, out, place * (share + 1), share)
    stay = [turn for turn in range(len(sent) + kept.shape[0]) if turn not in sent]
    for place, turn in enumerate(stay):
        for i in range(share):
            kept[place, i] = block((me ^ turn) * share + i)


def partner_part(split, parts, me, pattern, own, partner, factors, after=()):
    blocks, rows, width = own.shape
    share = blocks // parts
    sent = sum(len(turns) for turns in split)
    outs = [((parts - sent, share, rows, width), jnp.float32)]
    outs += [((len(turns) * (share + 1), rows, width), jnp.int16) for turns in split]
    return call(
        functools.partial(partner_kernel, split),
        "partner_part",
        [SMEM, SMEM, VMEM, VMEM, VMEM],
        outs,
        me,
        pattern,
        own,
        partner,
        factors,
        after=after,
        scratch_shapes=[pltpu.VMEM((sent, share, rows, width), jnp.float32)],
    )


def halve_kernel(chunks, *refs):
    *ins, kept, out, total = refs
    half, share = kept.shape[:2]
    start = 0
    for kept_ref, coded_ref in zip(ins[:chunks], ins[chunks:]):
        rows, width = kept_ref.shape[2:]
        where = pl.ds(start, rows)
        for place in range(2 * half):
            read = decoder(coded_ref, place * (share + 1), share)
            peak = jnp.zeros((rows, width), jnp.float32)
            for i in range(share):
                result = kept_ref[place, i] + read(i)
                if place < half:
                    kept[place, i, where] = result
                else:
                    total[i, where] = result
                    peak = jnp.maximum(peak, jnp.abs(result))
            if place >= half:
                encode(lambda i: total[i, where], peak, out, (place - half) * (share + 1), share, where)
        start += rows


def halve(kept, coded, after=()):
    held, share, _, width = kept[0].shape
    rows = sum(k.shape[2] for k in kept)
    return call(
        functools.partial(halve_kernel, len(kept)),
        "halve",
        [VMEM] * (2 * len(kept)),
        [((held // 2, share, rows, width), jnp.float32), ((held // 2 * (share + 1), rows, width), jnp.int16)],
        *kept,
        *coded,
        after=after,
        scratch_shapes=[pltpu.VMEM((share, rows, width), jnp.float32)],
    )


def sum_kernel(counts, *refs):
    *ins, total, out = refs
    share = total.shape[0]
    start = 0
    for count in counts:
        kept, *coded = ins[: 1 + count]
        ins = ins[1 + count :]
        rows = kept.shape[2]
        reads = [decoder(c, 0, share) for c in coded]
        peak = jnp.zeros(kept.shape[2:], jnp.float32)
        where = pl.ds(start, rows)
        for i in range(share):
            result = kept[0, i]
            for read in reads:
                result = result + read(i)
            total[i, where] = result
            peak = jnp.maximum(peak, jnp.abs(result))
        encode(lambda i: total[i, where], peak, out, 0, share, where)
        start += rows


def quarter_sum(groups, after=()):
    _, share, _, width = groups[0][0].shape
    rows = sum(group[0].shape[2] for group in groups)
    args = [array for group in groups for array in group]
    return call(
        functools.partial(sum_kernel, [len(group) - 1 for group in groups]),
        "quarter_sum",
        [VMEM] * len(args),
        [((share, rows, width), jnp.float32), ((share + 1, rows, width), jnp.int16)],
        *args,
        after=after,
    )


def second_kernel(start, own_ref, coded_ref, factor_ref, *rest):
    out_hbm, out, semaphore = rest[-3:]
    share, rows, width = own_ref.shape
    read = decoder(coded_ref, 0, share)
    for i in range(share):
        values = stacked(own_ref[i], read(i))
        high = values.astype(jnp.bfloat16)
        low = (values - high.astype(jnp.float32)).astype(jnp.bfloat16)
        product = dot(jnp.concatenate([high, low], axis=0), factor_ref[i].reshape(width, width))
        out[i] = folded(product[: 2 * rows] + product[2 * rows :])
    copy = pltpu.make_async_copy(out, out_hbm.at[:, pl.ds(start, rows)], semaphore)
    copy.start()
    copy.wait()


def second_level(own, coded, factors, start, rows_in_all, result=None):
    share, rows, width = own.shape
    args = (own, coded, factors) if result is None else (own, coded, factors, result)
    return pl.pallas_call(
        functools.partial(second_kernel, start),
        in_specs=[VMEM] * 3 + [ANY] * (len(args) - 3),
        out_specs=ANY,
        out_shape=jax.ShapeDtypeStruct((share, rows_in_all, width), jnp.float32),
        scratch_shapes=[pltpu.VMEM((share, rows, width), jnp.float32), pltpu.SemaphoreType.DMA],
        input_output_aliases={} if result is None else {3: 0},
        compiler_params=PARAMS,
        name="second_level",
    )(*args)


def on_device(sources, first_factors, second_factors, pattern):
    half = lax.axis_size("tgt") // 2
    parts = lax.axis_size("src")
    sources, first_factors = sources[0], first_factors[0]
    blocks, rows_in_all, _ = sources.shape
    share = blocks // parts
    me = lax.axis_index("src").astype(jnp.int32)
    starts = [sum(CHUNKS[:c]) for c in range(len(CHUNKS))]
    values = rows_of(sources, 0, CHUNKS)
    partners = [swapped(v, "tgt", half) for v in values]
    owns, factors = own_part(values, first_factors)
    mine = lax.dynamic_slice_in_dim(second_factors, me * share, share, 0)
    waiting, marks = {}, {"mine": mine}
    order = [('first', (0,)), ('halve', (0,)), ('first', (1,), ('first', (0,))), ('halve', (1,)), ('first', (2,), ('first', (1,)), ('halve', (0,))), ('first', (3,), ('first', (2,)), ('halve', (1,))), ('halve', (2,), ('first', (3,)))]
    for step, chunks, *before in order:
        last = [marks[b] for b in before]
        if step == "first":
            (c,) = chunks
            turns = range(1, parts)
            split = [[turn] for turn in turns] if DIRECT[c] else [[turn for turn in turns if turn & 1]]
            kept, *coded = partner_part(split, parts, me.reshape(1), pattern, owns[c], partners[c], factors, last)
            masks = turns if DIRECT[c] else [1]
            arrived = [swapped(s, "src", mask) for s, mask in zip(coded, masks)]
            waiting[chunks] = (kept, *arrived)
        else:
            kept, coded = halve([waiting[(c,)][0] for c in chunks], [waiting[(c,)][1] for c in chunks], last)
            mask = 2
            arrived = swapped(coded, "src", mask)
            while 2 * mask < parts:
                mask *= 2
                kept, coded = halve([kept], [arrived])
                arrived = swapped(coded, "src", mask)
            waiting[chunks] = (kept, arrived)
        marks[step, chunks] = kept
    result, start = None, 0
    for part in [[(0,), (1,), (2,)], [(3,)]]:
        total, coded = quarter_sum([waiting[chunks] for chunks in part], ())
        other = swapped(coded, "tgt", half // 2)
        result = second_level(total, other, mine, start, rows_in_all, result)
        start += total.shape[1]
    return result


def solution(mesh):
    return jax.shard_map(
        on_device,
        mesh=mesh,
        in_specs=(
            P("src", "tgt", None, None),
            P("src", "tgt", None, None, None),
            P("tgt", None, None, None),
            P("tgt"),
        ),
        out_specs=P(("tgt", "src"), None, None),
        check_vma=False,
    )
```

time: 120 us -> 48 us (0.40)
  waiting for transfers between devices: 62.8 us -> 6.56 us
  starting transfers between devices: 4.43 us -> 26.4 us
  local copies, waits for them, and re-layouts: 21.7 us -> 4.76 us
  between operations: 13.5 us -> 0.13 us
  Pallas kernels: 0 us -> 10 us
  matrix products: 8.71 us -> 0 us
  other arithmetic: 8.01 us -> 0 us
    reduce_scatter x1 -> x0, waiting for transfers between devices: 45.5 us -> none  [on_device(): lax.psum_scatter(apply_factor(local_values, local_factors[:, 0], False) +...]
    ppermute x2 -> x15, starting transfers between devices: 4.43 us -> 26.4 us  [swapped(): lax.ppermute(block, axis, [(i, i ^ mask) for i in range(lax.axis_size(axi...]
    ppermute x2 -> x15, waiting for transfers between devices: 17.3 us -> 6.56 us  [swapped(): lax.ppermute(block, axis, [(i, i ^ mask) for i in range(lax.axis_size(axi...]
    pallas_call x0 -> x13, Pallas kernels: none -> 10 us  [the longest x11 7.48 us: call(): pl.pallas_call(body, in_specs=in_specs + [ANY] * len(after), out_specs=[V...]
    dot_general x4 -> x0, matrix products: 8.71 us -> none  [the longest x2 5.34 us: apply_factor(): jnp.einsum('brck,bkj->brcj', split_values, factor, preferred_element_type...]
    unnamed x8 -> x6, local copies, waits for them, and re-layouts: 9.03 us -> 3.43 us
    add x4 -> x0, other arithmetic: 4.45 us -> none  [the longest x1 2.5 us: on_device(): apply_factor(local_values, local_factors[:, 0], False)]
    gather x2 -> x0, local copies, waits for them, and re-layouts: 3.72 us -> none  [on_device(): partner_values = jnp.take(remote_values, pattern, axis=0)]
  transfers between devices with their start and end apart: 3 -> 15, of which waited for: 3 -> 6; matrix products, arithmetic and copies ran while one was open for 14% -> 3% of each run, Pallas kernels for 0% -> 18%
where the time goes in v2:
time: 48 us; the launch traced here: 47.8 us
  starting transfers between devices  26.4 us (55%)
  Pallas kernels  10 us (21%)
  waiting for transfers between devices  6.56 us (14%)
  local copies, waits for them, and re-layouts  4.76 us (10%)
    ppermute x15, starting transfers between devices, swapped(): lax.ppermute(block, axis, [(i, i ^ mask) for i in range(lax.axis_size(axi...  26.4 us
    pallas_call x11, Pallas kernels, call(): pl.pallas_call(body, in_specs=in_specs + [ANY] * len(after), out_specs=[V...  7.48 us
    ppermute x15, waiting for transfers between devices, swapped(): lax.ppermute(block, axis, [(i, i ^ mask) for i in range(lax.axis_size(axi...  6.56 us
    unnamed x6, local copies, waits for them, and re-layouts  3.43 us
    pallas_call x2, Pallas kernels, second_level(): pl.pallas_call(functools.partial(second_kernel, start), in_specs=[VMEM] *...  2.53 us
    dynamic_slice x1, local copies, waits for them, and re-layouts, on_device(): mine = lax.dynamic_slice_in_dim(second_factors, me * share, share, 0)  1.33 us
  transfers between devices with their start and end apart: 15, of which 6 were waited for; matrix products, arithmetic and copies ran while one was open for 3% of the time, Pallas kernels for 18%

profile of v2, /device:TPU:0, one launch (start us, length us, event | category | flops | bytes accessed | tf_op | source)
XLA Modules:
  0.0 47.8 jit_solution(4232182966492626109)
XLA Ops:
  0.0 1.2 %copy-done.1 = bf16[1,128,32,128]{3,2,1,0:T(8,128)(2,1)S(1)} copy-done((bf16[1,128,32,128]{3,2,1,0:T(8,128)(2,1)S(1)}, bf16[1,128,32,128]{3,2,1,0:T(8,128)(2,1)}, u32[]{:S(2)}) %copy-start.1) | copy-done | bytes 1048600
  1.4 3.0 %collective-permute-start.3 = (bf16[128,8,128]{2,1,0:T(8,128)(2,1)S(1)}, bf16[128,8,128]{2,1,0:T(8,128)(2,1)S(1)}, u32[]{:S(2)}, u32[]{:S(2)}) collective-permute-start(bf16[128,8,128]{2,1,0:T(8,128)(2,1)S(1)} %get-tuple-element.34.refs_0_), channel_id=1, source_target_pairs={{0,16},{4,20},{8,24},{12,28},{16,0},{20,4},{24,8},{28,12},{1,17},{... | collective-permute-start | bytes 786440 | tf_op jit(solution)/shard_map/ppermute | solution.py:19
  4.5 1.9 %collective-permute-start.1 = (bf16[128,8,128]{2,1,0:T(8,128)(2,1)S(1)}, bf16[128,8,128]{2,1,0:T(8,128)(2,1)S(1)}, u32[]{:S(2)}, u32[]{:S(2)}) collective-permute-start(bf16[128,8,128]{2,1,0:T(8,128)(2,1)S(1)} %get-tuple-element.36.refs_2_), channel_id=1, source_target_pairs={{0,16},{4,20},{8,24},{12,28},{16,0},{20,4},{24,8},{28,12},{1,17},{... | collective-permute-start | bytes 786440 | tf_op jit(solution)/shard_map/ppermute | solution.py:19
  6.5 2.2 %copy-done = bf16[1,128,2,64,128]{4,3,2,1,0:T(8,128)(2,1)S(1)} copy-done((bf16[1,128,2,64,128]{4,3,2,1,0:T(8,128)(2,1)S(1)}, bf16[1,128,2,64,128]{4,3,2,1,0:T(8,128)(2,1)}, u32[]{:S(2)}) %copy-start) | copy-done | bytes 4194328
  8.7 1.3 %own_part.1 = (f32[128,8,128]{2,1,0:T(8,128)S(1)}, f32[128,8,128]{2,1,0:T(8,128)S(1)}, f32[128,8,128]{2,1,0:T(8,128)S(1)}, f32[128,8,128]{2,1,0:T(8,128)S(1)}, bf16[128,64,128]{2,1,0:T(8,128)(2,1)S(1)}) custom-call(bf16[128,8,128]{2,1,0:T(8,128)(2,1)S(1)} %get-tuple-element.34.refs_0_, bf16[128,8,128]{2,1,0:T(8,128)(2,1)S(1)} %get-tuple-element.35.refs_1_, ...), custom_call_target="tpu_custom_call" | custom-call | tf_op jit(solution)/shard_map/own_part/pallas_call | solution.py:72
  10.0 1.6 %collective-permute-done.3.refs_3_ = bf16[128,8,128]{2,1,0:T(8,128)(2,1)S(1)} collective-permute-done((bf16[128,8,128]{2,1,0:T(8,128)(2,1)S(1)}, bf16[128,8,128]{2,1,0:T(8,128)(2,1)S(1)}, u32[]{:S(2)}, u32[]{:S(2)}) %collective-permute-start.3) | collective-permute-done | bytes 262176 | tf_op jit(solution)/shard_map/ppermute | solution.py:19
  11.6 1.4 %partner_part.4 = (f32[2,32,8,128]{3,2,1,0:T(8,128)S(1)}, s16[66,8,128]{2,1,0:T(8,128)(2,1)S(1)}) custom-call(s32[1]{0:T(128)} %bitcast.refs_0_, s32[128]{0:T(128)S(1)} %copy-done.2, f32[128,8,128]{2,1,0:T(8,128)S(1)} %get-tuple-element.42.refs_2_, bf16[128,8,128]{2,1,0:T(8,128)(2,1)S(1)} %collective-permute-done.3.refs_3_, ...), custom_call_target="tpu_custom_call" | custom-call | tf_op jit(solution)/shard_map/partner_part/pallas_call | solution.py:72
  13.0 2.2 %collective-permute-start.4 = (s16[66,8,128]{2,1,0:T(8,128)(2,1)S(1)}, s16[66,8,128]{2,1,0:T(8,128)(2,1)S(1)}, u32[]{:S(2)}, u32[]{:S(2)}) collective-permute-start(s16[66,8,128]{2,1,0:T(8,128)(2,1)S(1)} %get-tuple-element.45), channel_id=1, source_target_pairs={{0,1},{1,0},{2,3},{3,2},{4,5},{5,4},{6,7},{7,6},{8,9},{9,8},{10,11... | collective-permute-start | bytes 405512 | tf_op jit(solution)/shard_map/ppermute | solution.py:19
  15.1 1.5 %collective-permute-start = (bf16[128,8,128]{2,1,0:T(8,128)(2,1)S(1)}, bf16[128,8,128]{2,1,0:T(8,128)(2,1)S(1)}, u32[]{:S(2)}, u32[]{:S(2)}) collective-permute-start(bf16[128,8,128]{2,1,0:T(8,128)(2,1)S(1)} %get-tuple-element.37.refs_3_), channel_id=1, source_target_pairs={{0,16},{4,20},{8,24},{12,28},{16,0},{20,4},{24,8},{28,12},{1,17},{... | collective-permute-start | bytes 786440 | tf_op jit(solution)/shard_map/ppermute | solution.py:19
  17.2 1.4 %partner_part.5 = (f32[2,32,8,128]{3,2,1,0:T(8,128)S(1)}, s16[66,8,128]{2,1,0:T(8,128)(2,1)S(1)}) custom-call(s32[1]{0:T(128)} %bitcast.refs_0_, s32[128]{0:T(128)S(1)} %copy-done.2, f32[128,8,128]{2,1,0:T(8,128)S(1)} %get-tuple-element.41.refs_2_, bf16[128,8,128]{2,1,0:T(8,128)(2,1)S(1)} %collective-permute-done.2.refs_3_, ...), custom_call_target="tpu_custom_call" | custom-call | tf_op jit(solution)/shard_map/partner_part/pallas_call | solution.py:72
  18.6 2.2 %collective-permute-start.5 = (s16[66,8,128]{2,1,0:T(8,128)(2,1)S(1)}, s16[66,8,128]{2,1,0:T(8,128)(2,1)S(1)}, u32[]{:S(2)}, u32[]{:S(2)}) collective-permute-start(s16[66,8,128]{2,1,0:T(8,128)(2,1)S(1)} %get-tuple-element.48), channel_id=1, source_target_pairs={{0,1},{1,0},{2,3},{3,2},{4,5},{5,4},{6,7},{7,6},{8,9},{9,8},{10,11... | collective-permute-start | bytes 405512 | tf_op jit(solution)/shard_map/ppermute | solution.py:19
  20.9 2.0 %collective-permute-done.1.refs_3_ = bf16[128,8,128]{2,1,0:T(8,128)(2,1)S(1)} collective-permute-done((bf16[128,8,128]{2,1,0:T(8,128)(2,1)S(1)}, bf16[128,8,128]{2,1,0:T(8,128)(2,1)S(1)}, u32[]{:S(2)}, u32[]{:S(2)}) %collective-permute-start.1) | collective-permute-done | bytes 262176 | tf_op jit(solution)/shard_map/ppermute | solution.py:19
  22.8 1.4 %partner_part.6 = (f32[2,32,8,128]{3,2,1,0:T(8,128)S(1)}, s16[66,8,128]{2,1,0:T(8,128)(2,1)S(1)}) custom-call(s32[1]{0:T(128)} %bitcast.refs_0_, s32[128]{0:T(128)S(1)} %copy-done.2, f32[128,8,128]{2,1,0:T(8,128)S(1)} %get-tuple-element.40.refs_2_, bf16[128,8,128]{2,1,0:T(8,128)(2,1)S(1)} %collective-permute-done.1.refs_3_, ...), custom_call_target="tpu_custom_call" | custom-call | tf_op jit(solution)/shard_map/partner_part/pallas_call | solution.py:72
  24.2 2.2 %collective-permute-start.12 = (s16[66,8,128]{2,1,0:T(8,128)(2,1)S(1)}, s16[66,8,128]{2,1,0:T(8,128)(2,1)S(1)}, u32[]{:S(2)}, u32[]{:S(2)}) collective-permute-start(s16[66,8,128]{2,1,0:T(8,128)(2,1)S(1)} %get-tuple-element.58), channel_id=1, source_target_pairs={{0,1},{1,0},{2,3},{3,2},{4,5},{5,4},{6,7},{7,6},{8,9},{9,8},{10,11... | collective-permute-start | bytes 405512 | tf_op jit(solution)/shard_map/ppermute | solution.py:19
  26.4 2.6 %collective-permute-start.10 = (s16[33,8,128]{2,1,0:T(8,128)(2,1)S(1)}, s16[33,8,128]{2,1,0:T(8,128)(2,1)S(1)}, u32[]{:S(2)}, u32[]{:S(2)}) collective-permute-start(s16[33,8,128]{2,1,0:T(8,128)(2,1)S(1)} %get-tuple-element.56), channel_id=1, source_target_pairs={{0,2},{1,3},{2,0},{3,1},{4,6},{5,7},{6,4},{7,5},{8,10},{9,11},{10,... | collective-permute-start | bytes 202760 | tf_op jit(solution)/shard_map/ppermute | solution.py:19
  29.5 1.3 %partner_part.7 = (f32[1,32,8,128]{3,2,1,0:T(8,128)S(1)}, s16[33,8,128]{2,1,0:T(8,128)(2,1)S(1)}, s16[33,8,128]{2,1,0:T(8,128)(2,1)S(1)}, s16[33,8,128]{2,1,0:T(8,128)(2,1)S(1)}) custom-call(s32[1]{0:T(128)} %bitcast.refs_0_, s32[128]{0:T(128)S(1)} %copy-done.2, f32[128,8,128]{2,1,0:T(8,128)S(1)} %get-tuple-element.38.refs_2_, ...), custom_call_target="tpu_custom_call" | custom-call | tf_op jit(solution)/shard_map/partner_part/pallas_call | solution.py:72
  30.9 2.7 %collective-permute-start.13 = (s16[33,8,128]{2,1,0:T(8,128)(2,1)S(1)}, s16[33,8,128]{2,1,0:T(8,128)(2,1)S(1)}, u32[]{:S(2)}, u32[]{:S(2)}) collective-permute-start(s16[33,8,128]{2,1,0:T(8,128)(2,1)S(1)} %get-tuple-element.60), channel_id=1, source_target_pairs={{0,2},{1,3},{2,0},{3,1},{4,6},{5,7},{6,4},{7,5},{8,10},{9,11},{10,... | collective-permute-start | bytes 202760 | tf_op jit(solution)/shard_map/ppermute | solution.py:19
  33.6 2.1 %collective-permute-start.6 = (s16[33,8,128]{2,1,0:T(8,128)(2,1)S(1)}, s16[33,8,128]{2,1,0:T(8,128)(2,1)S(1)}, u32[]{:S(2)}, u32[]{:S(2)}) collective-permute-start(s16[33,8,128]{2,1,0:T(8,128)(2,1)S(1)} %get-tuple-element.51), channel_id=1, source_target_pairs={{0,1},{1,0},{2,3},{3,2},{4,5},{5,4},{6,7},{7,6},{8,9},{9,8},{10,11... | collective-permute-start | bytes 202760 | tf_op jit(solution)/shard_map/ppermute | solution.py:19
  35.8 2.3 %collective-permute-start.8 = (s16[33,8,128]{2,1,0:T(8,128)(2,1)S(1)}, s16[33,8,128]{2,1,0:T(8,128)(2,1)S(1)}, u32[]{:S(2)}, u32[]{:S(2)}) collective-permute-start(s16[33,8,128]{2,1,0:T(8,128)(2,1)S(1)} %get-tuple-element.53), channel_id=1, source_target_pairs={{0,3},{1,2},{2,1},{3,0},{4,7},{5,6},{6,5},{7,4},{8,11},{9,10},{10,... | collective-permute-start | bytes 202760 | tf_op jit(solution)/shard_map/ppermute | solution.py:19
  38.1 1.2 %collective-permute-done.13.refs_5_ = s16[33,8,128]{2,1,0:T(8,128)(2,1)S(1)} collective-permute-done((s16[33,8,128]{2,1,0:T(8,128)(2,1)S(1)}, s16[33,8,128]{2,1,0:T(8,128)(2,1)S(1)}, u32[]{:S(2)}, u32[]{:S(2)}) %collective-permute-start.13) | collective-permute-done | bytes 67616 | tf_op jit(solution)/shard_map/ppermute | solution.py:19
  39.5 1.6 %collective-permute-start.14 = (s16[33,24,128]{2,1,0:T(8,128)(2,1)S(1)}, s16[33,24,128]{2,1,0:T(8,128)(2,1)S(1)}, u32[]{:S(2)}, u32[]{:S(2)}) collective-permute-start(s16[33,24,128]{2,1,0:T(8,128)(2,1)S(1)} %get-tuple-element.62), channel_id=1, source_target_pairs={{0,8},{4,12},{8,0},{12,4},{16,24},{20,28},{24,16},{28,20},{1,9},{5... | collective-permute-start | bytes 608264 | tf_op jit(solution)/shard_map/ppermute | solution.py:19
  42.2 1.6 %collective-permute-start.9 = (s16[33,8,128]{2,1,0:T(8,128)(2,1)S(1)}, s16[33,8,128]{2,1,0:T(8,128)(2,1)S(1)}, u32[]{:S(2)}, u32[]{:S(2)}) collective-permute-start(s16[33,8,128]{2,1,0:T(8,128)(2,1)S(1)} %get-tuple-element.55), channel_id=1, source_target_pairs={{0,8},{4,12},{8,0},{12,4},{16,24},{20,28},{24,16},{28,20},{1,9},{5... | collective-permute-start | bytes 202760 | tf_op jit(solution)/shard_map/ppermute | solution.py:19
  43.8 1.3 %constant_dynamic-slice_fusion.factor_ref = bf16[32,2,64,128]{3,2,1,0:T(8,128)(2,1)S(1)} fusion(bf16[128,2,64,128]{3,2,1,0:T(8,128)(2,1)} %param.6, s32[]{:T(128)S(6)} %select_n.3), kind=kLoop, calls=%fused_computation | loop fusion | bytes 2097156 | tf_op jit(solution)/shard_map/dynamic_slice | solution.py:276
  45.3 1.3 %second_level.2.rest_0_ = f32[32,32,128]{2,1,0:T(8,128)} custom-call(f32[32,24,128]{2,1,0:T(8,128)S(1)} %get-tuple-element.61.own_ref, s16[33,24,128]{2,1,0:T(8,128)(2,1)S(1)} %collective-permute-done.14.coded_ref, bf16[32,2,64,128]{3,2,1,0:T(8,128)(2,1)S(1)} %constant_dynamic-slice_fusion.factor_ref), custom_call_target="tpu_custom_call" | custom-call | tf_op jit(solution)/shard_map/second_level/pallas_call | solution.py:253
  (26 shorter events, 4.3 us)
Async XLA Ops:
  0.0 11.6 %copy-start.2 = (s32[128]{0:T(128)S(1)}, s32[128]{0:T(128)}, u32[]{:S(2)}) copy-start(s32[128]{0:T(128)} %refs_1_.7) | copy-start | bytes 1540
  0.0 1.2 %copy-start.1 = (bf16[1,128,32,128]{3,2,1,0:T(8,128)(2,1)S(1)}, bf16[1,128,32,128]{3,2,1,0:T(8,128)(2,1)}, u32[]{:S(2)}) copy-start(bf16[1,128,32,128]{3,2,1,0:T(8,128)(2,1)} %param.4) | copy-start | bytes 3145732
  1.4 10.2 %collective-permute-start.3 = (bf16[128,8,128]{2,1,0:T(8,128)(2,1)S(1)}, bf16[128,8,128]{2,1,0:T(8,128)(2,1)S(1)}, u32[]{:S(2)}, u32[]{:S(2)}) collective-permute-start(bf16[128,8,128]{2,1,0:T(8,128)(2,1)S(1)} %get-tuple-element.34.refs_0_), channel_id=1, source_target_pairs={{0,16},{4,20},{8,24},{12,28},{16,0},{20,4},{24,8},{28,12},{1,17},{... | collective-permute-start | bytes 786440 | tf_op jit(solution)/shard_map/ppermute | solution.py:19
  4.5 12.8 %collective-permute-start.2 = (bf16[128,8,128]{2,1,0:T(8,128)(2,1)S(1)}, bf16[128,8,128]{2,1,0:T(8,128)(2,1)S(1)}, u32[]{:S(2)}, u32[]{:S(2)}) collective-permute-start(bf16[128,8,128]{2,1,0:T(8,128)(2,1)S(1)} %get-tuple-element.35.refs_1_), channel_id=1, source_target_pairs={{0,16},{4,20},{8,24},{12,28},{16,0},{20,4},{24,8},{28,12},{1,17},{... | collective-permute-start | bytes 786440 | tf_op jit(solution)/shard_map/ppermute | solution.py:19
  4.5 18.3 %collective-permute-start.1 = (bf16[128,8,128]{2,1,0:T(8,128)(2,1)S(1)}, bf16[128,8,128]{2,1,0:T(8,128)(2,1)S(1)}, u32[]{:S(2)}, u32[]{:S(2)}) collective-permute-start(bf16[128,8,128]{2,1,0:T(8,128)(2,1)S(1)} %get-tuple-element.36.refs_2_), channel_id=1, source_target_pairs={{0,16},{4,20},{8,24},{12,28},{16,0},{20,4},{24,8},{28,12},{1,17},{... | collective-permute-start | bytes 786440 | tf_op jit(solution)/shard_map/ppermute | solution.py:19
  6.5 2.2 %copy-start = (bf16[1,128,2,64,128]{4,3,2,1,0:T(8,128)(2,1)S(1)}, bf16[1,128,2,64,128]{4,3,2,1,0:T(8,128)(2,1)}, u32[]{:S(2)}) copy-start(bf16[1,128,2,64,128]{4,3,2,1,0:T(8,128)(2,1)} %param.5) | copy-start | bytes 12582916
  13.0 7.8 %collective-permute-start.4 = (s16[66,8,128]{2,1,0:T(8,128)(2,1)S(1)}, s16[66,8,128]{2,1,0:T(8,128)(2,1)S(1)}, u32[]{:S(2)}, u32[]{:S(2)}) collective-permute-start(s16[66,8,128]{2,1,0:T(8,128)(2,1)S(1)} %get-tuple-element.45), channel_id=1, source_target_pairs={{0,1},{1,0},{2,3},{3,2},{4,5},{5,4},{6,7},{7,6},{8,9},{9,8},{10,11... | collective-permute-start | bytes 405512 | tf_op jit(solution)/shard_map/ppermute | solution.py:19
  15.1 14.3 %collective-permute-start = (bf16[128,8,128]{2,1,0:T(8,128)(2,1)S(1)}, bf16[128,8,128]{2,1,0:T(8,128)(2,1)S(1)}, u32[]{:S(2)}, u32[]{:S(2)}) collective-permute-start(bf16[128,8,128]{2,1,0:T(8,128)(2,1)S(1)} %get-tuple-element.37.refs_3_), channel_id=1, source_target_pairs={{0,16},{4,20},{8,24},{12,28},{16,0},{20,4},{24,8},{28,12},{1,17},{... | collective-permute-start | bytes 786440 | tf_op jit(solution)/shard_map/ppermute | solution.py:19
  18.6 10.4 %collective-permute-start.5 = (s16[66,8,128]{2,1,0:T(8,128)(2,1)S(1)}, s16[66,8,128]{2,1,0:T(8,128)(2,1)S(1)}, u32[]{:S(2)}, u32[]{:S(2)}) collective-permute-start(s16[66,8,128]{2,1,0:T(8,128)(2,1)S(1)} %get-tuple-element.48), channel_id=1, source_target_pairs={{0,1},{1,0},{2,3},{3,2},{4,5},{5,4},{6,7},{7,6},{8,9},{9,8},{10,11... | collective-permute-start | bytes 405512 | tf_op jit(solution)/shard_map/ppermute | solution.py:19
  24.2 6.6 %collective-permute-start.12 = (s16[66,8,128]{2,1,0:T(8,128)(2,1)S(1)}, s16[66,8,128]{2,1,0:T(8,128)(2,1)S(1)}, u32[]{:S(2)}, u32[]{:S(2)}) collective-permute-start(s16[66,8,128]{2,1,0:T(8,128)(2,1)S(1)} %get-tuple-element.58), channel_id=1, source_target_pairs={{0,1},{1,0},{2,3},{3,2},{4,5},{5,4},{6,7},{7,6},{8,9},{9,8},{10,11... | collective-permute-start | bytes 405512 | tf_op jit(solution)/shard_map/ppermute | solution.py:19
  26.4 9.4 %collective-permute-start.10 = (s16[33,8,128]{2,1,0:T(8,128)(2,1)S(1)}, s16[33,8,128]{2,1,0:T(8,128)(2,1)S(1)}, u32[]{:S(2)}, u32[]{:S(2)}) collective-permute-start(s16[33,8,128]{2,1,0:T(8,128)(2,1)S(1)} %get-tuple-element.56), channel_id=1, source_target_pairs={{0,2},{1,3},{2,0},{3,1},{4,6},{5,7},{6,4},{7,5},{8,10},{9,11},{10,... | collective-permute-start | bytes 202760 | tf_op jit(solution)/shard_map/ppermute | solution.py:19
  29.1 9.0 %collective-permute-start.11 = (s16[33,8,128]{2,1,0:T(8,128)(2,1)S(1)}, s16[33,8,128]{2,1,0:T(8,128)(2,1)S(1)}, u32[]{:S(2)}, u32[]{:S(2)}) collective-permute-start(s16[33,8,128]{2,1,0:T(8,128)(2,1)S(1)} %get-tuple-element.57), channel_id=1, source_target_pairs={{0,2},{1,3},{2,0},{3,1},{4,6},{5,7},{6,4},{7,5},{8,10},{9,11},{10,... | collective-permute-start | bytes 202760 | tf_op jit(solution)/shard_map/ppermute | solution.py:19
  30.9 8.3 %collective-permute-start.13 = (s16[33,8,128]{2,1,0:T(8,128)(2,1)S(1)}, s16[33,8,128]{2,1,0:T(8,128)(2,1)S(1)}, u32[]{:S(2)}, u32[]{:S(2)}) collective-permute-start(s16[33,8,128]{2,1,0:T(8,128)(2,1)S(1)} %get-tuple-element.60), channel_id=1, source_target_pairs={{0,2},{1,3},{2,0},{3,1},{4,6},{5,7},{6,4},{7,5},{8,10},{9,11},{10,... | collective-permute-start | bytes 202760 | tf_op jit(solution)/shard_map/ppermute | solution.py:19
  33.6 7.4 %collective-permute-start.6 = (s16[33,8,128]{2,1,0:T(8,128)(2,1)S(1)}, s16[33,8,128]{2,1,0:T(8,128)(2,1)S(1)}, u32[]{:S(2)}, u32[]{:S(2)}) collective-permute-start(s16[33,8,128]{2,1,0:T(8,128)(2,1)S(1)} %get-tuple-element.51), channel_id=1, source_target_pairs={{0,1},{1,0},{2,3},{3,2},{4,5},{5,4},{6,7},{7,6},{8,9},{9,8},{10,11... | collective-permute-start | bytes 202760 | tf_op jit(solution)/shard_map/ppermute | solution.py:19
  35.7 6.4 %collective-permute-start.7 = (s16[33,8,128]{2,1,0:T(8,128)(2,1)S(1)}, s16[33,8,128]{2,1,0:T(8,128)(2,1)S(1)}, u32[]{:S(2)}, u32[]{:S(2)}) collective-permute-start(s16[33,8,128]{2,1,0:T(8,128)(2,1)S(1)} %get-tuple-element.52), channel_id=1, source_target_pairs={{0,2},{1,3},{2,0},{3,1},{4,6},{5,7},{6,4},{7,5},{8,10},{9,11},{10,... | collective-permute-start | bytes 202760 | tf_op jit(solution)/shard_map/ppermute | solution.py:19
  35.8 6.3 %collective-permute-start.8 = (s16[33,8,128]{2,1,0:T(8,128)(2,1)S(1)}, s16[33,8,128]{2,1,0:T(8,128)(2,1)S(1)}, u32[]{:S(2)}, u32[]{:S(2)}) collective-permute-start(s16[33,8,128]{2,1,0:T(8,128)(2,1)S(1)} %get-tuple-element.53), channel_id=1, source_target_pairs={{0,3},{1,2},{2,1},{3,0},{4,7},{5,6},{6,5},{7,4},{8,11},{9,10},{10,... | collective-permute-start | bytes 202760 | tf_op jit(solution)/shard_map/ppermute | solution.py:19
  39.5 5.8 %collective-permute-start.14 = (s16[33,24,128]{2,1,0:T(8,128)(2,1)S(1)}, s16[33,24,128]{2,1,0:T(8,128)(2,1)S(1)}, u32[]{:S(2)}, u32[]{:S(2)}) collective-permute-start(s16[33,24,128]{2,1,0:T(8,128)(2,1)S(1)} %get-tuple-element.62), channel_id=1, source_target_pairs={{0,8},{4,12},{8,0},{12,4},{16,24},{20,28},{24,16},{28,20},{1,9},{5... | collective-permute-start | bytes 608264 | tf_op jit(solution)/shard_map/ppermute | solution.py:19
  42.2 4.4 %collective-permute-start.9 = (s16[33,8,128]{2,1,0:T(8,128)(2,1)S(1)}, s16[33,8,128]{2,1,0:T(8,128)(2,1)S(1)}, u32[]{:S(2)}, u32[]{:S(2)}) collective-permute-start(s16[33,8,128]{2,1,0:T(8,128)(2,1)S(1)} %get-tuple-element.55), channel_id=1, source_target_pairs={{0,8},{4,12},{8,0},{12,4},{16,24},{20,28},{24,16},{28,20},{1,9},{5... | collective-permute-start | bytes 202760 | tf_op jit(solution)/shard_map/ppermute | solution.py:19

commit v3 on v2

--- a/solution.py
+++ b/solution.py
@@ -9,6 +9,8 @@
 
 CHUNKS = (8, 8, 8, 8)
 DIRECT = (0, 0, 0, 1)
+GROUP = 8
+PACK = 4
 VMEM = pl.BlockSpec(memory_space=pltpu.VMEM)
 SMEM = pl.BlockSpec(memory_space=pltpu.SMEM)
 ANY = pl.BlockSpec(memory_space=pl.ANY)
@@ -114,32 +116,44 @@
     return owns, partner_factors
 
 
-def partner_kernel(split, me_ref, pattern_ref, own_ref, partner_ref, factor_ref, kept, *rest):
+def partner_kernel(split, pattern_ref, own_ref, partner_ref, factor_ref, kept, *rest):
     *outs, total = rest
-    me = me_ref[0]
+    me = lax.axis_index("src")
     share = kept.shape[1]
     rows, width = own_ref.shape[1:]
 
-    def block(b):
-        return own_ref[b] + folded(dot(halves(partner_ref[pattern_ref[b]]), factor_ref[b]))
+    left = left_half((rows, width))
+    zero = jnp.zeros((2 * rows, width), jnp.bfloat16)
+
+    def blocks(base):
+        values = []
+        for j in range(PACK):
+            value = partner_ref[pattern_ref[base + j]].astype(jnp.float32)
+            pair, side = ((value, turned(value)), left) if j % 2 == 0 else ((turned(value), value), ~left)
+            column = jnp.concatenate([jnp.where(side, v, 0.0) for v in pair], axis=0).astype(jnp.bfloat16)
+            values.append(jnp.concatenate([column if k == j // 2 else zero for k in range(PACK // 2)], axis=1))
+        factor = factor_ref[pl.ds(base, PACK)].reshape(PACK * (width // 2), width)
+        product = dot(jnp.concatenate(values, axis=0), factor)
+        return [own_ref[base + j] + folded(product[2 * rows * j : 2 * rows * (j + 1)]) for j in range(PACK)]
 
     sent = [turn for turns in split for turn in turns]
     for out, turns in zip(outs, split):
         for place, turn in enumerate(turns):
             peak = jnp.zeros((rows, width), jnp.float32)
             held = total.at[sent.index(turn)]
-            for i in range(share):
-                result = block((me ^ turn) * share + i)
-                held[i] = result
-                peak = jnp.maximum(peak, jnp.abs(result))
+            for i in range(0, share, PACK):
+                for j, result in enumerate(blocks((me ^ turn) * share + i)):
+                    held[i + j] = result
+                    peak = jnp.maximum(peak, jnp.abs(result))
             encode(lambda i: held[i], peak, out, place * (share + 1), share)
     stay = [turn for turn in range(len(sent) + kept.shape[0]) if turn not in sent]
     for place, turn in enumerate(stay):
-        for i in range(share):
-            kept[place, i] = block((me ^ turn) * share + i)
-
-
-def partner_part(split, parts, me, pattern, own, partner, factors, after=()):
+        for i in range(0, share, PACK):
+            for j, result in enumerate(blocks((me ^ turn) * share + i)):
+                kept[place, i + j] = result
+
+
+def partner_part(split, parts, pattern, own, partner, factors, after=()):
     blocks, rows, width = own.shape
     share = blocks // parts
     sent = sum(len(turns) for turns in split)
@@ -148,9 +162,8 @@
     return call(
         functools.partial(partner_kernel, split),
         "partner_part",
-        [SMEM, SMEM, VMEM, VMEM, VMEM],
+        [SMEM, VMEM, VMEM, VMEM],
         outs,
-        me,
         pattern,
         own,
         partner,
@@ -236,15 +249,22 @@
     out_hbm, out, semaphore = rest[-3:]
     share, rows, width = own_ref.shape
     read = decoder(coded_ref, 0, share)
+    copies = []
     for i in range(share):
         values = stacked(own_ref[i], read(i))
         high = values.astype(jnp.bfloat16)
         low = (values - high.astype(jnp.float32)).astype(jnp.bfloat16)
         product = dot(jnp.concatenate([high, low], axis=0), factor_ref[i].reshape(width, width))
         out[i] = folded(product[: 2 * rows] + product[2 * rows :])
-    copy = pltpu.make_async_copy(out, out_hbm.at[:, pl.ds(start, rows)], semaphore)
-    copy.start()
-    copy.wait()
+        if (i + 1) % GROUP == 0:
+            some = pl.ds(i + 1 - GROUP, GROUP)
+            copy = pltpu.make_async_copy(
+                out.at[some], out_hbm.at[some, pl.ds(start, rows)], semaphore.at[i // GROUP]
+            )
+            copy.start()
+            copies.append(copy)
+    for copy in copies:
+        copy.wait()
 
 
 def second_level(own, coded, factors, start, rows_in_all, result=None):
@@ -255,7 +275,7 @@
         in_specs=[VMEM] * 3 + [ANY] * (len(args) - 3),
         out_specs=ANY,
         out_shape=jax.ShapeDtypeStruct((share, rows_in_all, width), jnp.float32),
-        scratch_shapes=[pltpu.VMEM((share, rows, width), jnp.float32), pltpu.SemaphoreType.DMA],
+        scratch_shapes=[pltpu.VMEM((share, rows, width), jnp.float32), pltpu.SemaphoreType.DMA((share // GROUP,))],
         input_output_aliases={} if result is None else {3: 0},
         compiler_params=PARAMS,
         name="second_level",
@@ -270,19 +290,20 @@
     share = blocks // parts
     me = lax.axis_index("src").astype(jnp.int32)
     starts = [sum(CHUNKS[:c]) for c in range(len(CHUNKS))]
-    values = rows_of(sources, 0, CHUNKS)
+    values = [sources[:, : CHUNKS[0]]]
+    values += rows_of(sources, CHUNKS[0], CHUNKS[1:], values)
     partners = [swapped(v, "tgt", half) for v in values]
     owns, factors = own_part(values, first_factors)
     mine = lax.dynamic_slice_in_dim(second_factors, me * share, share, 0)
     waiting, marks = {}, {"mine": mine}
-    order = [('first', (0,)), ('halve', (0,)), ('first', (1,), ('first', (0,))), ('halve', (1,)), ('first', (2,), ('first', (1,)), ('halve', (0,))), ('first', (3,), ('first', (2,)), ('halve', (1,))), ('halve', (2,), ('first', (3,)))]
+    order = [('first', (0,)), ('first', (1,), ('first', (0,))), ('first', (2,), ('first', (1,))), ('halve', (0, 1), ('first', (2,))), ('first', (3,), ('first', (2,)), ('halve', (0, 1))), ('halve', (2,), ('first', (3,)))]
     for step, chunks, *before in order:
         last = [marks[b] for b in before]
         if step == "first":
             (c,) = chunks
             turns = range(1, parts)
             split = [[turn] for turn in turns] if DIRECT[c] else [[turn for turn in turns if turn & 1]]
-            kept, *coded = partner_part(split, parts, me.reshape(1), pattern, owns[c], partners[c], factors, last)
+            kept, *coded = partner_part(split, parts, pattern, owns[c], partners[c], factors, last)
             masks = turns if DIRECT[c] else [1]
             arrived = [swapped(s, "src", mask) for s, mask in zip(coded, masks)]
             waiting[chunks] = (kept, *arrived)
@@ -296,8 +317,9 @@
                 arrived = swapped(coded, "src", mask)
             waiting[chunks] = (kept, arrived)
         marks[step, chunks] = kept
+        marks["arrived", chunks] = waiting[chunks][1]
     result, start = None, 0
-    for part in [[(0,), (1,), (2,)], [(3,)]]:
+    for part in [[(0, 1), (2,)], [(3,)]]:
         total, coded = quarter_sum([waiting[chunks] for chunks in part], ())
         other = swapped(coded, "tgt", half // 2)
         result = second_level(total, other, mine, start, rows_in_all, result)

time: 48 us -> 47.2 us (0.983)
  starting transfers between devices: 26.4 us -> 25.1 us
  Pallas kernels: 10 us -> 8.97 us
  local copies, waits for them, and re-layouts: 4.76 us -> 5.69 us
  waiting for transfers between devices: 6.56 us -> 7.11 us
    ppermute x15 -> x14, starting transfers between devices: 26.4 us -> 25.1 us  [swapped(): lax.ppermute(block, axis, [(i, i ^ mask) for i in range(lax.axis_size(axi...]
    slice x0 -> x1, local copies, waits for them, and re-layouts: none -> 0.98 us  [on_device(): values = [sources[:, :CHUNKS[0]]]]
    pallas_call x11 -> x10, Pallas kernels: 7.48 us -> 6.55 us  [call(): pl.pallas_call(body, in_specs=in_specs + [ANY] * len(after), out_specs=[V...]
    ppermute x15 -> x14, waiting for transfers between devices: 6.56 us -> 7.11 us  [swapped(): lax.ppermute(block, axis, [(i, i ^ mask) for i in range(lax.axis_size(axi...]
  transfers between devices with their start and end apart: 15 -> 14, of which waited for: 6 -> 6; matrix products, arithmetic and copies ran while one was open for 3% -> 3% of each run, Pallas kernels for 18% -> 17%
where the time goes in v3:
time: 47.2 us; the launch traced here: 46.9 us
  starting transfers between devices  25.1 us (53%)
  Pallas kernels  8.97 us (19%)
  waiting for transfers between devices  7.11 us (15%)
  local copies, waits for them, and re-layouts  5.69 us (12%)
    ppermute x14, starting transfers between devices, swapped(): lax.ppermute(block, axis, [(i, i ^ mask) for i in range(lax.axis_size(axi...  25.1 us
    ppermute x14, waiting for transfers between devices, swapped(): lax.ppermute(block, axis, [(i, i ^ mask) for i in range(lax.axis_size(axi...  7.11 us
    pallas_call x10, Pallas kernels, call(): pl.pallas_call(body, in_specs=in_specs + [ANY] * len(after), out_specs=[V...  6.55 us
    unnamed x6, local copies, waits for them, and re-layouts  3.42 us
    pallas_call x2, Pallas kernels, second_level(): pl.pallas_call(functools.partial(second_kernel, start), in_specs=[VMEM] *...  2.42 us
    dynamic_slice x1, local copies, waits for them, and re-layouts, on_device(): mine = lax.dynamic_slice_in_dim(second_factors, me * share, share, 0)  1.3 us
    slice x1, local copies, waits for them, and re-layouts, on_device(): values = [sources[:, :CHUNKS[0]]]  0.98 us
  transfers between devices with their start and end apart: 14, of which 6 were waited for; matrix products, arithmetic and copies ran while one was open for 3% of the time, Pallas kernels for 17%

profile of v3, /device:TPU:0, one launch (start us, length us, event | category | flops | bytes accessed | tf_op | source)
XLA Modules:
  0.0 46.9 jit_solution(10907642591617639070)
XLA Ops:
  1.0 3.0 %collective-permute-start.3 = (bf16[128,8,128]{2,1,0:T(8,128)(2,1)S(1)}, bf16[128,8,128]{2,1,0:T(8,128)(2,1)S(1)}, u32[]{:S(2)}, u32[]{:S(2)}) collective-permute-start(bf16[128,8,128]{2,1,0:T(8,128)(2,1)S(1)} %slice.4.refs_1_.refs_0_), channel_id=1, source_target_pairs={{0,16},{4,20},{8,24},{12,28},{16,0},{20,4},{24,8},{28,12},{1,17},{... | collective-permute-start | bytes 786440 | tf_op jit(solution)/shard_map/ppermute | solution.py:21
  4.0 1.2 %copy-done.1 = bf16[1,128,32,128]{3,2,1,0:T(8,128)(2,1)S(1)} copy-done((bf16[1,128,32,128]{3,2,1,0:T(8,128)(2,1)S(1)}, bf16[1,128,32,128]{3,2,1,0:T(8,128)(2,1)}, u32[]{:S(2)}) %copy-start.1) | copy-done | bytes 1048600
  5.5 2.0 %collective-permute-start.1 = (bf16[128,8,128]{2,1,0:T(8,128)(2,1)S(1)}, bf16[128,8,128]{2,1,0:T(8,128)(2,1)S(1)}, u32[]{:S(2)}, u32[]{:S(2)}) collective-permute-start(bf16[128,8,128]{2,1,0:T(8,128)(2,1)S(1)} %get-tuple-element.32.refs_2_), channel_id=1, source_target_pairs={{0,16},{4,20},{8,24},{12,28},{16,0},{20,4},{24,8},{28,12},{1,17},{... | collective-permute-start | bytes 786440 | tf_op jit(solution)/shard_map/ppermute | solution.py:21
  7.6 2.2 %copy-done = bf16[1,128,2,64,128]{4,3,2,1,0:T(8,128)(2,1)S(1)} copy-done((bf16[1,128,2,64,128]{4,3,2,1,0:T(8,128)(2,1)S(1)}, bf16[1,128,2,64,128]{4,3,2,1,0:T(8,128)(2,1)}, u32[]{:S(2)}) %copy-start) | copy-done | bytes 4194328
  9.7 1.3 %own_part.1 = (f32[128,8,128]{2,1,0:T(8,128)S(1)}, f32[128,8,128]{2,1,0:T(8,128)S(1)}, f32[128,8,128]{2,1,0:T(8,128)S(1)}, f32[128,8,128]{2,1,0:T(8,128)S(1)}, bf16[128,64,128]{2,1,0:T(8,128)(2,1)S(1)}) custom-call(bf16[128,8,128]{2,1,0:T(8,128)(2,1)S(1)} %slice.4.refs_1_.refs_0_, bf16[128,8,128]{2,1,0:T(8,128)(2,1)S(1)} %get-tuple-element.31.refs_1_, ...), custom_call_target="tpu_custom_call" | custom-call | tf_op jit(solution)/shard_map/own_part/pallas_call | solution.py:74
  11.2 1.1 %partner_part.4 = (f32[2,32,8,128]{3,2,1,0:T(8,128)S(1)}, s16[66,8,128]{2,1,0:T(8,128)(2,1)S(1)}) custom-call(s32[128]{0:T(128)S(1)} %copy-done.2, f32[128,8,128]{2,1,0:T(8,128)S(1)} %get-tuple-element.38.refs_1_, bf16[128,8,128]{2,1,0:T(8,128)(2,1)S(1)} %collective-permute-done.3.refs_2_, bf16[128,64,128]{2,1,0:T(8,128)(2,1)S(1)} %get-tuple-element.35.refs_3_), custom_call_target="tpu_custom_call" | custom-call | tf_op jit(solution)/shard_map/partner_part/pallas_call | solution.py:74
  12.3 2.2 %collective-permute-start.4 = (s16[66,8,128]{2,1,0:T(8,128)(2,1)S(1)}, s16[66,8,128]{2,1,0:T(8,128)(2,1)S(1)}, u32[]{:S(2)}, u32[]{:S(2)}) collective-permute-start(s16[66,8,128]{2,1,0:T(8,128)(2,1)S(1)} %get-tuple-element.42), channel_id=1, source_target_pairs={{0,1},{1,0},{2,3},{3,2},{4,5},{5,4},{6,7},{7,6},{8,9},{9,8},{10,11... | collective-permute-start | bytes 405512 | tf_op jit(solution)/shard_map/ppermute | solution.py:21
  14.5 2.3 %collective-permute-done.2.refs_2_ = bf16[128,8,128]{2,1,0:T(8,128)(2,1)S(1)} collective-permute-done((bf16[128,8,128]{2,1,0:T(8,128)(2,1)S(1)}, bf16[128,8,128]{2,1,0:T(8,128)(2,1)S(1)}, u32[]{:S(2)}, u32[]{:S(2)}) %collective-permute-start.2) | collective-permute-done | bytes 262176 | tf_op jit(solution)/shard_map/ppermute | solution.py:21
  16.8 1.1 %partner_part.5 = (f32[2,32,8,128]{3,2,1,0:T(8,128)S(1)}, s16[66,8,128]{2,1,0:T(8,128)(2,1)S(1)}) custom-call(s32[128]{0:T(128)S(1)} %copy-done.2, f32[128,8,128]{2,1,0:T(8,128)S(1)} %get-tuple-element.37.refs_1_, bf16[128,8,128]{2,1,0:T(8,128)(2,1)S(1)} %collective-permute-done.2.refs_2_, bf16[128,64,128]{2,1,0:T(8,128)(2,1)S(1)} %get-tuple-element.35.refs_3_, ...), custom_call_target="tpu_custom_call" | custom-call | tf_op jit(solution)/shard_map/partner_part/pallas_call | solution.py:74
  17.9 2.2 %collective-permute-start.5 = (s16[66,8,128]{2,1,0:T(8,128)(2,1)S(1)}, s16[66,8,128]{2,1,0:T(8,128)(2,1)S(1)}, u32[]{:S(2)}, u32[]{:S(2)}) collective-permute-start(s16[66,8,128]{2,1,0:T(8,128)(2,1)S(1)} %get-tuple-element.43), channel_id=1, source_target_pairs={{0,1},{1,0},{2,3},{3,2},{4,5},{5,4},{6,7},{7,6},{8,9},{9,8},{10,11... | collective-permute-start | bytes 405512 | tf_op jit(solution)/shard_map/ppermute | solution.py:21
  20.1 2.3 %collective-permute-done.1.refs_2_ = bf16[128,8,128]{2,1,0:T(8,128)(2,1)S(1)} collective-permute-done((bf16[128,8,128]{2,1,0:T(8,128)(2,1)S(1)}, bf16[128,8,128]{2,1,0:T(8,128)(2,1)S(1)}, u32[]{:S(2)}, u32[]{:S(2)}) %collective-permute-start.1) | collective-permute-done | bytes 262176 | tf_op jit(solution)/shard_map/ppermute | solution.py:21
  22.4 1.1 %partner_part.6 = (f32[2,32,8,128]{3,2,1,0:T(8,128)S(1)}, s16[66,8,128]{2,1,0:T(8,128)(2,1)S(1)}) custom-call(s32[128]{0:T(128)S(1)} %copy-done.2, f32[128,8,128]{2,1,0:T(8,128)S(1)} %get-tuple-element.36.refs_1_, bf16[128,8,128]{2,1,0:T(8,128)(2,1)S(1)} %collective-permute-done.1.refs_2_, bf16[128,64,128]{2,1,0:T(8,128)(2,1)S(1)} %get-tuple-element.35.refs_3_, ...), custom_call_target="tpu_custom_call" | custom-call | tf_op jit(solution)/shard_map/partner_part/pallas_call | solution.py:74
  23.5 2.2 %collective-permute-start.11 = (s16[66,8,128]{2,1,0:T(8,128)(2,1)S(1)}, s16[66,8,128]{2,1,0:T(8,128)(2,1)S(1)}, u32[]{:S(2)}, u32[]{:S(2)}) collective-permute-start(s16[66,8,128]{2,1,0:T(8,128)(2,1)S(1)} %get-tuple-element.52), channel_id=1, source_target_pairs={{0,1},{1,0},{2,3},{3,2},{4,5},{5,4},{6,7},{7,6},{8,9},{9,8},{10,11... | collective-permute-start | bytes 405512 | tf_op jit(solution)/shard_map/ppermute | solution.py:21
  25.9 2.7 %collective-permute-start.10 = (s16[33,16,128]{2,1,0:T(8,128)(2,1)S(1)}, s16[33,16,128]{2,1,0:T(8,128)(2,1)S(1)}, u32[]{:S(2)}, u32[]{:S(2)}) collective-permute-start(s16[33,16,128]{2,1,0:T(8,128)(2,1)S(1)} %get-tuple-element.51), channel_id=1, source_target_pairs={{0,2},{1,3},{2,0},{3,1},{4,6},{5,7},{6,4},{7,5},{8,10},{9,11},{10,... | collective-permute-start | bytes 405512 | tf_op jit(solution)/shard_map/ppermute | solution.py:21
  28.5 1.2 %partner_part.7 = (f32[1,32,8,128]{3,2,1,0:T(8,128)S(1)}, s16[33,8,128]{2,1,0:T(8,128)(2,1)S(1)}, s16[33,8,128]{2,1,0:T(8,128)(2,1)S(1)}, s16[33,8,128]{2,1,0:T(8,128)(2,1)S(1)}) custom-call(s32[128]{0:T(128)S(1)} %copy-done.2, f32[128,8,128]{2,1,0:T(8,128)S(1)} %get-tuple-element.34.refs_1_, bf16[128,8,128]{2,1,0:T(8,128)(2,1)S(1)} %collective-permute-done.refs_2_, ...), custom_call_target="tpu_custom_call" | custom-call | tf_op jit(solution)/shard_map/partner_part/pallas_call | solution.py:74
  29.8 2.1 %collective-permute-start.12 = (s16[33,8,128]{2,1,0:T(8,128)(2,1)S(1)}, s16[33,8,128]{2,1,0:T(8,128)(2,1)S(1)}, u32[]{:S(2)}, u32[]{:S(2)}) collective-permute-start(s16[33,8,128]{2,1,0:T(8,128)(2,1)S(1)} %get-tuple-element.54), channel_id=1, source_target_pairs={{0,2},{1,3},{2,0},{3,1},{4,6},{5,7},{6,4},{7,5},{8,10},{9,11},{10,... | collective-permute-start | bytes 202760 | tf_op jit(solution)/shard_map/ppermute | solution.py:21
  31.9 3.0 %collective-permute-start.6 = (s16[33,8,128]{2,1,0:T(8,128)(2,1)S(1)}, s16[33,8,128]{2,1,0:T(8,128)(2,1)S(1)}, u32[]{:S(2)}, u32[]{:S(2)}) collective-permute-start(s16[33,8,128]{2,1,0:T(8,128)(2,1)S(1)} %get-tuple-element.46), channel_id=1, source_target_pairs={{0,1},{1,0},{2,3},{3,2},{4,5},{5,4},{6,7},{7,6},{8,9},{9,8},{10,11... | collective-permute-start | bytes 202760 | tf_op jit(solution)/shard_map/ppermute | solution.py:21
  35.0 2.3 %collective-permute-start.8 = (s16[33,8,128]{2,1,0:T(8,128)(2,1)S(1)}, s16[33,8,128]{2,1,0:T(8,128)(2,1)S(1)}, u32[]{:S(2)}, u32[]{:S(2)}) collective-permute-start(s16[33,8,128]{2,1,0:T(8,128)(2,1)S(1)} %get-tuple-element.48), channel_id=1, source_target_pairs={{0,3},{1,2},{2,1},{3,0},{4,7},{5,6},{6,5},{7,4},{8,11},{9,10},{10,... | collective-permute-start | bytes 202760 | tf_op jit(solution)/shard_map/ppermute | solution.py:21
  38.5 1.7 %collective-permute-start.13 = (s16[33,24,128]{2,1,0:T(8,128)(2,1)S(1)}, s16[33,24,128]{2,1,0:T(8,128)(2,1)S(1)}, u32[]{:S(2)}, u32[]{:S(2)}) collective-permute-start(s16[33,24,128]{2,1,0:T(8,128)(2,1)S(1)} %get-tuple-element.56), channel_id=1, source_target_pairs={{0,8},{4,12},{8,0},{12,4},{16,24},{20,28},{24,16},{28,20},{1,9},{5... | collective-permute-start | bytes 608264 | tf_op jit(solution)/shard_map/ppermute | solution.py:21
  40.2 1.1 %collective-permute-done.7.refs_2_ = s16[33,8,128]{2,1,0:T(8,128)(2,1)S(1)} collective-permute-done((s16[33,8,128]{2,1,0:T(8,128)(2,1)S(1)}, s16[33,8,128]{2,1,0:T(8,128)(2,1)S(1)}, u32[]{:S(2)}, u32[]{:S(2)}) %collective-permute-start.7) | collective-permute-done | bytes 67616 | tf_op jit(solution)/shard_map/ppermute | solution.py:21
  41.4 1.6 %collective-permute-start.9 = (s16[33,8,128]{2,1,0:T(8,128)(2,1)S(1)}, s16[33,8,128]{2,1,0:T(8,128)(2,1)S(1)}, u32[]{:S(2)}, u32[]{:S(2)}) collective-permute-start(s16[33,8,128]{2,1,0:T(8,128)(2,1)S(1)} %get-tuple-element.50), channel_id=1, source_target_pairs={{0,8},{4,12},{8,0},{12,4},{16,24},{20,28},{24,16},{28,20},{1,9},{5... | collective-permute-start | bytes 202760 | tf_op jit(solution)/shard_map/ppermute | solution.py:21
  43.0 1.3 %constant_dynamic-slice_fusion.factor_ref = bf16[32,2,64,128]{3,2,1,0:T(8,128)(2,1)S(1)} fusion(bf16[128,2,64,128]{3,2,1,0:T(8,128)(2,1)} %param.6, s32[]{:T(128)S(6)} %select_n.3), kind=kLoop, calls=%fused_computation | loop fusion | bytes 2097156 | tf_op jit(solution)/shard_map/dynamic_slice | solution.py:297
  44.3 1.2 %second_level.2.rest_0_ = f32[32,32,128]{2,1,0:T(8,128)} custom-call(f32[32,24,128]{2,1,0:T(8,128)S(1)} %get-tuple-element.55.own_ref, s16[33,24,128]{2,1,0:T(8,128)(2,1)S(1)} %collective-permute-done.13.coded_ref, bf16[32,2,64,128]{3,2,1,0:T(8,128)(2,1)S(1)} %constant_dynamic-slice_fusion.factor_ref), custom_call_target="tpu_custom_call" | custom-call | tf_op jit(solution)/shard_map/second_level/pallas_call | solution.py:273
  45.8 1.2 %second_level.3 = f32[32,32,128]{2,1,0:T(8,128)} custom-call(f32[32,8,128]{2,1,0:T(8,128)S(1)} %get-tuple-element.49.own_ref, s16[33,8,128]{2,1,0:T(8,128)(2,1)S(1)} %collective-permute-done.9.coded_ref, bf16[32,2,64,128]{3,2,1,0:T(8,128)(2,1)S(1)} %constant_dynamic-slice_fusion.factor_ref, ...), custom_call_target="tpu_custom_call", output_to_operand_aliasing={{}: (3, {})} | custom-call | tf_op jit(solution)/shard_map/second_level/pallas_call | solution.py:273
  (24 shorter events, 3.3 us)
Async XLA Ops:
  0.0 11.2 %copy-start.2 = (s32[128]{0:T(128)S(1)}, s32[128]{0:T(128)}, u32[]{:S(2)}) copy-start(s32[128]{0:T(128)} %refs_0_.7) | copy-start | bytes 1540
  1.0 10.2 %collective-permute-start.3 = (bf16[128,8,128]{2,1,0:T(8,128)(2,1)S(1)}, bf16[128,8,128]{2,1,0:T(8,128)(2,1)S(1)}, u32[]{:S(2)}, u32[]{:S(2)}) collective-permute-start(bf16[128,8,128]{2,1,0:T(8,128)(2,1)S(1)} %slice.4.refs_1_.refs_0_), channel_id=1, source_target_pairs={{0,16},{4,20},{8,24},{12,28},{16,0},{20,4},{24,8},{28,12},{1,17},{... | collective-permute-start | bytes 786440 | tf_op jit(solution)/shard_map/ppermute | solution.py:21
  4.0 1.2 %copy-start.1 = (bf16[1,128,32,128]{3,2,1,0:T(8,128)(2,1)S(1)}, bf16[1,128,32,128]{3,2,1,0:T(8,128)(2,1)}, u32[]{:S(2)}) copy-start(bf16[1,128,32,128]{3,2,1,0:T(8,128)(2,1)} %param.4) | copy-start | bytes 3145732
  5.4 11.4 %collective-permute-start.2 = (bf16[128,8,128]{2,1,0:T(8,128)(2,1)S(1)}, bf16[128,8,128]{2,1,0:T(8,128)(2,1)S(1)}, u32[]{:S(2)}, u32[]{:S(2)}) collective-permute-start(bf16[128,8,128]{2,1,0:T(8,128)(2,1)S(1)} %get-tuple-element.31.refs_1_), channel_id=1, source_target_pairs={{0,16},{4,20},{8,24},{12,28},{16,0},{20,4},{24,8},{28,12},{1,17},{... | collective-permute-start | bytes 786440 | tf_op jit(solution)/shard_map/ppermute | solution.py:21
  5.5 16.9 %collective-permute-start.1 = (bf16[128,8,128]{2,1,0:T(8,128)(2,1)S(1)}, bf16[128,8,128]{2,1,0:T(8,128)(2,1)S(1)}, u32[]{:S(2)}, u32[]{:S(2)}) collective-permute-start(bf16[128,8,128]{2,1,0:T(8,128)(2,1)S(1)} %get-tuple-element.32.refs_2_), channel_id=1, source_target_pairs={{0,16},{4,20},{8,24},{12,28},{16,0},{20,4},{24,8},{28,12},{1,17},{... | collective-permute-start | bytes 786440 | tf_op jit(solution)/shard_map/ppermute | solution.py:21
  7.5 21.1 %collective-permute-start = (bf16[128,8,128]{2,1,0:T(8,128)(2,1)S(1)}, bf16[128,8,128]{2,1,0:T(8,128)(2,1)S(1)}, u32[]{:S(2)}, u32[]{:S(2)}) collective-permute-start(bf16[128,8,128]{2,1,0:T(8,128)(2,1)S(1)} %get-tuple-element.33.refs_3_), channel_id=1, source_target_pairs={{0,16},{4,20},{8,24},{12,28},{16,0},{20,4},{24,8},{28,12},{1,17},{... | collective-permute-start | bytes 786440 | tf_op jit(solution)/shard_map/ppermute | solution.py:21
  7.6 2.2 %copy-start = (bf16[1,128,2,64,128]{4,3,2,1,0:T(8,128)(2,1)S(1)}, bf16[1,128,2,64,128]{4,3,2,1,0:T(8,128)(2,1)}, u32[]{:S(2)}) copy-start(bf16[1,128,2,64,128]{4,3,2,1,0:T(8,128)(2,1)} %param.5) | copy-start | bytes 12582916
  12.3 13.4 %collective-permute-start.4 = (s16[66,8,128]{2,1,0:T(8,128)(2,1)S(1)}, s16[66,8,128]{2,1,0:T(8,128)(2,1)S(1)}, u32[]{:S(2)}, u32[]{:S(2)}) collective-permute-start(s16[66,8,128]{2,1,0:T(8,128)(2,1)S(1)} %get-tuple-element.42), channel_id=1, source_target_pairs={{0,1},{1,0},{2,3},{3,2},{4,5},{5,4},{6,7},{7,6},{8,9},{9,8},{10,11... | collective-permute-start | bytes 405512 | tf_op jit(solution)/shard_map/ppermute | solution.py:21
  17.9 7.8 %collective-permute-start.5 = (s16[66,8,128]{2,1,0:T(8,128)(2,1)S(1)}, s16[66,8,128]{2,1,0:T(8,128)(2,1)S(1)}, u32[]{:S(2)}, u32[]{:S(2)}) collective-permute-start(s16[66,8,128]{2,1,0:T(8,128)(2,1)S(1)} %get-tuple-element.43), channel_id=1, source_target_pairs={{0,1},{1,0},{2,3},{3,2},{4,5},{5,4},{6,7},{7,6},{8,9},{9,8},{10,11... | collective-permute-start | bytes 405512 | tf_op jit(solution)/shard_map/ppermute | solution.py:21
  23.5 6.2 %collective-permute-start.11 = (s16[66,8,128]{2,1,0:T(8,128)(2,1)S(1)}, s16[66,8,128]{2,1,0:T(8,128)(2,1)S(1)}, u32[]{:S(2)}, u32[]{:S(2)}) collective-permute-start(s16[66,8,128]{2,1,0:T(8,128)(2,1)S(1)} %get-tuple-element.52), channel_id=1, source_target_pairs={{0,1},{1,0},{2,3},{3,2},{4,5},{5,4},{6,7},{7,6},{8,9},{9,8},{10,11... | collective-permute-start | bytes 405512 | tf_op jit(solution)/shard_map/ppermute | solution.py:21
  25.9 12.5 %collective-permute-start.10 = (s16[33,16,128]{2,1,0:T(8,128)(2,1)S(1)}, s16[33,16,128]{2,1,0:T(8,128)(2,1)S(1)}, u32[]{:S(2)}, u32[]{:S(2)}) collective-permute-start(s16[33,16,128]{2,1,0:T(8,128)(2,1)S(1)} %get-tuple-element.51), channel_id=1, source_target_pairs={{0,2},{1,3},{2,0},{3,1},{4,6},{5,7},{6,4},{7,5},{8,10},{9,11},{10,... | collective-permute-start | bytes 405512 | tf_op jit(solution)/shard_map/ppermute | solution.py:21
  29.8 8.5 %collective-permute-start.12 = (s16[33,8,128]{2,1,0:T(8,128)(2,1)S(1)}, s16[33,8,128]{2,1,0:T(8,128)(2,1)S(1)}, u32[]{:S(2)}, u32[]{:S(2)}) collective-permute-start(s16[33,8,128]{2,1,0:T(8,128)(2,1)S(1)} %get-tuple-element.54), channel_id=1, source_target_pairs={{0,2},{1,3},{2,0},{3,1},{4,6},{5,7},{6,4},{7,5},{8,10},{9,11},{10,... | collective-permute-start | bytes 202760 | tf_op jit(solution)/shard_map/ppermute | solution.py:21
  31.9 8.3 %collective-permute-start.6 = (s16[33,8,128]{2,1,0:T(8,128)(2,1)S(1)}, s16[33,8,128]{2,1,0:T(8,128)(2,1)S(1)}, u32[]{:S(2)}, u32[]{:S(2)}) collective-permute-start(s16[33,8,128]{2,1,0:T(8,128)(2,1)S(1)} %get-tuple-element.46), channel_id=1, source_target_pairs={{0,1},{1,0},{2,3},{3,2},{4,5},{5,4},{6,7},{7,6},{8,9},{9,8},{10,11... | collective-permute-start | bytes 202760 | tf_op jit(solution)/shard_map/ppermute | solution.py:21
  34.9 6.4 %collective-permute-start.7 = (s16[33,8,128]{2,1,0:T(8,128)(2,1)S(1)}, s16[33,8,128]{2,1,0:T(8,128)(2,1)S(1)}, u32[]{:S(2)}, u32[]{:S(2)}) collective-permute-start(s16[33,8,128]{2,1,0:T(8,128)(2,1)S(1)} %get-tuple-element.47), channel_id=1, source_target_pairs={{0,2},{1,3},{2,0},{3,1},{4,6},{5,7},{6,4},{7,5},{8,10},{9,11},{10,... | collective-permute-start | bytes 202760 | tf_op jit(solution)/shard_map/ppermute | solution.py:21
  35.0 6.4 %collective-permute-start.8 = (s16[33,8,128]{2,1,0:T(8,128)(2,1)S(1)}, s16[33,8,128]{2,1,0:T(8,128)(2,1)S(1)}, u32[]{:S(2)}, u32[]{:S(2)}) collective-permute-start(s16[33,8,128]{2,1,0:T(8,128)(2,1)S(1)} %get-tuple-element.48), channel_id=1, source_target_pairs={{0,3},{1,2},{2,1},{3,0},{4,7},{5,6},{6,5},{7,4},{8,11},{9,10},{10,... | collective-permute-start | bytes 202760 | tf_op jit(solution)/shard_map/ppermute | solution.py:21
  38.5 5.8 %collective-permute-start.13 = (s16[33,24,128]{2,1,0:T(8,128)(2,1)S(1)}, s16[33,24,128]{2,1,0:T(8,128)(2,1)S(1)}, u32[]{:S(2)}, u32[]{:S(2)}) collective-permute-start(s16[33,24,128]{2,1,0:T(8,128)(2,1)S(1)} %get-tuple-element.56), channel_id=1, source_target_pairs={{0,8},{4,12},{8,0},{12,4},{16,24},{20,28},{24,16},{28,20},{1,9},{5... | collective-permute-start | bytes 608264 | tf_op jit(solution)/shard_map/ppermute | solution.py:21
  41.4 4.4 %collective-permute-start.9 = (s16[33,8,128]{2,1,0:T(8,128)(2,1)S(1)}, s16[33,8,128]{2,1,0:T(8,128)(2,1)S(1)}, u32[]{:S(2)}, u32[]{:S(2)}) collective-permute-start(s16[33,8,128]{2,1,0:T(8,128)(2,1)S(1)} %get-tuple-element.50), channel_id=1, source_target_pairs={{0,8},{4,12},{8,0},{12,4},{16,24},{20,28},{24,16},{28,20},{1,9},{5... | collective-permute-start | bytes 202760 | tf_op jit(solution)/shard_map/ppermute | solution.py:21

commit v4 on v3

--- a/solution.py
+++ b/solution.py
@@ -296,7 +296,7 @@
     owns, factors = own_part(values, first_factors)
     mine = lax.dynamic_slice_in_dim(second_factors, me * share, share, 0)
     waiting, marks = {}, {"mine": mine}
-    order = [('first', (0,)), ('first', (1,), ('first', (0,))), ('first', (2,), ('first', (1,))), ('halve', (0, 1), ('first', (2,))), ('first', (3,), ('first', (2,)), ('halve', (0, 1))), ('halve', (2,), ('first', (3,)))]
+    order = [('first', (0,)), ('first', (1,), ('first', (0,))), ('first', (2,), ('first', (1,))), ('halve', (0, 1), ('first', (2,))), ('first', (3,), ('first', (2,))), ('halve', (2,), ('first', (3,)))]
     for step, chunks, *before in order:
         last = [marks[b] for b in before]
         if step == "first":

time: 47.2 us -> 47.2 us (level)
  transfers between devices with their start and end apart: 14 -> 14, of which waited for: 6 -> 7; matrix products, arithmetic and copies ran while one was open for 3% -> 3% of each run, Pallas kernels for 17% -> 17%
where the time goes in v4:
time: 47.2 us; the launch traced here: 47 us
  starting transfers between devices  25 us (53%)
  Pallas kernels  8.97 us (19%)
  waiting for transfers between devices  7.22 us (15%)
  local copies, waits for them, and re-layouts  5.69 us (12%)
    ppermute x14, starting transfers between devices, swapped(): lax.ppermute(block, axis, [(i, i ^ mask) for i in range(lax.axis_size(axi...  25 us
    ppermute x14, waiting for transfers between devices, swapped(): lax.ppermute(block, axis, [(i, i ^ mask) for i in range(lax.axis_size(axi...  7.22 us
    pallas_call x10, Pallas kernels, call(): pl.pallas_call(body, in_specs=in_specs + [ANY] * len(after), out_specs=[V...  6.54 us
    unnamed x6, local copies, waits for them, and re-layouts  3.42 us
    pallas_call x2, Pallas kernels, second_level(): pl.pallas_call(functools.partial(second_kernel, start), in_specs=[VMEM] *...  2.43 us
    dynamic_slice x1, local copies, waits for them, and re-layouts, on_device(): mine = lax.dynamic_slice_in_dim(second_factors, me * share, share, 0)  1.3 us
    slice x1, local copies, waits for them, and re-layouts, on_device(): values = [sources[:, :CHUNKS[0]]]  0.98 us
  transfers between devices with their start and end apart: 14, of which 7 were waited for; matrix products, arithmetic and copies ran while one was open for 3% of the time, Pallas kernels for 17%

profile of v4, /device:TPU:0, one launch (start us, length us, event | category | flops | bytes accessed | tf_op | source)
XLA Modules:
  0.0 47.0 jit_solution(4696018112723892657)
XLA Ops:
  1.0 3.0 %collective-permute-start.3 = (bf16[128,8,128]{2,1,0:T(8,128)(2,1)S(1)}, bf16[128,8,128]{2,1,0:T(8,128)(2,1)S(1)}, u32[]{:S(2)}, u32[]{:S(2)}) collective-permute-start(bf16[128,8,128]{2,1,0:T(8,128)(2,1)S(1)} %slice.4.refs_1_.refs_0_), channel_id=1, source_target_pairs={{0,16},{4,20},{8,24},{12,28},{16,0},{20,4},{24,8},{28,12},{1,17},{... | collective-permute-start | bytes 786440 | tf_op jit(solution)/shard_map/ppermute | solution.py:21
  4.0 1.2 %copy-done.1 = bf16[1,128,32,128]{3,2,1,0:T(8,128)(2,1)S(1)} copy-done((bf16[1,128,32,128]{3,2,1,0:T(8,128)(2,1)S(1)}, bf16[1,128,32,128]{3,2,1,0:T(8,128)(2,1)}, u32[]{:S(2)}) %copy-start.1) | copy-done | bytes 1048600
  5.5 2.0 %collective-permute-start.1 = (bf16[128,8,128]{2,1,0:T(8,128)(2,1)S(1)}, bf16[128,8,128]{2,1,0:T(8,128)(2,1)S(1)}, u32[]{:S(2)}, u32[]{:S(2)}) collective-permute-start(bf16[128,8,128]{2,1,0:T(8,128)(2,1)S(1)} %get-tuple-element.32.refs_2_), channel_id=1, source_target_pairs={{0,16},{4,20},{8,24},{12,28},{16,0},{20,4},{24,8},{28,12},{1,17},{... | collective-permute-start | bytes 786440 | tf_op jit(solution)/shard_map/ppermute | solution.py:21
  7.6 2.2 %copy-done = bf16[1,128,2,64,128]{4,3,2,1,0:T(8,128)(2,1)S(1)} copy-done((bf16[1,128,2,64,128]{4,3,2,1,0:T(8,128)(2,1)S(1)}, bf16[1,128,2,64,128]{4,3,2,1,0:T(8,128)(2,1)}, u32[]{:S(2)}) %copy-start) | copy-done | bytes 4194328
  9.7 1.3 %own_part.1 = (f32[128,8,128]{2,1,0:T(8,128)S(1)}, f32[128,8,128]{2,1,0:T(8,128)S(1)}, f32[128,8,128]{2,1,0:T(8,128)S(1)}, f32[128,8,128]{2,1,0:T(8,128)S(1)}, bf16[128,64,128]{2,1,0:T(8,128)(2,1)S(1)}) custom-call(bf16[128,8,128]{2,1,0:T(8,128)(2,1)S(1)} %slice.4.refs_1_.refs_0_, bf16[128,8,128]{2,1,0:T(8,128)(2,1)S(1)} %get-tuple-element.31.refs_1_, ...), custom_call_target="tpu_custom_call" | custom-call | tf_op jit(solution)/shard_map/own_part/pallas_call | solution.py:74
  11.2 1.1 %partner_part.4 = (f32[2,32,8,128]{3,2,1,0:T(8,128)S(1)}, s16[66,8,128]{2,1,0:T(8,128)(2,1)S(1)}) custom-call(s32[128]{0:T(128)S(1)} %copy-done.2, f32[128,8,128]{2,1,0:T(8,128)S(1)} %get-tuple-element.38.refs_1_, bf16[128,8,128]{2,1,0:T(8,128)(2,1)S(1)} %collective-permute-done.3.refs_2_, bf16[128,64,128]{2,1,0:T(8,128)(2,1)S(1)} %get-tuple-element.35.refs_3_), custom_call_target="tpu_custom_call" | custom-call | tf_op jit(solution)/shard_map/partner_part/pallas_call | solution.py:74
  12.3 2.2 %collective-permute-start.8 = (s16[66,8,128]{2,1,0:T(8,128)(2,1)S(1)}, s16[66,8,128]{2,1,0:T(8,128)(2,1)S(1)}, u32[]{:S(2)}, u32[]{:S(2)}) collective-permute-start(s16[66,8,128]{2,1,0:T(8,128)(2,1)S(1)} %get-tuple-element.48), channel_id=1, source_target_pairs={{0,1},{1,0},{2,3},{3,2},{4,5},{5,4},{6,7},{7,6},{8,9},{9,8},{10,11... | collective-permute-start | bytes 405512 | tf_op jit(solution)/shard_map/ppermute | solution.py:21
  14.5 2.3 %collective-permute-done.2.refs_2_ = bf16[128,8,128]{2,1,0:T(8,128)(2,1)S(1)} collective-permute-done((bf16[128,8,128]{2,1,0:T(8,128)(2,1)S(1)}, bf16[128,8,128]{2,1,0:T(8,128)(2,1)S(1)}, u32[]{:S(2)}, u32[]{:S(2)}) %collective-permute-start.2) | collective-permute-done | bytes 262176 | tf_op jit(solution)/shard_map/ppermute | solution.py:21
  16.8 1.1 %partner_part.5 = (f32[2,32,8,128]{3,2,1,0:T(8,128)S(1)}, s16[66,8,128]{2,1,0:T(8,128)(2,1)S(1)}) custom-call(s32[128]{0:T(128)S(1)} %copy-done.2, f32[128,8,128]{2,1,0:T(8,128)S(1)} %get-tuple-element.37.refs_1_, bf16[128,8,128]{2,1,0:T(8,128)(2,1)S(1)} %collective-permute-done.2.refs_2_, bf16[128,64,128]{2,1,0:T(8,128)(2,1)S(1)} %get-tuple-element.35.refs_3_, ...), custom_call_target="tpu_custom_call" | custom-call | tf_op jit(solution)/shard_map/partner_part/pallas_call | solution.py:74
  17.9 2.2 %collective-permute-start.9 = (s16[66,8,128]{2,1,0:T(8,128)(2,1)S(1)}, s16[66,8,128]{2,1,0:T(8,128)(2,1)S(1)}, u32[]{:S(2)}, u32[]{:S(2)}) collective-permute-start(s16[66,8,128]{2,1,0:T(8,128)(2,1)S(1)} %get-tuple-element.49), channel_id=1, source_target_pairs={{0,1},{1,0},{2,3},{3,2},{4,5},{5,4},{6,7},{7,6},{8,9},{9,8},{10,11... | collective-permute-start | bytes 405512 | tf_op jit(solution)/shard_map/ppermute | solution.py:21
  20.1 2.3 %collective-permute-done.1.refs_2_ = bf16[128,8,128]{2,1,0:T(8,128)(2,1)S(1)} collective-permute-done((bf16[128,8,128]{2,1,0:T(8,128)(2,1)S(1)}, bf16[128,8,128]{2,1,0:T(8,128)(2,1)S(1)}, u32[]{:S(2)}, u32[]{:S(2)}) %collective-permute-start.1) | collective-permute-done | bytes 262176 | tf_op jit(solution)/shard_map/ppermute | solution.py:21
  22.4 1.1 %partner_part.6 = (f32[2,32,8,128]{3,2,1,0:T(8,128)S(1)}, s16[66,8,128]{2,1,0:T(8,128)(2,1)S(1)}) custom-call(s32[128]{0:T(128)S(1)} %copy-done.2, f32[128,8,128]{2,1,0:T(8,128)S(1)} %get-tuple-element.36.refs_1_, bf16[128,8,128]{2,1,0:T(8,128)(2,1)S(1)} %collective-permute-done.1.refs_2_, bf16[128,64,128]{2,1,0:T(8,128)(2,1)S(1)} %get-tuple-element.35.refs_3_, ...), custom_call_target="tpu_custom_call" | custom-call | tf_op jit(solution)/shard_map/partner_part/pallas_call | solution.py:74
  23.5 2.2 %collective-permute-start.11 = (s16[66,8,128]{2,1,0:T(8,128)(2,1)S(1)}, s16[66,8,128]{2,1,0:T(8,128)(2,1)S(1)}, u32[]{:S(2)}, u32[]{:S(2)}) collective-permute-start(s16[66,8,128]{2,1,0:T(8,128)(2,1)S(1)} %get-tuple-element.52), channel_id=1, source_target_pairs={{0,1},{1,0},{2,3},{3,2},{4,5},{5,4},{6,7},{7,6},{8,9},{9,8},{10,11... | collective-permute-start | bytes 405512 | tf_op jit(solution)/shard_map/ppermute | solution.py:21
  25.9 2.6 %collective-permute-start.10 = (s16[33,16,128]{2,1,0:T(8,128)(2,1)S(1)}, s16[33,16,128]{2,1,0:T(8,128)(2,1)S(1)}, u32[]{:S(2)}, u32[]{:S(2)}) collective-permute-start(s16[33,16,128]{2,1,0:T(8,128)(2,1)S(1)} %get-tuple-element.51), channel_id=1, source_target_pairs={{0,2},{1,3},{2,0},{3,1},{4,6},{5,7},{6,4},{7,5},{8,10},{9,11},{10,... | collective-permute-start | bytes 405512 | tf_op jit(solution)/shard_map/ppermute | solution.py:21
  28.6 1.1 %partner_part.7 = (f32[1,32,8,128]{3,2,1,0:T(8,128)S(1)}, s16[33,8,128]{2,1,0:T(8,128)(2,1)S(1)}, s16[33,8,128]{2,1,0:T(8,128)(2,1)S(1)}, s16[33,8,128]{2,1,0:T(8,128)(2,1)S(1)}) custom-call(s32[128]{0:T(128)S(1)} %copy-done.2, f32[128,8,128]{2,1,0:T(8,128)S(1)} %get-tuple-element.34.refs_1_, bf16[128,8,128]{2,1,0:T(8,128)(2,1)S(1)} %collective-permute-done.refs_2_, ...), custom_call_target="tpu_custom_call" | custom-call | tf_op jit(solution)/shard_map/partner_part/pallas_call | solution.py:74
  29.8 2.1 %collective-permute-start.12 = (s16[33,8,128]{2,1,0:T(8,128)(2,1)S(1)}, s16[33,8,128]{2,1,0:T(8,128)(2,1)S(1)}, u32[]{:S(2)}, u32[]{:S(2)}) collective-permute-start(s16[33,8,128]{2,1,0:T(8,128)(2,1)S(1)} %get-tuple-element.54), channel_id=1, source_target_pairs={{0,2},{1,3},{2,0},{3,1},{4,6},{5,7},{6,4},{7,5},{8,10},{9,11},{10,... | collective-permute-start | bytes 202760 | tf_op jit(solution)/shard_map/ppermute | solution.py:21
  31.9 3.1 %collective-permute-start.4 = (s16[33,8,128]{2,1,0:T(8,128)(2,1)S(1)}, s16[33,8,128]{2,1,0:T(8,128)(2,1)S(1)}, u32[]{:S(2)}, u32[]{:S(2)}) collective-permute-start(s16[33,8,128]{2,1,0:T(8,128)(2,1)S(1)} %get-tuple-element.43), channel_id=1, source_target_pairs={{0,1},{1,0},{2,3},{3,2},{4,5},{5,4},{6,7},{7,6},{8,9},{9,8},{10,11... | collective-permute-start | bytes 202760 | tf_op jit(solution)/shard_map/ppermute | solution.py:21
  35.1 2.3 %collective-permute-start.6 = (s16[33,8,128]{2,1,0:T(8,128)(2,1)S(1)}, s16[33,8,128]{2,1,0:T(8,128)(2,1)S(1)}, u32[]{:S(2)}, u32[]{:S(2)}) collective-permute-start(s16[33,8,128]{2,1,0:T(8,128)(2,1)S(1)} %get-tuple-element.45), channel_id=1, source_target_pairs={{0,3},{1,2},{2,1},{3,0},{4,7},{5,6},{6,5},{7,4},{8,11},{9,10},{10,... | collective-permute-start | bytes 202760 | tf_op jit(solution)/shard_map/ppermute | solution.py:21
  38.6 1.6 %collective-permute-start.13 = (s16[33,24,128]{2,1,0:T(8,128)(2,1)S(1)}, s16[33,24,128]{2,1,0:T(8,128)(2,1)S(1)}, u32[]{:S(2)}, u32[]{:S(2)}) collective-permute-start(s16[33,24,128]{2,1,0:T(8,128)(2,1)S(1)} %get-tuple-element.56), channel_id=1, source_target_pairs={{0,8},{4,12},{8,0},{12,4},{16,24},{20,28},{24,16},{28,20},{1,9},{5... | collective-permute-start | bytes 608264 | tf_op jit(solution)/shard_map/ppermute | solution.py:21
  40.1 1.2 %collective-permute-done.5.refs_2_ = s16[33,8,128]{2,1,0:T(8,128)(2,1)S(1)} collective-permute-done((s16[33,8,128]{2,1,0:T(8,128)(2,1)S(1)}, s16[33,8,128]{2,1,0:T(8,128)(2,1)S(1)}, u32[]{:S(2)}, u32[]{:S(2)}) %collective-permute-start.5) | collective-permute-done | bytes 67616 | tf_op jit(solution)/shard_map/ppermute | solution.py:21
  41.5 1.5 %collective-permute-start.7 = (s16[33,8,128]{2,1,0:T(8,128)(2,1)S(1)}, s16[33,8,128]{2,1,0:T(8,128)(2,1)S(1)}, u32[]{:S(2)}, u32[]{:S(2)}) collective-permute-start(s16[33,8,128]{2,1,0:T(8,128)(2,1)S(1)} %get-tuple-element.47), channel_id=1, source_target_pairs={{0,8},{4,12},{8,0},{12,4},{16,24},{20,28},{24,16},{28,20},{1,9},{5... | collective-permute-start | bytes 202760 | tf_op jit(solution)/shard_map/ppermute | solution.py:21
  43.0 1.3 %constant_dynamic-slice_fusion.factor_ref = bf16[32,2,64,128]{3,2,1,0:T(8,128)(2,1)S(1)} fusion(bf16[128,2,64,128]{3,2,1,0:T(8,128)(2,1)} %param.6, s32[]{:T(128)S(6)} %select_n.3), kind=kLoop, calls=%fused_computation | loop fusion | bytes 2097156 | tf_op jit(solution)/shard_map/dynamic_slice | solution.py:297
  44.4 1.3 %second_level.2.rest_0_ = f32[32,32,128]{2,1,0:T(8,128)} custom-call(f32[32,24,128]{2,1,0:T(8,128)S(1)} %get-tuple-element.55.own_ref, s16[33,24,128]{2,1,0:T(8,128)(2,1)S(1)} %collective-permute-done.13.coded_ref, bf16[32,2,64,128]{3,2,1,0:T(8,128)(2,1)S(1)} %constant_dynamic-slice_fusion.factor_ref), custom_call_target="tpu_custom_call" | custom-call | tf_op jit(solution)/shard_map/second_level/pallas_call | solution.py:273
  45.8 1.2 %second_level.3 = f32[32,32,128]{2,1,0:T(8,128)} custom-call(f32[32,8,128]{2,1,0:T(8,128)S(1)} %get-tuple-element.46.own_ref, s16[33,8,128]{2,1,0:T(8,128)(2,1)S(1)} %collective-permute-done.7.coded_ref, bf16[32,2,64,128]{3,2,1,0:T(8,128)(2,1)S(1)} %constant_dynamic-slice_fusion.factor_ref, ...), custom_call_target="tpu_custom_call", output_to_operand_aliasing={{}: (3, {})} | custom-call | tf_op jit(solution)/shard_map/second_level/pallas_call | solution.py:273
  (24 shorter events, 3.3 us)
Async XLA Ops:
  0.0 11.2 %copy-start.2 = (s32[128]{0:T(128)S(1)}, s32[128]{0:T(128)}, u32[]{:S(2)}) copy-start(s32[128]{0:T(128)} %refs_0_.7) | copy-start | bytes 1540
  1.0 10.2 %collective-permute-start.3 = (bf16[128,8,128]{2,1,0:T(8,128)(2,1)S(1)}, bf16[128,8,128]{2,1,0:T(8,128)(2,1)S(1)}, u32[]{:S(2)}, u32[]{:S(2)}) collective-permute-start(bf16[128,8,128]{2,1,0:T(8,128)(2,1)S(1)} %slice.4.refs_1_.refs_0_), channel_id=1, source_target_pairs={{0,16},{4,20},{8,24},{12,28},{16,0},{20,4},{24,8},{28,12},{1,17},{... | collective-permute-start | bytes 786440 | tf_op jit(solution)/shard_map/ppermute | solution.py:21
  4.0 1.2 %copy-start.1 = (bf16[1,128,32,128]{3,2,1,0:T(8,128)(2,1)S(1)}, bf16[1,128,32,128]{3,2,1,0:T(8,128)(2,1)}, u32[]{:S(2)}) copy-start(bf16[1,128,32,128]{3,2,1,0:T(8,128)(2,1)} %param.4) | copy-start | bytes 3145732
  5.4 11.4 %collective-permute-start.2 = (bf16[128,8,128]{2,1,0:T(8,128)(2,1)S(1)}, bf16[128,8,128]{2,1,0:T(8,128)(2,1)S(1)}, u32[]{:S(2)}, u32[]{:S(2)}) collective-permute-start(bf16[128,8,128]{2,1,0:T(8,128)(2,1)S(1)} %get-tuple-element.31.refs_1_), channel_id=1, source_target_pairs={{0,16},{4,20},{8,24},{12,28},{16,0},{20,4},{24,8},{28,12},{1,17},{... | collective-permute-start | bytes 786440 | tf_op jit(solution)/shard_map/ppermute | solution.py:21
  5.5 16.9 %collective-permute-start.1 = (bf16[128,8,128]{2,1,0:T(8,128)(2,1)S(1)}, bf16[128,8,128]{2,1,0:T(8,128)(2,1)S(1)}, u32[]{:S(2)}, u32[]{:S(2)}) collective-permute-start(bf16[128,8,128]{2,1,0:T(8,128)(2,1)S(1)} %get-tuple-element.32.refs_2_), channel_id=1, source_target_pairs={{0,16},{4,20},{8,24},{12,28},{16,0},{20,4},{24,8},{28,12},{1,17},{... | collective-permute-start | bytes 786440 | tf_op jit(solution)/shard_map/ppermute | solution.py:21
  7.5 21.1 %collective-permute-start = (bf16[128,8,128]{2,1,0:T(8,128)(2,1)S(1)}, bf16[128,8,128]{2,1,0:T(8,128)(2,1)S(1)}, u32[]{:S(2)}, u32[]{:S(2)}) collective-permute-start(bf16[128,8,128]{2,1,0:T(8,128)(2,1)S(1)} %get-tuple-element.33.refs_3_), channel_id=1, source_target_pairs={{0,16},{4,20},{8,24},{12,28},{16,0},{20,4},{24,8},{28,12},{1,17},{... | collective-permute-start | bytes 786440 | tf_op jit(solution)/shard_map/ppermute | solution.py:21
  7.6 2.2 %copy-start = (bf16[1,128,2,64,128]{4,3,2,1,0:T(8,128)(2,1)S(1)}, bf16[1,128,2,64,128]{4,3,2,1,0:T(8,128)(2,1)}, u32[]{:S(2)}) copy-start(bf16[1,128,2,64,128]{4,3,2,1,0:T(8,128)(2,1)} %param.5) | copy-start | bytes 12582916
  12.3 13.4 %collective-permute-start.8 = (s16[66,8,128]{2,1,0:T(8,128)(2,1)S(1)}, s16[66,8,128]{2,1,0:T(8,128)(2,1)S(1)}, u32[]{:S(2)}, u32[]{:S(2)}) collective-permute-start(s16[66,8,128]{2,1,0:T(8,128)(2,1)S(1)} %get-tuple-element.48), channel_id=1, source_target_pairs={{0,1},{1,0},{2,3},{3,2},{4,5},{5,4},{6,7},{7,6},{8,9},{9,8},{10,11... | collective-permute-start | bytes 405512 | tf_op jit(solution)/shard_map/ppermute | solution.py:21
  17.9 7.8 %collective-permute-start.9 = (s16[66,8,128]{2,1,0:T(8,128)(2,1)S(1)}, s16[66,8,128]{2,1,0:T(8,128)(2,1)S(1)}, u32[]{:S(2)}, u32[]{:S(2)}) collective-permute-start(s16[66,8,128]{2,1,0:T(8,128)(2,1)S(1)} %get-tuple-element.49), channel_id=1, source_target_pairs={{0,1},{1,0},{2,3},{3,2},{4,5},{5,4},{6,7},{7,6},{8,9},{9,8},{10,11... | collective-permute-start | bytes 405512 | tf_op jit(solution)/shard_map/ppermute | solution.py:21
  23.5 6.2 %collective-permute-start.11 = (s16[66,8,128]{2,1,0:T(8,128)(2,1)S(1)}, s16[66,8,128]{2,1,0:T(8,128)(2,1)S(1)}, u32[]{:S(2)}, u32[]{:S(2)}) collective-permute-start(s16[66,8,128]{2,1,0:T(8,128)(2,1)S(1)} %get-tuple-element.52), channel_id=1, source_target_pairs={{0,1},{1,0},{2,3},{3,2},{4,5},{5,4},{6,7},{7,6},{8,9},{9,8},{10,11... | collective-permute-start | bytes 405512 | tf_op jit(solution)/shard_map/ppermute | solution.py:21
  25.9 12.5 %collective-permute-start.10 = (s16[33,16,128]{2,1,0:T(8,128)(2,1)S(1)}, s16[33,16,128]{2,1,0:T(8,128)(2,1)S(1)}, u32[]{:S(2)}, u32[]{:S(2)}) collective-permute-start(s16[33,16,128]{2,1,0:T(8,128)(2,1)S(1)} %get-tuple-element.51), channel_id=1, source_target_pairs={{0,2},{1,3},{2,0},{3,1},{4,6},{5,7},{6,4},{7,5},{8,10},{9,11},{10,... | collective-permute-start | bytes 405512 | tf_op jit(solution)/shard_map/ppermute | solution.py:21
  29.8 8.6 %collective-permute-start.12 = (s16[33,8,128]{2,1,0:T(8,128)(2,1)S(1)}, s16[33,8,128]{2,1,0:T(8,128)(2,1)S(1)}, u32[]{:S(2)}, u32[]{:S(2)}) collective-permute-start(s16[33,8,128]{2,1,0:T(8,128)(2,1)S(1)} %get-tuple-element.54), channel_id=1, source_target_pairs={{0,2},{1,3},{2,0},{3,1},{4,6},{5,7},{6,4},{7,5},{8,10},{9,11},{10,... | collective-permute-start | bytes 202760 | tf_op jit(solution)/shard_map/ppermute | solution.py:21
  31.9 8.2 %collective-permute-start.4 = (s16[33,8,128]{2,1,0:T(8,128)(2,1)S(1)}, s16[33,8,128]{2,1,0:T(8,128)(2,1)S(1)}, u32[]{:S(2)}, u32[]{:S(2)}) collective-permute-start(s16[33,8,128]{2,1,0:T(8,128)(2,1)S(1)} %get-tuple-element.43), channel_id=1, source_target_pairs={{0,1},{1,0},{2,3},{3,2},{4,5},{5,4},{6,7},{7,6},{8,9},{9,8},{10,11... | collective-permute-start | bytes 202760 | tf_op jit(solution)/shard_map/ppermute | solution.py:21
  35.0 6.4 %collective-permute-start.5 = (s16[33,8,128]{2,1,0:T(8,128)(2,1)S(1)}, s16[33,8,128]{2,1,0:T(8,128)(2,1)S(1)}, u32[]{:S(2)}, u32[]{:S(2)}) collective-permute-start(s16[33,8,128]{2,1,0:T(8,128)(2,1)S(1)} %get-tuple-element.44), channel_id=1, source_target_pairs={{0,2},{1,3},{2,0},{3,1},{4,6},{5,7},{6,4},{7,5},{8,10},{9,11},{10,... | collective-permute-start | bytes 202760 | tf_op jit(solution)/shard_map/ppermute | solution.py:21
  35.1 6.3 %collective-permute-start.6 = (s16[33,8,128]{2,1,0:T(8,128)(2,1)S(1)}, s16[33,8,128]{2,1,0:T(8,128)(2,1)S(1)}, u32[]{:S(2)}, u32[]{:S(2)}) collective-permute-start(s16[33,8,128]{2,1,0:T(8,128)(2,1)S(1)} %get-tuple-element.45), channel_id=1, source_target_pairs={{0,3},{1,2},{2,1},{3,0},{4,7},{5,6},{6,5},{7,4},{8,11},{9,10},{10,... | collective-permute-start | bytes 202760 | tf_op jit(solution)/shard_map/ppermute | solution.py:21
  38.6 5.8 %collective-permute-start.13 = (s16[33,24,128]{2,1,0:T(8,128)(2,1)S(1)}, s16[33,24,128]{2,1,0:T(8,128)(2,1)S(1)}, u32[]{:S(2)}, u32[]{:S(2)}) collective-permute-start(s16[33,24,128]{2,1,0:T(8,128)(2,1)S(1)} %get-tuple-element.56), channel_id=1, source_target_pairs={{0,8},{4,12},{8,0},{12,4},{16,24},{20,28},{24,16},{28,20},{1,9},{5... | collective-permute-start | bytes 608264 | tf_op jit(solution)/shard_map/ppermute | solution.py:21
  41.5 4.4 %collective-permute-start.7 = (s16[33,8,128]{2,1,0:T(8,128)(2,1)S(1)}, s16[33,8,128]{2,1,0:T(8,128)(2,1)S(1)}, u32[]{:S(2)}, u32[]{:S(2)}) collective-permute-start(s16[33,8,128]{2,1,0:T(8,128)(2,1)S(1)} %get-tuple-element.47), channel_id=1, source_target_pairs={{0,8},{4,12},{8,0},{12,4},{16,24},{20,28},{24,16},{28,20},{1,9},{5... | collective-permute-start | bytes 202760 | tf_op jit(solution)/shard_map/ppermute | solution.py:21

commit v5 on v3

--- a/solution.py
+++ b/solution.py
@@ -250,12 +250,20 @@
     share, rows, width = own_ref.shape
     read = decoder(coded_ref, 0, share)
     copies = []
-    for i in range(share):
-        values = stacked(own_ref[i], read(i))
-        high = values.astype(jnp.bfloat16)
-        low = (values - high.astype(jnp.float32)).astype(jnp.bfloat16)
-        product = dot(jnp.concatenate([high, low], axis=0), factor_ref[i].reshape(width, width))
-        out[i] = folded(product[: 2 * rows] + product[2 * rows :])
+    zero = jnp.zeros((4 * rows, width), jnp.bfloat16)
+    for i in range(1, share, 2):
+        lines = []
+        for j in (i - 1, i):
+            values = stacked(own_ref[j], read(j))
+            high = values.astype(jnp.bfloat16)
+            low = (values - high.astype(jnp.float32)).astype(jnp.bfloat16)
+            both = jnp.concatenate([high, low], axis=0)
+            lines.append(jnp.concatenate([both, zero] if j < i else [zero, both], axis=1))
+        factor = factor_ref[pl.ds(i - 1, 2)].reshape(2 * width, width)
+        product = dot(jnp.concatenate(lines, axis=0), factor)
+        for j in range(2):
+            part = product[4 * rows * j : 4 * rows * (j + 1)]
+            out[i - 1 + j] = folded(part[: 2 * rows] + part[2 * rows :])
         if (i + 1) % GROUP == 0:
             some = pl.ds(i + 1 - GROUP, GROUP)
             copy = pltpu.make_async_copy(

time: 47.2 us -> 47.1 us (level)
  no operation moved by 1% of the time
where the time goes in v5:
time: 47.1 us; the launch traced here: 46.9 us
  starting transfers between devices  25 us (53%)
  Pallas kernels  9.02 us (19%)
  waiting for transfers between devices  7.08 us (15%)
  local copies, waits for them, and re-layouts  5.69 us (12%)
    ppermute x14, starting transfers between devices, swapped(): lax.ppermute(block, axis, [(i, i ^ mask) for i in range(lax.axis_size(axi...  25 us
    ppermute x14, waiting for transfers between devices, swapped(): lax.ppermute(block, axis, [(i, i ^ mask) for i in range(lax.axis_size(axi...  7.08 us
    pallas_call x10, Pallas kernels, call(): pl.pallas_call(body, in_specs=in_specs + [ANY] * len(after), out_specs=[V...  6.55 us
    unnamed x6, local copies, waits for them, and re-layouts  3.42 us
    pallas_call x2, Pallas kernels, second_level(): pl.pallas_call(functools.partial(second_kernel, start), in_specs=[VMEM] *...  2.47 us
    dynamic_slice x1, local copies, waits for them, and re-layouts, on_device(): mine = lax.dynamic_slice_in_dim(second_factors, me * share, share, 0)  1.3 us
    slice x1, local copies, waits for them, and re-layouts, on_device(): values = [sources[:, :CHUNKS[0]]]  0.98 us
  transfers between devices with their start and end apart: 14, of which 6 were waited for; matrix products, arithmetic and copies ran while one was open for 3% of the time, Pallas kernels for 17%

profile of v5, /device:TPU:0, one launch (start us, length us, event | category | flops | bytes accessed | tf_op | source)
XLA Modules:
  0.0 46.9 jit_solution(5100963826250064225)
XLA Ops:
  1.0 3.0 %collective-permute-start.3 = (bf16[128,8,128]{2,1,0:T(8,128)(2,1)S(1)}, bf16[128,8,128]{2,1,0:T(8,128)(2,1)S(1)}, u32[]{:S(2)}, u32[]{:S(2)}) collective-permute-start(bf16[128,8,128]{2,1,0:T(8,128)(2,1)S(1)} %slice.4.refs_1_.refs_0_), channel_id=1, source_target_pairs={{0,16},{4,20},{8,24},{12,28},{16,0},{20,4},{24,8},{28,12},{1,17},{... | collective-permute-start | bytes 786440 | tf_op jit(solution)/shard_map/ppermute | solution.py:21
  4.0 1.2 %copy-done.1 = bf16[1,128,32,128]{3,2,1,0:T(8,128)(2,1)S(1)} copy-done((bf16[1,128,32,128]{3,2,1,0:T(8,128)(2,1)S(1)}, bf16[1,128,32,128]{3,2,1,0:T(8,128)(2,1)}, u32[]{:S(2)}) %copy-start.1) | copy-done | bytes 1048600
  5.5 2.0 %collective-permute-start.1 = (bf16[128,8,128]{2,1,0:T(8,128)(2,1)S(1)}, bf16[128,8,128]{2,1,0:T(8,128)(2,1)S(1)}, u32[]{:S(2)}, u32[]{:S(2)}) collective-permute-start(bf16[128,8,128]{2,1,0:T(8,128)(2,1)S(1)} %get-tuple-element.32.refs_2_), channel_id=1, source_target_pairs={{0,16},{4,20},{8,24},{12,28},{16,0},{20,4},{24,8},{28,12},{1,17},{... | collective-permute-start | bytes 786440 | tf_op jit(solution)/shard_map/ppermute | solution.py:21
  7.6 2.2 %copy-done = bf16[1,128,2,64,128]{4,3,2,1,0:T(8,128)(2,1)S(1)} copy-done((bf16[1,128,2,64,128]{4,3,2,1,0:T(8,128)(2,1)S(1)}, bf16[1,128,2,64,128]{4,3,2,1,0:T(8,128)(2,1)}, u32[]{:S(2)}) %copy-start) | copy-done | bytes 4194328
  9.7 1.3 %own_part.1 = (f32[128,8,128]{2,1,0:T(8,128)S(1)}, f32[128,8,128]{2,1,0:T(8,128)S(1)}, f32[128,8,128]{2,1,0:T(8,128)S(1)}, f32[128,8,128]{2,1,0:T(8,128)S(1)}, bf16[128,64,128]{2,1,0:T(8,128)(2,1)S(1)}) custom-call(bf16[128,8,128]{2,1,0:T(8,128)(2,1)S(1)} %slice.4.refs_1_.refs_0_, bf16[128,8,128]{2,1,0:T(8,128)(2,1)S(1)} %get-tuple-element.31.refs_1_, ...), custom_call_target="tpu_custom_call" | custom-call | tf_op jit(solution)/shard_map/own_part/pallas_call | solution.py:74
  11.2 1.1 %partner_part.4 = (f32[2,32,8,128]{3,2,1,0:T(8,128)S(1)}, s16[66,8,128]{2,1,0:T(8,128)(2,1)S(1)}) custom-call(s32[128]{0:T(128)S(1)} %copy-done.2, f32[128,8,128]{2,1,0:T(8,128)S(1)} %get-tuple-element.38.refs_1_, bf16[128,8,128]{2,1,0:T(8,128)(2,1)S(1)} %collective-permute-done.3.refs_2_, bf16[128,64,128]{2,1,0:T(8,128)(2,1)S(1)} %get-tuple-element.35.refs_3_), custom_call_target="tpu_custom_call" | custom-call | tf_op jit(solution)/shard_map/partner_part/pallas_call | solution.py:74
  12.3 2.2 %collective-permute-start.4 = (s16[66,8,128]{2,1,0:T(8,128)(2,1)S(1)}, s16[66,8,128]{2,1,0:T(8,128)(2,1)S(1)}, u32[]{:S(2)}, u32[]{:S(2)}) collective-permute-start(s16[66,8,128]{2,1,0:T(8,128)(2,1)S(1)} %get-tuple-element.42), channel_id=1, source_target_pairs={{0,1},{1,0},{2,3},{3,2},{4,5},{5,4},{6,7},{7,6},{8,9},{9,8},{10,11... | collective-permute-start | bytes 405512 | tf_op jit(solution)/shard_map/ppermute | solution.py:21
  14.5 2.3 %collective-permute-done.2.refs_2_ = bf16[128,8,128]{2,1,0:T(8,128)(2,1)S(1)} collective-permute-done((bf16[128,8,128]{2,1,0:T(8,128)(2,1)S(1)}, bf16[128,8,128]{2,1,0:T(8,128)(2,1)S(1)}, u32[]{:S(2)}, u32[]{:S(2)}) %collective-permute-start.2) | collective-permute-done | bytes 262176 | tf_op jit(solution)/shard_map/ppermute | solution.py:21
  16.8 1.2 %partner_part.5 = (f32[2,32,8,128]{3,2,1,0:T(8,128)S(1)}, s16[66,8,128]{2,1,0:T(8,128)(2,1)S(1)}) custom-call(s32[128]{0:T(128)S(1)} %copy-done.2, f32[128,8,128]{2,1,0:T(8,128)S(1)} %get-tuple-element.37.refs_1_, bf16[128,8,128]{2,1,0:T(8,128)(2,1)S(1)} %collective-permute-done.2.refs_2_, bf16[128,64,128]{2,1,0:T(8,128)(2,1)S(1)} %get-tuple-element.35.refs_3_, ...), custom_call_target="tpu_custom_call" | custom-call | tf_op jit(solution)/shard_map/partner_part/pallas_call | solution.py:74
  17.9 2.2 %collective-permute-start.5 = (s16[66,8,128]{2,1,0:T(8,128)(2,1)S(1)}, s16[66,8,128]{2,1,0:T(8,128)(2,1)S(1)}, u32[]{:S(2)}, u32[]{:S(2)}) collective-permute-start(s16[66,8,128]{2,1,0:T(8,128)(2,1)S(1)} %get-tuple-element.43), channel_id=1, source_target_pairs={{0,1},{1,0},{2,3},{3,2},{4,5},{5,4},{6,7},{7,6},{8,9},{9,8},{10,11... | collective-permute-start | bytes 405512 | tf_op jit(solution)/shard_map/ppermute | solution.py:21
  20.1 2.3 %collective-permute-done.1.refs_2_ = bf16[128,8,128]{2,1,0:T(8,128)(2,1)S(1)} collective-permute-done((bf16[128,8,128]{2,1,0:T(8,128)(2,1)S(1)}, bf16[128,8,128]{2,1,0:T(8,128)(2,1)S(1)}, u32[]{:S(2)}, u32[]{:S(2)}) %collective-permute-start.1) | collective-permute-done | bytes 262176 | tf_op jit(solution)/shard_map/ppermute | solution.py:21
  22.4 1.1 %partner_part.6 = (f32[2,32,8,128]{3,2,1,0:T(8,128)S(1)}, s16[66,8,128]{2,1,0:T(8,128)(2,1)S(1)}) custom-call(s32[128]{0:T(128)S(1)} %copy-done.2, f32[128,8,128]{2,1,0:T(8,128)S(1)} %get-tuple-element.36.refs_1_, bf16[128,8,128]{2,1,0:T(8,128)(2,1)S(1)} %collective-permute-done.1.refs_2_, bf16[128,64,128]{2,1,0:T(8,128)(2,1)S(1)} %get-tuple-element.35.refs_3_, ...), custom_call_target="tpu_custom_call" | custom-call | tf_op jit(solution)/shard_map/partner_part/pallas_call | solution.py:74
  23.5 2.2 %collective-permute-start.11 = (s16[66,8,128]{2,1,0:T(8,128)(2,1)S(1)}, s16[66,8,128]{2,1,0:T(8,128)(2,1)S(1)}, u32[]{:S(2)}, u32[]{:S(2)}) collective-permute-start(s16[66,8,128]{2,1,0:T(8,128)(2,1)S(1)} %get-tuple-element.52), channel_id=1, source_target_pairs={{0,1},{1,0},{2,3},{3,2},{4,5},{5,4},{6,7},{7,6},{8,9},{9,8},{10,11... | collective-permute-start | bytes 405512 | tf_op jit(solution)/shard_map/ppermute | solution.py:21
  25.9 2.7 %collective-permute-start.10 = (s16[33,16,128]{2,1,0:T(8,128)(2,1)S(1)}, s16[33,16,128]{2,1,0:T(8,128)(2,1)S(1)}, u32[]{:S(2)}, u32[]{:S(2)}) collective-permute-start(s16[33,16,128]{2,1,0:T(8,128)(2,1)S(1)} %get-tuple-element.51), channel_id=1, source_target_pairs={{0,2},{1,3},{2,0},{3,1},{4,6},{5,7},{6,4},{7,5},{8,10},{9,11},{10,... | collective-permute-start | bytes 405512 | tf_op jit(solution)/shard_map/ppermute | solution.py:21
  28.5 1.1 %partner_part.7 = (f32[1,32,8,128]{3,2,1,0:T(8,128)S(1)}, s16[33,8,128]{2,1,0:T(8,128)(2,1)S(1)}, s16[33,8,128]{2,1,0:T(8,128)(2,1)S(1)}, s16[33,8,128]{2,1,0:T(8,128)(2,1)S(1)}) custom-call(s32[128]{0:T(128)S(1)} %copy-done.2, f32[128,8,128]{2,1,0:T(8,128)S(1)} %get-tuple-element.34.refs_1_, bf16[128,8,128]{2,1,0:T(8,128)(2,1)S(1)} %collective-permute-done.refs_2_, ...), custom_call_target="tpu_custom_call" | custom-call | tf_op jit(solution)/shard_map/partner_part/pallas_call | solution.py:74
  29.8 2.1 %collective-permute-start.12 = (s16[33,8,128]{2,1,0:T(8,128)(2,1)S(1)}, s16[33,8,128]{2,1,0:T(8,128)(2,1)S(1)}, u32[]{:S(2)}, u32[]{:S(2)}) collective-permute-start(s16[33,8,128]{2,1,0:T(8,128)(2,1)S(1)} %get-tuple-element.54), channel_id=1, source_target_pairs={{0,2},{1,3},{2,0},{3,1},{4,6},{5,7},{6,4},{7,5},{8,10},{9,11},{10,... | collective-permute-start | bytes 202760 | tf_op jit(solution)/shard_map/ppermute | solution.py:21
  31.9 3.0 %collective-permute-start.6 = (s16[33,8,128]{2,1,0:T(8,128)(2,1)S(1)}, s16[33,8,128]{2,1,0:T(8,128)(2,1)S(1)}, u32[]{:S(2)}, u32[]{:S(2)}) collective-permute-start(s16[33,8,128]{2,1,0:T(8,128)(2,1)S(1)} %get-tuple-element.46), channel_id=1, source_target_pairs={{0,1},{1,0},{2,3},{3,2},{4,5},{5,4},{6,7},{7,6},{8,9},{9,8},{10,11... | collective-permute-start | bytes 202760 | tf_op jit(solution)/shard_map/ppermute | solution.py:21
  35.0 2.3 %collective-permute-start.8 = (s16[33,8,128]{2,1,0:T(8,128)(2,1)S(1)}, s16[33,8,128]{2,1,0:T(8,128)(2,1)S(1)}, u32[]{:S(2)}, u32[]{:S(2)}) collective-permute-start(s16[33,8,128]{2,1,0:T(8,128)(2,1)S(1)} %get-tuple-element.48), channel_id=1, source_target_pairs={{0,3},{1,2},{2,1},{3,0},{4,7},{5,6},{6,5},{7,4},{8,11},{9,10},{10,... | collective-permute-start | bytes 202760 | tf_op jit(solution)/shard_map/ppermute | solution.py:21
  37.2 1.1 %collective-permute-done.12.refs_3_ = s16[33,8,128]{2,1,0:T(8,128)(2,1)S(1)} collective-permute-done((s16[33,8,128]{2,1,0:T(8,128)(2,1)S(1)}, s16[33,8,128]{2,1,0:T(8,128)(2,1)S(1)}, u32[]{:S(2)}, u32[]{:S(2)}) %collective-permute-start.12) | collective-permute-done | bytes 67616 | tf_op jit(solution)/shard_map/ppermute | solution.py:21
  38.5 1.6 %collective-permute-start.13 = (s16[33,24,128]{2,1,0:T(8,128)(2,1)S(1)}, s16[33,24,128]{2,1,0:T(8,128)(2,1)S(1)}, u32[]{:S(2)}, u32[]{:S(2)}) collective-permute-start(s16[33,24,128]{2,1,0:T(8,128)(2,1)S(1)} %get-tuple-element.56), channel_id=1, source_target_pairs={{0,8},{4,12},{8,0},{12,4},{16,24},{20,28},{24,16},{28,20},{1,9},{5... | collective-permute-start | bytes 608264 | tf_op jit(solution)/shard_map/ppermute | solution.py:21
  40.1 1.2 %collective-permute-done.7.refs_2_ = s16[33,8,128]{2,1,0:T(8,128)(2,1)S(1)} collective-permute-done((s16[33,8,128]{2,1,0:T(8,128)(2,1)S(1)}, s16[33,8,128]{2,1,0:T(8,128)(2,1)S(1)}, u32[]{:S(2)}, u32[]{:S(2)}) %collective-permute-start.7) | collective-permute-done | bytes 67616 | tf_op jit(solution)/shard_map/ppermute | solution.py:21
  41.4 1.6 %collective-permute-start.9 = (s16[33,8,128]{2,1,0:T(8,128)(2,1)S(1)}, s16[33,8,128]{2,1,0:T(8,128)(2,1)S(1)}, u32[]{:S(2)}, u32[]{:S(2)}) collective-permute-start(s16[33,8,128]{2,1,0:T(8,128)(2,1)S(1)} %get-tuple-element.50), channel_id=1, source_target_pairs={{0,8},{4,12},{8,0},{12,4},{16,24},{20,28},{24,16},{28,20},{1,9},{5... | collective-permute-start | bytes 202760 | tf_op jit(solution)/shard_map/ppermute | solution.py:21
  43.0 1.3 %constant_dynamic-slice_fusion.factor_ref = bf16[32,2,64,128]{3,2,1,0:T(8,128)(2,1)S(1)} fusion(bf16[128,2,64,128]{3,2,1,0:T(8,128)(2,1)} %param.6, s32[]{:T(128)S(6)} %select_n.3), kind=kLoop, calls=%fused_computation | loop fusion | bytes 2097156 | tf_op jit(solution)/shard_map/dynamic_slice | solution.py:305
  44.3 1.4 %second_level.2.rest_0_ = f32[32,32,128]{2,1,0:T(8,128)} custom-call(f32[32,24,128]{2,1,0:T(8,128)S(1)} %get-tuple-element.55.own_ref, s16[33,24,128]{2,1,0:T(8,128)(2,1)S(1)} %collective-permute-done.13.coded_ref, bf16[32,2,64,128]{3,2,1,0:T(8,128)(2,1)S(1)} %constant_dynamic-slice_fusion.factor_ref), custom_call_target="tpu_custom_call" | custom-call | tf_op jit(solution)/shard_map/second_level/pallas_call | solution.py:281
  (24 shorter events, 3.1 us)
Async XLA Ops:
  0.0 11.2 %copy-start.2 = (s32[128]{0:T(128)S(1)}, s32[128]{0:T(128)}, u32[]{:S(2)}) copy-start(s32[128]{0:T(128)} %refs_0_.7) | copy-start | bytes 1540
  1.0 10.2 %collective-permute-start.3 = (bf16[128,8,128]{2,1,0:T(8,128)(2,1)S(1)}, bf16[128,8,128]{2,1,0:T(8,128)(2,1)S(1)}, u32[]{:S(2)}, u32[]{:S(2)}) collective-permute-start(bf16[128,8,128]{2,1,0:T(8,128)(2,1)S(1)} %slice.4.refs_1_.refs_0_), channel_id=1, source_target_pairs={{0,16},{4,20},{8,24},{12,28},{16,0},{20,4},{24,8},{28,12},{1,17},{... | collective-permute-start | bytes 786440 | tf_op jit(solution)/shard_map/ppermute | solution.py:21
  4.0 1.2 %copy-start.1 = (bf16[1,128,32,128]{3,2,1,0:T(8,128)(2,1)S(1)}, bf16[1,128,32,128]{3,2,1,0:T(8,128)(2,1)}, u32[]{:S(2)}) copy-start(bf16[1,128,32,128]{3,2,1,0:T(8,128)(2,1)} %param.4) | copy-start | bytes 3145732
  5.4 11.4 %collective-permute-start.2 = (bf16[128,8,128]{2,1,0:T(8,128)(2,1)S(1)}, bf16[128,8,128]{2,1,0:T(8,128)(2,1)S(1)}, u32[]{:S(2)}, u32[]{:S(2)}) collective-permute-start(bf16[128,8,128]{2,1,0:T(8,128)(2,1)S(1)} %get-tuple-element.31.refs_1_), channel_id=1, source_target_pairs={{0,16},{4,20},{8,24},{12,28},{16,0},{20,4},{24,8},{28,12},{1,17},{... | collective-permute-start | bytes 786440 | tf_op jit(solution)/shard_map/ppermute | solution.py:21
  5.5 16.9 %collective-permute-start.1 = (bf16[128,8,128]{2,1,0:T(8,128)(2,1)S(1)}, bf16[128,8,128]{2,1,0:T(8,128)(2,1)S(1)}, u32[]{:S(2)}, u32[]{:S(2)}) collective-permute-start(bf16[128,8,128]{2,1,0:T(8,128)(2,1)S(1)} %get-tuple-element.32.refs_2_), channel_id=1, source_target_pairs={{0,16},{4,20},{8,24},{12,28},{16,0},{20,4},{24,8},{28,12},{1,17},{... | collective-permute-start | bytes 786440 | tf_op jit(solution)/shard_map/ppermute | solution.py:21
  7.5 21.1 %collective-permute-start = (bf16[128,8,128]{2,1,0:T(8,128)(2,1)S(1)}, bf16[128,8,128]{2,1,0:T(8,128)(2,1)S(1)}, u32[]{:S(2)}, u32[]{:S(2)}) collective-permute-start(bf16[128,8,128]{2,1,0:T(8,128)(2,1)S(1)} %get-tuple-element.33.refs_3_), channel_id=1, source_target_pairs={{0,16},{4,20},{8,24},{12,28},{16,0},{20,4},{24,8},{28,12},{1,17},{... | collective-permute-start | bytes 786440 | tf_op jit(solution)/shard_map/ppermute | solution.py:21
  7.6 2.2 %copy-start = (bf16[1,128,2,64,128]{4,3,2,1,0:T(8,128)(2,1)S(1)}, bf16[1,128,2,64,128]{4,3,2,1,0:T(8,128)(2,1)}, u32[]{:S(2)}) copy-start(bf16[1,128,2,64,128]{4,3,2,1,0:T(8,128)(2,1)} %param.5) | copy-start | bytes 12582916
  12.3 13.4 %collective-permute-start.4 = (s16[66,8,128]{2,1,0:T(8,128)(2,1)S(1)}, s16[66,8,128]{2,1,0:T(8,128)(2,1)S(1)}, u32[]{:S(2)}, u32[]{:S(2)}) collective-permute-start(s16[66,8,128]{2,1,0:T(8,128)(2,1)S(1)} %get-tuple-element.42), channel_id=1, source_target_pairs={{0,1},{1,0},{2,3},{3,2},{4,5},{5,4},{6,7},{7,6},{8,9},{9,8},{10,11... | collective-permute-start | bytes 405512 | tf_op jit(solution)/shard_map/ppermute | solution.py:21
  17.9 7.8 %collective-permute-start.5 = (s16[66,8,128]{2,1,0:T(8,128)(2,1)S(1)}, s16[66,8,128]{2,1,0:T(8,128)(2,1)S(1)}, u32[]{:S(2)}, u32[]{:S(2)}) collective-permute-start(s16[66,8,128]{2,1,0:T(8,128)(2,1)S(1)} %get-tuple-element.43), channel_id=1, source_target_pairs={{0,1},{1,0},{2,3},{3,2},{4,5},{5,4},{6,7},{7,6},{8,9},{9,8},{10,11... | collective-permute-start | bytes 405512 | tf_op jit(solution)/shard_map/ppermute | solution.py:21
  23.5 6.2 %collective-permute-start.11 = (s16[66,8,128]{2,1,0:T(8,128)(2,1)S(1)}, s16[66,8,128]{2,1,0:T(8,128)(2,1)S(1)}, u32[]{:S(2)}, u32[]{:S(2)}) collective-permute-start(s16[66,8,128]{2,1,0:T(8,128)(2,1)S(1)} %get-tuple-element.52), channel_id=1, source_target_pairs={{0,1},{1,0},{2,3},{3,2},{4,5},{5,4},{6,7},{7,6},{8,9},{9,8},{10,11... | collective-permute-start | bytes 405512 | tf_op jit(solution)/shard_map/ppermute | solution.py:21
  25.9 12.5 %collective-permute-start.10 = (s16[33,16,128]{2,1,0:T(8,128)(2,1)S(1)}, s16[33,16,128]{2,1,0:T(8,128)(2,1)S(1)}, u32[]{:S(2)}, u32[]{:S(2)}) collective-permute-start(s16[33,16,128]{2,1,0:T(8,128)(2,1)S(1)} %get-tuple-element.51), channel_id=1, source_target_pairs={{0,2},{1,3},{2,0},{3,1},{4,6},{5,7},{6,4},{7,5},{8,10},{9,11},{10,... | collective-permute-start | bytes 405512 | tf_op jit(solution)/shard_map/ppermute | solution.py:21
  29.8 8.5 %collective-permute-start.12 = (s16[33,8,128]{2,1,0:T(8,128)(2,1)S(1)}, s16[33,8,128]{2,1,0:T(8,128)(2,1)S(1)}, u32[]{:S(2)}, u32[]{:S(2)}) collective-permute-start(s16[33,8,128]{2,1,0:T(8,128)(2,1)S(1)} %get-tuple-element.54), channel_id=1, source_target_pairs={{0,2},{1,3},{2,0},{3,1},{4,6},{5,7},{6,4},{7,5},{8,10},{9,11},{10,... | collective-permute-start | bytes 202760 | tf_op jit(solution)/shard_map/ppermute | solution.py:21
  31.9 8.2 %collective-permute-start.6 = (s16[33,8,128]{2,1,0:T(8,128)(2,1)S(1)}, s16[33,8,128]{2,1,0:T(8,128)(2,1)S(1)}, u32[]{:S(2)}, u32[]{:S(2)}) collective-permute-start(s16[33,8,128]{2,1,0:T(8,128)(2,1)S(1)} %get-tuple-element.46), channel_id=1, source_target_pairs={{0,1},{1,0},{2,3},{3,2},{4,5},{5,4},{6,7},{7,6},{8,9},{9,8},{10,11... | collective-permute-start | bytes 202760 | tf_op jit(solution)/shard_map/ppermute | solution.py:21
  34.9 6.4 %collective-permute-start.7 = (s16[33,8,128]{2,1,0:T(8,128)(2,1)S(1)}, s16[33,8,128]{2,1,0:T(8,128)(2,1)S(1)}, u32[]{:S(2)}, u32[]{:S(2)}) collective-permute-start(s16[33,8,128]{2,1,0:T(8,128)(2,1)S(1)} %get-tuple-element.47), channel_id=1, source_target_pairs={{0,2},{1,3},{2,0},{3,1},{4,6},{5,7},{6,4},{7,5},{8,10},{9,11},{10,... | collective-permute-start | bytes 202760 | tf_op jit(solution)/shard_map/ppermute | solution.py:21
  35.0 6.4 %collective-permute-start.8 = (s16[33,8,128]{2,1,0:T(8,128)(2,1)S(1)}, s16[33,8,128]{2,1,0:T(8,128)(2,1)S(1)}, u32[]{:S(2)}, u32[]{:S(2)}) collective-permute-start(s16[33,8,128]{2,1,0:T(8,128)(2,1)S(1)} %get-tuple-element.48), channel_id=1, source_target_pairs={{0,3},{1,2},{2,1},{3,0},{4,7},{5,6},{6,5},{7,4},{8,11},{9,10},{10,... | collective-permute-start | bytes 202760 | tf_op jit(solution)/shard_map/ppermute | solution.py:21
  38.5 5.8 %collective-permute-start.13 = (s16[33,24,128]{2,1,0:T(8,128)(2,1)S(1)}, s16[33,24,128]{2,1,0:T(8,128)(2,1)S(1)}, u32[]{:S(2)}, u32[]{:S(2)}) collective-permute-start(s16[33,24,128]{2,1,0:T(8,128)(2,1)S(1)} %get-tuple-element.56), channel_id=1, source_target_pairs={{0,8},{4,12},{8,0},{12,4},{16,24},{20,28},{24,16},{28,20},{1,9},{5... | collective-permute-start | bytes 608264 | tf_op jit(solution)/shard_map/ppermute | solution.py:21
  41.4 4.4 %collective-permute-start.9 = (s16[33,8,128]{2,1,0:T(8,128)(2,1)S(1)}, s16[33,8,128]{2,1,0:T(8,128)(2,1)S(1)}, u32[]{:S(2)}, u32[]{:S(2)}) collective-permute-start(s16[33,8,128]{2,1,0:T(8,128)(2,1)S(1)} %get-tuple-element.50), channel_id=1, source_target_pairs={{0,8},{4,12},{8,0},{12,4},{16,24},{20,28},{24,16},{28,20},{1,9},{5... | collective-permute-start | bytes 202760 | tf_op jit(solution)/shard_map/ppermute | solution.py:21

commit v6 on v5

--- a/solution.py
+++ b/solution.py
@@ -304,7 +304,7 @@
     owns, factors = own_part(values, first_factors)
     mine = lax.dynamic_slice_in_dim(second_factors, me * share, share, 0)
     waiting, marks = {}, {"mine": mine}
-    order = [('first', (0,)), ('first', (1,), ('first', (0,))), ('first', (2,), ('first', (1,))), ('halve', (0, 1), ('first', (2,))), ('first', (3,), ('first', (2,)), ('halve', (0, 1))), ('halve', (2,), ('first', (3,)))]
+    order = [('first', (0,)), ('first', (1,), ('first', (0,))), ('first', (2,), ('first', (1,))), ('halve', (0, 1), ('first', (2,))), ('first', (3,), ('first', (2,))), ('halve', (2,), ('first', (3,)))]
     for step, chunks, *before in order:
         last = [marks[b] for b in before]
         if step == "first":

time: 47.1 us -> 47.1 us (level)
  no operation moved by 1% of the time
where the time goes in v6:
time: 47.1 us; the launch traced here: 46.9 us
  starting transfers between devices  25 us (53%)
  Pallas kernels  8.99 us (19%)
  waiting for transfers between devices  7.11 us (15%)
  local copies, waits for them, and re-layouts  5.69 us (12%)
    ppermute x14, starting transfers between devices, swapped(): lax.ppermute(block, axis, [(i, i ^ mask) for i in range(lax.axis_size(axi...  25 us
    ppermute x14, waiting for transfers between devices, swapped(): lax.ppermute(block, axis, [(i, i ^ mask) for i in range(lax.axis_size(axi...  7.11 us
    pallas_call x10, Pallas kernels, call(): pl.pallas_call(body, in_specs=in_specs + [ANY] * len(after), out_specs=[V...  6.51 us
    unnamed x6, local copies, waits for them, and re-layouts  3.42 us
    pallas_call x2, Pallas kernels, second_level(): pl.pallas_call(functools.partial(second_kernel, start), in_specs=[VMEM] *...  2.48 us
    dynamic_slice x1, local copies, waits for them, and re-layouts, on_device(): mine = lax.dynamic_slice_in_dim(second_factors, me * share, share, 0)  1.3 us
    slice x1, local copies, waits for them, and re-layouts, on_device(): values = [sources[:, :CHUNKS[0]]]  0.98 us
  transfers between devices with their start and end apart: 14, of which 6 were waited for; matrix products, arithmetic and copies ran while one was open for 3% of the time, Pallas kernels for 17%

profile of v6, /device:TPU:0, one launch (start us, length us, event | category | flops | bytes accessed | tf_op | source)
XLA Modules:
  0.0 46.9 jit_solution(16133165567177698472)
XLA Ops:
  1.0 3.0 %collective-permute-start.3 = (bf16[128,8,128]{2,1,0:T(8,128)(2,1)S(1)}, bf16[128,8,128]{2,1,0:T(8,128)(2,1)S(1)}, u32[]{:S(2)}, u32[]{:S(2)}) collective-permute-start(bf16[128,8,128]{2,1,0:T(8,128)(2,1)S(1)} %slice.4.refs_1_.refs_0_), channel_id=1, source_target_pairs={{0,16},{4,20},{8,24},{12,28},{16,0},{20,4},{24,8},{28,12},{1,17},{... | collective-permute-start | bytes 786440 | tf_op jit(solution)/shard_map/ppermute | solution.py:21
  4.0 1.2 %copy-done.1 = bf16[1,128,32,128]{3,2,1,0:T(8,128)(2,1)S(1)} copy-done((bf16[1,128,32,128]{3,2,1,0:T(8,128)(2,1)S(1)}, bf16[1,128,32,128]{3,2,1,0:T(8,128)(2,1)}, u32[]{:S(2)}) %copy-start.1) | copy-done | bytes 1048600
  5.5 2.0 %collective-permute-start.1 = (bf16[128,8,128]{2,1,0:T(8,128)(2,1)S(1)}, bf16[128,8,128]{2,1,0:T(8,128)(2,1)S(1)}, u32[]{:S(2)}, u32[]{:S(2)}) collective-permute-start(bf16[128,8,128]{2,1,0:T(8,128)(2,1)S(1)} %get-tuple-element.32.refs_2_), channel_id=1, source_target_pairs={{0,16},{4,20},{8,24},{12,28},{16,0},{20,4},{24,8},{28,12},{1,17},{... | collective-permute-start | bytes 786440 | tf_op jit(solution)/shard_map/ppermute | solution.py:21
  7.6 2.2 %copy-done = bf16[1,128,2,64,128]{4,3,2,1,0:T(8,128)(2,1)S(1)} copy-done((bf16[1,128,2,64,128]{4,3,2,1,0:T(8,128)(2,1)S(1)}, bf16[1,128,2,64,128]{4,3,2,1,0:T(8,128)(2,1)}, u32[]{:S(2)}) %copy-start) | copy-done | bytes 4194328
  9.7 1.3 %own_part.1 = (f32[128,8,128]{2,1,0:T(8,128)S(1)}, f32[128,8,128]{2,1,0:T(8,128)S(1)}, f32[128,8,128]{2,1,0:T(8,128)S(1)}, f32[128,8,128]{2,1,0:T(8,128)S(1)}, bf16[128,64,128]{2,1,0:T(8,128)(2,1)S(1)}) custom-call(bf16[128,8,128]{2,1,0:T(8,128)(2,1)S(1)} %slice.4.refs_1_.refs_0_, bf16[128,8,128]{2,1,0:T(8,128)(2,1)S(1)} %get-tuple-element.31.refs_1_, ...), custom_call_target="tpu_custom_call" | custom-call | tf_op jit(solution)/shard_map/own_part/pallas_call | solution.py:74
  11.2 1.1 %partner_part.4 = (f32[2,32,8,128]{3,2,1,0:T(8,128)S(1)}, s16[66,8,128]{2,1,0:T(8,128)(2,1)S(1)}) custom-call(s32[128]{0:T(128)S(1)} %copy-done.2, f32[128,8,128]{2,1,0:T(8,128)S(1)} %get-tuple-element.38.refs_1_, bf16[128,8,128]{2,1,0:T(8,128)(2,1)S(1)} %collective-permute-done.3.refs_2_, bf16[128,64,128]{2,1,0:T(8,128)(2,1)S(1)} %get-tuple-element.35.refs_3_), custom_call_target="tpu_custom_call" | custom-call | tf_op jit(solution)/shard_map/partner_part/pallas_call | solution.py:74
  12.3 2.2 %collective-permute-start.8 = (s16[66,8,128]{2,1,0:T(8,128)(2,1)S(1)}, s16[66,8,128]{2,1,0:T(8,128)(2,1)S(1)}, u32[]{:S(2)}, u32[]{:S(2)}) collective-permute-start(s16[66,8,128]{2,1,0:T(8,128)(2,1)S(1)} %get-tuple-element.48), channel_id=1, source_target_pairs={{0,1},{1,0},{2,3},{3,2},{4,5},{5,4},{6,7},{7,6},{8,9},{9,8},{10,11... | collective-permute-start | bytes 405512 | tf_op jit(solution)/shard_map/ppermute | solution.py:21
  14.5 2.3 %collective-permute-done.2.refs_2_ = bf16[128,8,128]{2,1,0:T(8,128)(2,1)S(1)} collective-permute-done((bf16[128,8,128]{2,1,0:T(8,128)(2,1)S(1)}, bf16[128,8,128]{2,1,0:T(8,128)(2,1)S(1)}, u32[]{:S(2)}, u32[]{:S(2)}) %collective-permute-start.2) | collective-permute-done | bytes 262176 | tf_op jit(solution)/shard_map/ppermute | solution.py:21
  16.8 1.1 %partner_part.5 = (f32[2,32,8,128]{3,2,1,0:T(8,128)S(1)}, s16[66,8,128]{2,1,0:T(8,128)(2,1)S(1)}) custom-call(s32[128]{0:T(128)S(1)} %copy-done.2, f32[128,8,128]{2,1,0:T(8,128)S(1)} %get-tuple-element.37.refs_1_, bf16[128,8,128]{2,1,0:T(8,128)(2,1)S(1)} %collective-permute-done.2.refs_2_, bf16[128,64,128]{2,1,0:T(8,128)(2,1)S(1)} %get-tuple-element.35.refs_3_, ...), custom_call_target="tpu_custom_call" | custom-call | tf_op jit(solution)/shard_map/partner_part/pallas_call | solution.py:74
  17.9 2.2 %collective-permute-start.9 = (s16[66,8,128]{2,1,0:T(8,128)(2,1)S(1)}, s16[66,8,128]{2,1,0:T(8,128)(2,1)S(1)}, u32[]{:S(2)}, u32[]{:S(2)}) collective-permute-start(s16[66,8,128]{2,1,0:T(8,128)(2,1)S(1)} %get-tuple-element.49), channel_id=1, source_target_pairs={{0,1},{1,0},{2,3},{3,2},{4,5},{5,4},{6,7},{7,6},{8,9},{9,8},{10,11... | collective-permute-start | bytes 405512 | tf_op jit(solution)/shard_map/ppermute | solution.py:21
  20.1 2.3 %collective-permute-done.1.refs_2_ = bf16[128,8,128]{2,1,0:T(8,128)(2,1)S(1)} collective-permute-done((bf16[128,8,128]{2,1,0:T(8,128)(2,1)S(1)}, bf16[128,8,128]{2,1,0:T(8,128)(2,1)S(1)}, u32[]{:S(2)}, u32[]{:S(2)}) %collective-permute-start.1) | collective-permute-done | bytes 262176 | tf_op jit(solution)/shard_map/ppermute | solution.py:21
  22.4 1.1 %partner_part.6 = (f32[2,32,8,128]{3,2,1,0:T(8,128)S(1)}, s16[66,8,128]{2,1,0:T(8,128)(2,1)S(1)}) custom-call(s32[128]{0:T(128)S(1)} %copy-done.2, f32[128,8,128]{2,1,0:T(8,128)S(1)} %get-tuple-element.36.refs_1_, bf16[128,8,128]{2,1,0:T(8,128)(2,1)S(1)} %collective-permute-done.1.refs_2_, bf16[128,64,128]{2,1,0:T(8,128)(2,1)S(1)} %get-tuple-element.35.refs_3_, ...), custom_call_target="tpu_custom_call" | custom-call | tf_op jit(solution)/shard_map/partner_part/pallas_call | solution.py:74
  23.5 2.2 %collective-permute-start.11 = (s16[66,8,128]{2,1,0:T(8,128)(2,1)S(1)}, s16[66,8,128]{2,1,0:T(8,128)(2,1)S(1)}, u32[]{:S(2)}, u32[]{:S(2)}) collective-permute-start(s16[66,8,128]{2,1,0:T(8,128)(2,1)S(1)} %get-tuple-element.52), channel_id=1, source_target_pairs={{0,1},{1,0},{2,3},{3,2},{4,5},{5,4},{6,7},{7,6},{8,9},{9,8},{10,11... | collective-permute-start | bytes 405512 | tf_op jit(solution)/shard_map/ppermute | solution.py:21
  25.9 2.7 %collective-permute-start.10 = (s16[33,16,128]{2,1,0:T(8,128)(2,1)S(1)}, s16[33,16,128]{2,1,0:T(8,128)(2,1)S(1)}, u32[]{:S(2)}, u32[]{:S(2)}) collective-permute-start(s16[33,16,128]{2,1,0:T(8,128)(2,1)S(1)} %get-tuple-element.51), channel_id=1, source_target_pairs={{0,2},{1,3},{2,0},{3,1},{4,6},{5,7},{6,4},{7,5},{8,10},{9,11},{10,... | collective-permute-start | bytes 405512 | tf_op jit(solution)/shard_map/ppermute | solution.py:21
  28.6 1.1 %partner_part.7 = (f32[1,32,8,128]{3,2,1,0:T(8,128)S(1)}, s16[33,8,128]{2,1,0:T(8,128)(2,1)S(1)}, s16[33,8,128]{2,1,0:T(8,128)(2,1)S(1)}, s16[33,8,128]{2,1,0:T(8,128)(2,1)S(1)}) custom-call(s32[128]{0:T(128)S(1)} %copy-done.2, f32[128,8,128]{2,1,0:T(8,128)S(1)} %get-tuple-element.34.refs_1_, bf16[128,8,128]{2,1,0:T(8,128)(2,1)S(1)} %collective-permute-done.refs_2_, ...), custom_call_target="tpu_custom_call" | custom-call | tf_op jit(solution)/shard_map/partner_part/pallas_call | solution.py:74
  29.8 2.1 %collective-permute-start.12 = (s16[33,8,128]{2,1,0:T(8,128)(2,1)S(1)}, s16[33,8,128]{2,1,0:T(8,128)(2,1)S(1)}, u32[]{:S(2)}, u32[]{:S(2)}) collective-permute-start(s16[33,8,128]{2,1,0:T(8,128)(2,1)S(1)} %get-tuple-element.54), channel_id=1, source_target_pairs={{0,2},{1,3},{2,0},{3,1},{4,6},{5,7},{6,4},{7,5},{8,10},{9,11},{10,... | collective-permute-start | bytes 202760 | tf_op jit(solution)/shard_map/ppermute | solution.py:21
  31.9 3.0 %collective-permute-start.4 = (s16[33,8,128]{2,1,0:T(8,128)(2,1)S(1)}, s16[33,8,128]{2,1,0:T(8,128)(2,1)S(1)}, u32[]{:S(2)}, u32[]{:S(2)}) collective-permute-start(s16[33,8,128]{2,1,0:T(8,128)(2,1)S(1)} %get-tuple-element.43), channel_id=1, source_target_pairs={{0,1},{1,0},{2,3},{3,2},{4,5},{5,4},{6,7},{7,6},{8,9},{9,8},{10,11... | collective-permute-start | bytes 202760 | tf_op jit(solution)/shard_map/ppermute | solution.py:21
  35.0 2.3 %collective-permute-start.6 = (s16[33,8,128]{2,1,0:T(8,128)(2,1)S(1)}, s16[33,8,128]{2,1,0:T(8,128)(2,1)S(1)}, u32[]{:S(2)}, u32[]{:S(2)}) collective-permute-start(s16[33,8,128]{2,1,0:T(8,128)(2,1)S(1)} %get-tuple-element.45), channel_id=1, source_target_pairs={{0,3},{1,2},{2,1},{3,0},{4,7},{5,6},{6,5},{7,4},{8,11},{9,10},{10,... | collective-permute-start | bytes 202760 | tf_op jit(solution)/shard_map/ppermute | solution.py:21
  38.6 1.5 %collective-permute-start.13 = (s16[33,24,128]{2,1,0:T(8,128)(2,1)S(1)}, s16[33,24,128]{2,1,0:T(8,128)(2,1)S(1)}, u32[]{:S(2)}, u32[]{:S(2)}) collective-permute-start(s16[33,24,128]{2,1,0:T(8,128)(2,1)S(1)} %get-tuple-element.56), channel_id=1, source_target_pairs={{0,8},{4,12},{8,0},{12,4},{16,24},{20,28},{24,16},{28,20},{1,9},{5... | collective-permute-start | bytes 608264 | tf_op jit(solution)/shard_map/ppermute | solution.py:21
  40.1 1.2 %collective-permute-done.5.refs_2_ = s16[33,8,128]{2,1,0:T(8,128)(2,1)S(1)} collective-permute-done((s16[33,8,128]{2,1,0:T(8,128)(2,1)S(1)}, s16[33,8,128]{2,1,0:T(8,128)(2,1)S(1)}, u32[]{:S(2)}, u32[]{:S(2)}) %collective-permute-start.5) | collective-permute-done | bytes 67616 | tf_op jit(solution)/shard_map/ppermute | solution.py:21
  41.4 1.5 %collective-permute-start.7 = (s16[33,8,128]{2,1,0:T(8,128)(2,1)S(1)}, s16[33,8,128]{2,1,0:T(8,128)(2,1)S(1)}, u32[]{:S(2)}, u32[]{:S(2)}) collective-permute-start(s16[33,8,128]{2,1,0:T(8,128)(2,1)S(1)} %get-tuple-element.47), channel_id=1, source_target_pairs={{0,8},{4,12},{8,0},{12,4},{16,24},{20,28},{24,16},{28,20},{1,9},{5... | collective-permute-start | bytes 202760 | tf_op jit(solution)/shard_map/ppermute | solution.py:21
  43.0 1.3 %constant_dynamic-slice_fusion.factor_ref = bf16[32,2,64,128]{3,2,1,0:T(8,128)(2,1)S(1)} fusion(bf16[128,2,64,128]{3,2,1,0:T(8,128)(2,1)} %param.6, s32[]{:T(128)S(6)} %select_n.3), kind=kLoop, calls=%fused_computation | loop fusion | bytes 2097156 | tf_op jit(solution)/shard_map/dynamic_slice | solution.py:305
  44.4 1.4 %second_level.2.rest_0_ = f32[32,32,128]{2,1,0:T(8,128)} custom-call(f32[32,24,128]{2,1,0:T(8,128)S(1)} %get-tuple-element.55.own_ref, s16[33,24,128]{2,1,0:T(8,128)(2,1)S(1)} %collective-permute-done.13.coded_ref, bf16[32,2,64,128]{3,2,1,0:T(8,128)(2,1)S(1)} %constant_dynamic-slice_fusion.factor_ref), custom_call_target="tpu_custom_call" | custom-call | tf_op jit(solution)/shard_map/second_level/pallas_call | solution.py:281
  45.8 1.1 %second_level.3 = f32[32,32,128]{2,1,0:T(8,128)} custom-call(f32[32,8,128]{2,1,0:T(8,128)S(1)} %get-tuple-element.46.own_ref, s16[33,8,128]{2,1,0:T(8,128)(2,1)S(1)} %collective-permute-done.7.coded_ref, bf16[32,2,64,128]{3,2,1,0:T(8,128)(2,1)S(1)} %constant_dynamic-slice_fusion.factor_ref, ...), custom_call_target="tpu_custom_call", output_to_operand_aliasing={{}: (3, {})} | custom-call | tf_op jit(solution)/shard_map/second_level/pallas_call | solution.py:281
  (24 shorter events, 3.2 us)
Async XLA Ops:
  0.0 11.2 %copy-start.2 = (s32[128]{0:T(128)S(1)}, s32[128]{0:T(128)}, u32[]{:S(2)}) copy-start(s32[128]{0:T(128)} %refs_0_.7) | copy-start | bytes 1540
  1.0 10.2 %collective-permute-start.3 = (bf16[128,8,128]{2,1,0:T(8,128)(2,1)S(1)}, bf16[128,8,128]{2,1,0:T(8,128)(2,1)S(1)}, u32[]{:S(2)}, u32[]{:S(2)}) collective-permute-start(bf16[128,8,128]{2,1,0:T(8,128)(2,1)S(1)} %slice.4.refs_1_.refs_0_), channel_id=1, source_target_pairs={{0,16},{4,20},{8,24},{12,28},{16,0},{20,4},{24,8},{28,12},{1,17},{... | collective-permute-start | bytes 786440 | tf_op jit(solution)/shard_map/ppermute | solution.py:21
  4.0 1.2 %copy-start.1 = (bf16[1,128,32,128]{3,2,1,0:T(8,128)(2,1)S(1)}, bf16[1,128,32,128]{3,2,1,0:T(8,128)(2,1)}, u32[]{:S(2)}) copy-start(bf16[1,128,32,128]{3,2,1,0:T(8,128)(2,1)} %param.4) | copy-start | bytes 3145732
  5.4 11.4 %collective-permute-start.2 = (bf16[128,8,128]{2,1,0:T(8,128)(2,1)S(1)}, bf16[128,8,128]{2,1,0:T(8,128)(2,1)S(1)}, u32[]{:S(2)}, u32[]{:S(2)}) collective-permute-start(bf16[128,8,128]{2,1,0:T(8,128)(2,1)S(1)} %get-tuple-element.31.refs_1_), channel_id=1, source_target_pairs={{0,16},{4,20},{8,24},{12,28},{16,0},{20,4},{24,8},{28,12},{1,17},{... | collective-permute-start | bytes 786440 | tf_op jit(solution)/shard_map/ppermute | solution.py:21
  5.5 16.9 %collective-permute-start.1 = (bf16[128,8,128]{2,1,0:T(8,128)(2,1)S(1)}, bf16[128,8,128]{2,1,0:T(8,128)(2,1)S(1)}, u32[]{:S(2)}, u32[]{:S(2)}) collective-permute-start(bf16[128,8,128]{2,1,0:T(8,128)(2,1)S(1)} %get-tuple-element.32.refs_2_), channel_id=1, source_target_pairs={{0,16},{4,20},{8,24},{12,28},{16,0},{20,4},{24,8},{28,12},{1,17},{... | collective-permute-start | bytes 786440 | tf_op jit(solution)/shard_map/ppermute | solution.py:21
  7.5 21.1 %collective-permute-start = (bf16[128,8,128]{2,1,0:T(8,128)(2,1)S(1)}, bf16[128,8,128]{2,1,0:T(8,128)(2,1)S(1)}, u32[]{:S(2)}, u32[]{:S(2)}) collective-permute-start(bf16[128,8,128]{2,1,0:T(8,128)(2,1)S(1)} %get-tuple-element.33.refs_3_), channel_id=1, source_target_pairs={{0,16},{4,20},{8,24},{12,28},{16,0},{20,4},{24,8},{28,12},{1,17},{... | collective-permute-start | bytes 786440 | tf_op jit(solution)/shard_map/ppermute | solution.py:21
  7.6 2.2 %copy-start = (bf16[1,128,2,64,128]{4,3,2,1,0:T(8,128)(2,1)S(1)}, bf16[1,128,2,64,128]{4,3,2,1,0:T(8,128)(2,1)}, u32[]{:S(2)}) copy-start(bf16[1,128,2,64,128]{4,3,2,1,0:T(8,128)(2,1)} %param.5) | copy-start | bytes 12582916
  12.3 13.4 %collective-permute-start.8 = (s16[66,8,128]{2,1,0:T(8,128)(2,1)S(1)}, s16[66,8,128]{2,1,0:T(8,128)(2,1)S(1)}, u32[]{:S(2)}, u32[]{:S(2)}) collective-permute-start(s16[66,8,128]{2,1,0:T(8,128)(2,1)S(1)} %get-tuple-element.48), channel_id=1, source_target_pairs={{0,1},{1,0},{2,3},{3,2},{4,5},{5,4},{6,7},{7,6},{8,9},{9,8},{10,11... | collective-permute-start | bytes 405512 | tf_op jit(solution)/shard_map/ppermute | solution.py:21
  17.9 7.8 %collective-permute-start.9 = (s16[66,8,128]{2,1,0:T(8,128)(2,1)S(1)}, s16[66,8,128]{2,1,0:T(8,128)(2,1)S(1)}, u32[]{:S(2)}, u32[]{:S(2)}) collective-permute-start(s16[66,8,128]{2,1,0:T(8,128)(2,1)S(1)} %get-tuple-element.49), channel_id=1, source_target_pairs={{0,1},{1,0},{2,3},{3,2},{4,5},{5,4},{6,7},{7,6},{8,9},{9,8},{10,11... | collective-permute-start | bytes 405512 | tf_op jit(solution)/shard_map/ppermute | solution.py:21
  23.5 6.2 %collective-permute-start.11 = (s16[66,8,128]{2,1,0:T(8,128)(2,1)S(1)}, s16[66,8,128]{2,1,0:T(8,128)(2,1)S(1)}, u32[]{:S(2)}, u32[]{:S(2)}) collective-permute-start(s16[66,8,128]{2,1,0:T(8,128)(2,1)S(1)} %get-tuple-element.52), channel_id=1, source_target_pairs={{0,1},{1,0},{2,3},{3,2},{4,5},{5,4},{6,7},{7,6},{8,9},{9,8},{10,11... | collective-permute-start | bytes 405512 | tf_op jit(solution)/shard_map/ppermute | solution.py:21
  25.9 12.5 %collective-permute-start.10 = (s16[33,16,128]{2,1,0:T(8,128)(2,1)S(1)}, s16[33,16,128]{2,1,0:T(8,128)(2,1)S(1)}, u32[]{:S(2)}, u32[]{:S(2)}) collective-permute-start(s16[33,16,128]{2,1,0:T(8,128)(2,1)S(1)} %get-tuple-element.51), channel_id=1, source_target_pairs={{0,2},{1,3},{2,0},{3,1},{4,6},{5,7},{6,4},{7,5},{8,10},{9,11},{10,... | collective-permute-start | bytes 405512 | tf_op jit(solution)/shard_map/ppermute | solution.py:21
  29.8 8.6 %collective-permute-start.12 = (s16[33,8,128]{2,1,0:T(8,128)(2,1)S(1)}, s16[33,8,128]{2,1,0:T(8,128)(2,1)S(1)}, u32[]{:S(2)}, u32[]{:S(2)}) collective-permute-start(s16[33,8,128]{2,1,0:T(8,128)(2,1)S(1)} %get-tuple-element.54), channel_id=1, source_target_pairs={{0,2},{1,3},{2,0},{3,1},{4,6},{5,7},{6,4},{7,5},{8,10},{9,11},{10,... | collective-permute-start | bytes 202760 | tf_op jit(solution)/shard_map/ppermute | solution.py:21
  31.9 8.2 %collective-permute-start.4 = (s16[33,8,128]{2,1,0:T(8,128)(2,1)S(1)}, s16[33,8,128]{2,1,0:T(8,128)(2,1)S(1)}, u32[]{:S(2)}, u32[]{:S(2)}) collective-permute-start(s16[33,8,128]{2,1,0:T(8,128)(2,1)S(1)} %get-tuple-element.43), channel_id=1, source_target_pairs={{0,1},{1,0},{2,3},{3,2},{4,5},{5,4},{6,7},{7,6},{8,9},{9,8},{10,11... | collective-permute-start | bytes 202760 | tf_op jit(solution)/shard_map/ppermute | solution.py:21
  34.9 6.4 %collective-permute-start.5 = (s16[33,8,128]{2,1,0:T(8,128)(2,1)S(1)}, s16[33,8,128]{2,1,0:T(8,128)(2,1)S(1)}, u32[]{:S(2)}, u32[]{:S(2)}) collective-permute-start(s16[33,8,128]{2,1,0:T(8,128)(2,1)S(1)} %get-tuple-element.44), channel_id=1, source_target_pairs={{0,2},{1,3},{2,0},{3,1},{4,6},{5,7},{6,4},{7,5},{8,10},{9,11},{10,... | collective-permute-start | bytes 202760 | tf_op jit(solution)/shard_map/ppermute | solution.py:21
  35.0 6.3 %collective-permute-start.6 = (s16[33,8,128]{2,1,0:T(8,128)(2,1)S(1)}, s16[33,8,128]{2,1,0:T(8,128)(2,1)S(1)}, u32[]{:S(2)}, u32[]{:S(2)}) collective-permute-start(s16[33,8,128]{2,1,0:T(8,128)(2,1)S(1)} %get-tuple-element.45), channel_id=1, source_target_pairs={{0,3},{1,2},{2,1},{3,0},{4,7},{5,6},{6,5},{7,4},{8,11},{9,10},{10,... | collective-permute-start | bytes 202760 | tf_op jit(solution)/shard_map/ppermute | solution.py:21
  38.6 5.8 %collective-permute-start.13 = (s16[33,24,128]{2,1,0:T(8,128)(2,1)S(1)}, s16[33,24,128]{2,1,0:T(8,128)(2,1)S(1)}, u32[]{:S(2)}, u32[]{:S(2)}) collective-permute-start(s16[33,24,128]{2,1,0:T(8,128)(2,1)S(1)} %get-tuple-element.56), channel_id=1, source_target_pairs={{0,8},{4,12},{8,0},{12,4},{16,24},{20,28},{24,16},{28,20},{1,9},{5... | collective-permute-start | bytes 608264 | tf_op jit(solution)/shard_map/ppermute | solution.py:21
  41.4 4.4 %collective-permute-start.7 = (s16[33,8,128]{2,1,0:T(8,128)(2,1)S(1)}, s16[33,8,128]{2,1,0:T(8,128)(2,1)S(1)}, u32[]{:S(2)}, u32[]{:S(2)}) collective-permute-start(s16[33,8,128]{2,1,0:T(8,128)(2,1)S(1)} %get-tuple-element.47), channel_id=1, source_target_pairs={{0,8},{4,12},{8,0},{12,4},{16,24},{20,28},{24,16},{28,20},{1,9},{5... | collective-permute-start | bytes 202760 | tf_op jit(solution)/shard_map/ppermute | solution.py:21
